TPU v7x, 512 devices: a whole 4x8x8 slice. The times are simulated.
512 devices in a mesh: cell: 128 (over y, z, core), view: 4 (over x).
Axes of the slice: x: 4, y: 8, z: 8, core: 2. Of those that a mesh axis runs over, the one named last changes fastest.
Arguments:
- params: float32 [59, 262144], P(None, 'cell'), may hold values from -8 to 8, as said below
- cameras: float32 [4, 3], P('view'), may hold values from -0.005 to 0.005
- targets: float32 [4, 256, 3, 256], P('view', 'cell'), may hold values from 0 to 1
- tile_ids: int32 [4, 256], P('view', 'cell'), may hold values from 0 to 255, as said below
- send_slots: int32 [4, 128, 2048], P('view', 'cell'), may hold values from 0 to 2047, as said below
- tile_lists: int32 [4, 256, 512], P('view', 'cell'), may hold values from 0 to 2047, as said below
- tile_len: int32 [4, 256], P('view', 'cell'), may hold values from 0 to 512
Outputs:
- rendered: float32 [4, 256, 3, 256], P('view', 'cell')
- gradient: float32 [59, 262144], P(None, 'cell')
Inputs may be any that keep to these rules, and one draw needn't show every extreme that they name: `params`: row 2 (depth) lies in [2, 8]; row 6 in [0.5, 1]; rows 3 to 5 in [-4.5, -2.8]; row 10 in [-8, 3]; rows 0 and 1 place each Gaussian in front of the camera. `tile_ids`: each view's entries name every window tile once. `send_slots`: for one view, source cell and destination, the live slots come first and name distinct Gaussians of that cell; slots past them hold 0 and no tile list refers to them. `tile_lists`: live entries of one list are distinct live slots of the device owning the tile, nearest first; entries past tile_len are 0.
All inputs are finite; a program needn't handle non-finite values.
Results may differ from a plain program's by a relative error of at most 0.0003.
Values sent between devices are 32-bit elements; how exact they have to be, the bound alone decides.
A program may use at most 64 MiB of HBM per device.

v0:
```python
import jax
import jax.numpy as jnp
from jax import lax
from jax.sharding import PartitionSpec as P

TILE_SIDE = 16
TILE_COLS = 32


focal_length = 800.0
dilation = 0.3
sh_first = 0.28209479177387814
sh_second = 0.4886025119029199
sh_third = (
    1.0925484305920792,
    -1.0925484305920792,
    0.31539156525252005,
    -1.0925484305920792,
    0.5462742152960396,
)
sh_fourth = (
    -0.5900435899266435,
    2.890611442640554,
    -0.4570457994644658,
    0.3731763325901154,
    -0.4570457994644658,
    1.445305721320277,
    -0.5900435899266435,
)


def project(raw_rows, camera):
    pos_x = raw_rows[0] - camera[0]
    pos_y = raw_rows[1] - camera[1]
    depth_cam = raw_rows[2] - camera[2]
    inv_depth = 1.0 / depth_cam
    screen_x = focal_length * pos_x * inv_depth
    screen_y = focal_length * pos_y * inv_depth
    scales = jnp.exp(raw_rows[3:6])
    quaternion = raw_rows[6:10]
    quaternion = quaternion / jnp.sqrt(jnp.sum(quaternion * quaternion, axis=0))
    q_w, q_x, q_y, q_z = (quaternion[0], quaternion[1], quaternion[2], quaternion[3])
    rotation = [
        [
            1.0 - 2.0 * (q_y * q_y + q_z * q_z),
            2.0 * (q_x * q_y - q_w * q_z),
            2.0 * (q_x * q_z + q_w * q_y),
        ],
        [
            2.0 * (q_x * q_y + q_w * q_z),
            1.0 - 2.0 * (q_x * q_x + q_z * q_z),
            2.0 * (q_y * q_z - q_w * q_x),
        ],
        [
            2.0 * (q_x * q_z - q_w * q_y),
            2.0 * (q_y * q_z + q_w * q_x),
            1.0 - 2.0 * (q_x * q_x + q_y * q_y),
        ],
    ]
    jac_diag = focal_length * inv_depth
    jac_x = -screen_x * inv_depth
    jac_y = -screen_y * inv_depth
    row_u = [(jac_diag * rotation[0][j] + jac_x * rotation[2][j]) * scales[j] for j in range(3)]
    row_v = [(jac_diag * rotation[1][j] + jac_y * rotation[2][j]) * scales[j] for j in range(3)]
    cov_xx = row_u[0] * row_u[0] + row_u[1] * row_u[1] + row_u[2] * row_u[2] + dilation
    cov_yy = row_v[0] * row_v[0] + row_v[1] * row_v[1] + row_v[2] * row_v[2] + dilation
    cov_xy = row_u[0] * row_v[0] + row_u[1] * row_v[1] + row_u[2] * row_v[2]
    determinant = cov_xx * cov_yy - cov_xy * cov_xy
    conic_a = cov_yy / determinant
    conic_b = -cov_xy / determinant
    conic_c = cov_xx / determinant
    opacity = jax.nn.sigmoid(raw_rows[10])
    distance = jnp.sqrt(pos_x * pos_x + pos_y * pos_y + depth_cam * depth_cam)
    dir_x = pos_x / distance
    dir_y = pos_y / distance
    dir_z = depth_cam / distance
    dir_xx = dir_x * dir_x
    dir_yy = dir_y * dir_y
    dir_zz = dir_z * dir_z
    sh_basis = jnp.stack(
        [
            sh_first * jnp.ones_like(dir_x),
            -sh_second * dir_y,
            sh_second * dir_z,
            -sh_second * dir_x,
            sh_third[0] * dir_x * dir_y,
            sh_third[1] * dir_y * dir_z,
            sh_third[2] * (2.0 * dir_zz - dir_xx - dir_yy),
            sh_third[3] * dir_x * dir_z,
            sh_third[4] * (dir_xx - dir_yy),
            sh_fourth[0] * dir_y * (3.0 * dir_xx - dir_yy),
            sh_fourth[1] * dir_x * dir_y * dir_z,
            sh_fourth[2] * dir_y * (4.0 * dir_zz - dir_xx - dir_yy),
            sh_fourth[3] * dir_z * (2.0 * dir_zz - 3.0 * dir_xx - 3.0 * dir_yy),
            sh_fourth[4] * dir_x * (4.0 * dir_zz - dir_xx - dir_yy),
            sh_fourth[5] * dir_z * (dir_xx - dir_yy),
            sh_fourth[6] * dir_x * (dir_xx - 3.0 * dir_yy),
        ]
    )
    coeffs = raw_rows[11:59].reshape(3, 16, -1)
    colors = jnp.maximum(jnp.sum(coeffs * sh_basis[None], axis=1) + 0.5, 0.0)
    geometry = jnp.stack([screen_x, screen_y, conic_a, conic_b, conic_c, opacity])
    return jnp.concatenate([geometry, colors], axis=0)


def shade_tile(feature_block, live_mask, pixel_x, pixel_y):
    delta_x = feature_block[0][None, :] - pixel_x[:, None]
    delta_y = feature_block[1][None, :] - pixel_y[:, None]
    exponent = (
        -0.5
        * (
            feature_block[2][None, :] * delta_x * delta_x
            + feature_block[4][None, :] * delta_y * delta_y
        )
        - feature_block[3][None, :] * delta_x * delta_y
    )
    alphas = (feature_block[5] * live_mask)[None, :] * jnp.exp(exponent)
    keep_log = jnp.log1p(-alphas)
    before = jnp.cumsum(keep_log, axis=1) - keep_log
    weights = jnp.exp(before) * alphas
    return jnp.einsum("cl,pl->cp", feature_block[6:9], weights, precision=lax.Precision.HIGHEST)


def pixel_grid(tile_number):
    offsets = jnp.arange(TILE_SIDE * TILE_SIDE, dtype=jnp.int32)
    column = tile_number % TILE_COLS
    row_index = tile_number // TILE_COLS
    pixel_x = (TILE_SIDE * column + offsets % TILE_SIDE).astype(jnp.float32) + 0.5
    pixel_y = (TILE_SIDE * row_index + offsets // TILE_SIDE).astype(jnp.float32) + 0.5
    return (pixel_x, pixel_y)


def sum_views(local_grad):
    return lax.psum(local_grad, "view")


def local(params, cameras, targets, tile_ids, send_slots, tile_lists, tile_len):
    camera = cameras[0]
    slot_rows = send_slots[0, 0]
    depth_len = tile_lists.shape[2]
    projected, pull_owner = jax.vjp(lambda raw_rows: project(raw_rows, camera), params)
    outgoing = jnp.take(projected, slot_rows, axis=1)
    received = lax.all_to_all(outgoing, "cell", split_axis=1, concat_axis=1, tiled=True)

    def one_tile(tile_items):
        tile_number, entries, length, target = tile_items
        gathered = jnp.take(received, entries, axis=1)
        pixel_x, pixel_y = pixel_grid(tile_number)
        live_mask = (jnp.arange(depth_len, dtype=jnp.int32) < length).astype(jnp.float32)
        picture, pull_back = jax.vjp(
            lambda feature_block: shade_tile(feature_block, live_mask, pixel_x, pixel_y), gathered
        )
        return (picture, pull_back(picture - target)[0])

    pictures, entry_grads = lax.map(one_tile, (tile_ids[0], tile_lists[0], tile_len[0], targets[0]))
    flat_entries = tile_lists[0].reshape(-1)
    flat_grads = jnp.transpose(entry_grads, (1, 0, 2)).reshape(entry_grads.shape[1], -1)
    slot_grads = jnp.zeros_like(received).at[:, flat_entries].add(flat_grads)
    returned = lax.all_to_all(slot_grads, "cell", split_axis=1, concat_axis=1, tiled=True)
    gauss_grads = (
        jnp.zeros((returned.shape[0], params.shape[1]), jnp.float32).at[:, slot_rows].add(returned)
    )
    summed = sum_views(pull_owner(gauss_grads)[0])
    return (pictures[None], summed)


def solution(mesh):
    return jax.shard_map(
        local,
        mesh=mesh,
        in_specs=(
            P(None, "cell"),
            P("view", None),
            P("view", "cell", None, None),
            P("view", "cell"),
            P("view", "cell", None),
            P("view", "cell", None),
            P("view", "cell"),
        ),
        out_specs=(P("view", "cell", None, None), P(None, "cell")),
        check_vma=False,
    )
```

profile of v0, /device:TPU:1, one launch (start us, length us, event | category | flops | bytes accessed | tf_op | source)
XLA Modules:
  0.0 270.3 jit_solution(1962463132966548270)
XLA Ops:
  7.2 0.9 multiply_reduce_fusion.4
  8.1 0.9 slice_exponential_fusion
  9.0 1.1 slice.158
  10.7 0.9 slice_divide_fusion
  12.3 3.8 %multiply_multiply_fusion.10 = (f32[1,2048]{1,0:T(1,128)S(1)}, f32[1,2048]{1,0:T(1,128)S(1)}, f32[1,2048]{1,0:T(1,128)S(1)}, f32[1,2048]{1,0:T(1,128)S(1)}, f32[...) fusion(f32[]{:T(128)} %bitcast.30, ...), kind=kLoop, calls=%fused_computation.224 | loop fusion | flops 206848 | bytes 278540 | tf_op jit(solution)/shard_map/jvp()/mul | solution.py:97
  16.1 3.4 %multiply_multiply_fusion.11 = (f32[1,2048]{1,0:T(1,128)S(1)}, f32[1,2048]{1,0:T(1,128)S(1)}, f32[1,2048]{1,0:T(1,128)S(1)}, f32[1,2048]{1,0:T(1,128)S(1)}, f32[...) fusion(f32[1,2048]{1,0:T(1,128)S(1)} %get-tuple-element.201, ...), kind=kLoop, calls=%fused_computation.225 | loop fusion | flops 51200 | bytes 172044 | tf_op jit(solution)/shard_map/jvp()/mul | solution.py:96
  21.5 1.1 copy.380
  22.6 2.1 copy.381
  24.7 2.0 copy.382
  26.7 2.0 copy.383
  28.7 1.4 copy.385
  30.1 2.1 copy.384
  33.3 2.0 reduce.3
  35.3 1.4 squeeze.72
  36.7 1.5 compare_and_fusion.1
  38.1 5.0 %concatenate.3 = f32[9,2048]{0,1:T(8,128)} concatenate(f32[1,2048]{0,1:T(8,128)S(1)} %copy.380, f32[1,2048]{0,1:T(8,128)} %copy.381, f32[1,2048]{0,1:T(8,128)} %copy.382, f32[1,2048]{0,1:T(8,128)} %copy.383, f32[1,2048]{0,1:T(8,128)} %copy.384, f32[1,2048]{0,1:T(8,128)} %copy.385, f32[3,2048]{0,1:T(8,128)S(1)} %add_maximum_fusion), dimensions={0} | concatenate | bytes 147456 | tf_op jit(solution)/shard_map/jvp()/concatenate | solution.py:103
  43.1 6.7 %gather_fusion.1 = f32[2048,9]{1,0:T(8,128)S(1)} fusion(f32[9,2048]{0,1:T(8,128)} %concatenate.3, s32[2048]{0:T(1024)S(1)} %broadcast_clamp_fusion), kind=kCustom, calls=%fused_computation.1 | custom fusion | bytes 155648 | tf_op jit(solution)/shard_map/jit(_take)/gather | solution.py:142
  49.8 1.1 fusion.81
  50.8 1.4 reshape.400
  52.3 18.6 %all-to-all-start = ((f32[128,1,144]{2,1,0:T(1,128)}), f32[128,1,144]{2,1,0:T(1,128)S(1)}, u32[]{:S(2)}, u32[]{:S(2)}) async-start(f32[128,1,144]{2,1,0:T(1,128)} %reshape.400), calls=%async_computation | async-start | bytes 262144 | tf_op jit(solution)/shard_map/all_to_all | solution.py:143
  71.7 11.3 %all-to-all-done = f32[128,1,144]{2,1,0:T(1,128)S(1)} async-done(((f32[128,1,144]{2,1,0:T(1,128)}), f32[128,1,144]{2,1,0:T(1,128)S(1)}, u32[]{:S(2)}, u32[]{:S(2)}) %all-to-all-start) | async-done | bytes 73760 | tf_op jit(solution)/shard_map/all_to_all | solution.py:143
  83.6 0.9 reduce.4
  84.5 1.6 reshape.401
  86.8 44.3 %while.15 = (s32[]{:T(128)}, f32[2,3,256]{2,0,1:T(2,128)}, f32[2,9,512]{2,1,0:T(8,128)}, s32[2,512]{1,0:T(2,128)S(1)}, f32[9,2048]{0,1:T(8,128)}, /*index=5*/s32...) while((s32[]{:T(128)}, f32[2,3,256]{2,0,1:T(2,128)}, ...), condition=%wide.region_13.14_spmd, body=%wide.region_2.13_spmd.sunk | while | flops 62047768 | bytes 13186664 | solution.py:155
  90.1 2.3 gather_fusion
  94.3 0.9 fusion.101
  95.7 1.0 fusion.102
  96.7 1.5 fusion.105
  98.2 1.8 multiply_multiply_fusion.22
  100.4 2.2 fusion.103
  103.7 1.9 fusion.104
  112.2 2.3 gather_fusion
  116.5 0.9 fusion.101
  117.8 1.0 fusion.102
  118.9 1.5 fusion.105
  120.4 1.8 multiply_multiply_fusion.22
  122.6 2.2 fusion.103
  125.8 1.9 fusion.104
  131.1 0.9 copy.388
  132.2 7.4 %scatter_custom_fusion = f32[9,2048]{0,1:T(8,128)S(1)} fusion(s32[1024]{0:T(1024)} %bitcast.272, f32[1024,9]{1,0:T(8,128)S(1)} %copy.389, f32[]{:T(128)} %constant.214.clone.1), kind=kCustom, calls=%fused_computation.105 | custom fusion | flops 9216 | bytes 74240 | tf_op jit(solution)/shard_map/scatter-add | solution.py:158
  140.4 17.6 %all_to_all.21 = f32[128,1,144]{2,1,0:T(1,128)S(1)} all-to-all(f32[128,1,144]{2,1,0:T(1,128)S(1)} %reshape.402), channel_id=1, replica_groups=mesh['cell'=128,'view'=4] {'cell'}, dimensions={0} | all-to-all | bytes 147456 | tf_op jit(solution)/shard_map/all_to_all | solution.py:159
  158.0 0.9 reduce.5
  159.6 12.0 %scatter_custom_fusion.1 = f32[9,2048]{0,1:T(8,128)S(1)} fusion(s32[2048]{0:T(1024)} %bitcast.269, f32[2048,9]{1,0:T(8,128)S(1)} %bitcast.219, f32[]{:T(128)} %constant.214.clone.1), kind=kCustom, calls=%fused_computation.103 | custom fusion | flops 18432 | bytes 74240 | tf_op jit(solution)/shard_map/scatter-add | solution.py:161
  171.5 3.8 %fusion.79 = (f32[1,2048]{0,1:T(8,128)S(1)}, f32[1,2048]{0,1:T(8,128)}, f32[1,2048]{0,1:T(8,128)}, f32[1,2048]{0,1:T(8,128)}, f32[1,2048]{0,1:T(8,128)}, /*index=5*/f32[1,2048]{0,1:T(8,128)}) fusion(f32[9,2048]{0,1:T(8,128)S(1)} %scatter_custom_fusion.1), kind=kLoop, calls=%fused_computation.263 | loop fusion | bytes 98304 | tf_op jit(solution)/shard_map/transpose(jvp())/unstack | solution.py:102
  175.3 2.1 copy.400
  177.5 2.1 copy.401
  179.6 2.2 copy.402
  181.8 0.9 multiply_add_fusion.7
  183.6 2.9 %add_add_fusion.9 = (f32[1,2048]{1,0:T(1,128)S(1)}, f32[1,2048]{1,0:T(1,128)S(1)}, f32[1,2048]{1,0:T(1,128)}, f32[1,2048]{1,0:T(1,128)S(1)}, f32[1,2048]{1,0:T(1...) fusion(f32[4,2048]{1,0:T(4,128)S(1)} %copy-done.3, ...), kind=kLoop, calls=%fused_computation.130 | loop fusion | flops 165888 | bytes 262152 | tf_op jit(solution)/shard_map/transpose(jvp())/add_any | solution.py:45
  186.5 2.2 add_add_fusion.8
  188.7 2.2 multiply_add_fusion.5
  191.0 2.2 multiply_add_fusion.4
  193.2 1.3 slice_multiply_fusion
  194.5 1.0 multiply_reduce_fusion.3
  196.2 1.6 add_add_fusion
  197.8 2.2 copy.390
  200.0 2.5 broadcast_multiply_fusion
  203.8 3.3 %fusion.65 = (f32[1,2048]{1,0:T(1,128)S(1)}, f32[1,2048]{1,0:T(1,128)S(1)}, f32[1,2048]{1,0:T(1,128)S(1)}, f32[1,2048]{1,0:T(1,128)S(1)}) fusion(f32[1,2048]{1,0:T(1,128)S(1)} %copy-done.18, f32[1,2048]{1,0:T(1,128)S(1)} %copy-done.16, f32[1,2048]{1,0:T(1,128)S(1)} %get-tuple-element.187, f32[1,2048]{1,0:T(1,128)S(1)} %copy-done.24, ...), kind=kLoop, calls=%fused_computation.147 | loop fusion | flops 436224 | bytes 335884 | tf_op jit(solution)/shard_map/transpose(jvp())/add_any | solution.py:36
  207.1 1.5 fusion.66
  208.6 1.6 fusion.67
  215.2 0.9 add_multiply_fusion
  216.1 0.9 pad_add_fusion
  217.0 44.6 %all-reduce.26.cloned.1.call-done = f32[59,2048]{1,0:T(8,128)} async-done(((f32[59,2048]{1,0:T(8,128)}), f32[59,2048]{1,0:T(8,128)}) %all-reduce.26.cloned.1.call-update) | async-done | bytes 483344 | tf_op jit(solution)/shard_map/psum | solution.py:134
  261.6 1.9 copy.484
  (332 shorter events, 30.9 us)
Async XLA Ops:
  8.1 2.0 copy-start.54
  9.0 3.3 %copy-start.28 = (f32[3,2048]{1,0:T(4,128)}, f32[3,2048]{1,0:T(4,128)S(1)}, u32[]{:S(2)}) copy-start(f32[3,2048]{1,0:T(4,128)S(1)} %slice_exponential_fusion) | copy-start | bytes 73732
  10.7 0.9 copy-start.52
  10.7 1.0 copy-start.86
  11.6 4.4 %copy-start.2 = (f32[4,2048]{1,0:T(4,128)}, f32[4,2048]{1,0:T(4,128)S(1)}, u32[]{:S(2)}) copy-start(f32[4,2048]{1,0:T(4,128)S(1)} %slice_divide_fusion) | copy-start | bytes 98308
  16.0 3.5 %copy-start.31 = (f32[1,2048]{1,0:T(1,128)}, f32[1,2048]{1,0:T(1,128)S(1)}, u32[]{:S(2)}) copy-start(f32[1,2048]{1,0:T(1,128)S(1)} %get-tuple-element.202) | copy-start | bytes 24580
  16.1 3.5 %copy-start.36 = (f32[1,2048]{1,0:T(1,128)}, f32[1,2048]{1,0:T(1,128)S(1)}, u32[]{:S(2)}) copy-start(f32[1,2048]{1,0:T(1,128)S(1)} %get-tuple-element.250) | copy-start | bytes 24580
  16.1 3.5 %copy-start.38 = (f32[1,2048]{1,0:T(1,128)}, f32[1,2048]{1,0:T(1,128)S(1)}, u32[]{:S(2)}) copy-start(f32[1,2048]{1,0:T(1,128)S(1)} %get-tuple-element.251) | copy-start | bytes 24580
  16.1 3.5 %copy-start.40 = (f32[1,2048]{1,0:T(1,128)}, f32[1,2048]{1,0:T(1,128)S(1)}, u32[]{:S(2)}) copy-start(f32[1,2048]{1,0:T(1,128)S(1)} %get-tuple-element.252) | copy-start | bytes 24580
  16.1 3.5 %copy-start.42 = (f32[1,2048]{1,0:T(1,128)}, f32[1,2048]{1,0:T(1,128)S(1)}, u32[]{:S(2)}) copy-start(f32[1,2048]{1,0:T(1,128)S(1)} %get-tuple-element.200) | copy-start | bytes 24580
  16.1 3.5 %copy-start.44 = (f32[1,2048]{1,0:T(1,128)}, f32[1,2048]{1,0:T(1,128)S(1)}, u32[]{:S(2)}) copy-start(f32[1,2048]{1,0:T(1,128)S(1)} %get-tuple-element.201) | copy-start | bytes 24580
  19.6 9.1 %copy-start.50 = (f32[1,2048]{1,0:T(1,128)}, f32[1,2048]{1,0:T(1,128)S(1)}, u32[]{:S(2)}) copy-start(f32[1,2048]{1,0:T(1,128)S(1)} %get-tuple-element.248) | copy-start | bytes 24580
  30.1 2.1 copy-start.81
  52.3 18.8 %copy-start.85 = (f32[1,2,3,256]{3,1,2,0:T(2,128)S(1)}, f32[1,2,3,256]{3,1,2,0:T(2,128)}, u32[]{:S(2)}) copy-start(f32[1,2,3,256]{3,1,2,0:T(2,128)} %param.11) | copy-start | bytes 18436
  52.3 18.8 %copy-start.60 = (s32[1,2,512]{2,1,0:T(2,128)S(1)}, s32[1,2,512]{2,1,0:T(2,128)}, u32[]{:S(2)}) copy-start(s32[1,2,512]{2,1,0:T(2,128)} %param.14) | copy-start | bytes 12292
  52.3 30.8 %all-to-all-start = ((f32[128,1,144]{2,1,0:T(1,128)}), f32[128,1,144]{2,1,0:T(1,128)S(1)}, u32[]{:S(2)}, u32[]{:S(2)}) async-start(f32[128,1,144]{2,1,0:T(1,128)} %reshape.400), calls=%async_computation | async-start | bytes 262144 | tf_op jit(solution)/shard_map/all_to_all | solution.py:143
  70.8 190.8 %all-reduce.26.cloned.1.call-start = ((), (), s32[]{:S(2)}) async-start(), calls=%async_computation.2 | async-start | bytes 1048576 | tf_op jit(solution)/shard_map/psum | solution.py:134
  86.8 9.9 %copy-start.83 = (f32[2,3,256]{2,1,0:T(4,128)}, f32[2,3,256]{2,1,0:T(4,128)S(1)}, u32[]{:S(2)}) copy-start(f32[2,3,256]{2,1,0:T(4,128)S(1)} %get-tuple-element.416) | copy-start | bytes 18436 | tf_op jit(solution)/shard_map/while
  90.0 6.7 %copy-start.25 = (f32[256]{0:T(256)}, f32[256]{0:T(256)S(1)}, u32[]{:S(2)}) copy-start(f32[256]{0:T(256)S(1)} %get-tuple-element.362) | copy-start | bytes 3076 | tf_op jit(solution)/shard_map/while
  90.0 6.7 %copy-start.27 = (f32[256]{0:T(256)}, f32[256]{0:T(256)S(1)}, u32[]{:S(2)}) copy-start(f32[256]{0:T(256)S(1)} %get-tuple-element.365) | copy-start | bytes 3076 | tf_op jit(solution)/shard_map/while
  92.5 3.2 %copy-start.6 = (f32[9,512]{1,0:T(8,128)}, f32[9,512]{1,0:T(8,128)S(1)}, u32[]{:S(2)}) copy-start(f32[9,512]{1,0:T(8,128)S(1)} %select_bitcast_fusion.2) | copy-start | bytes 55300 | tf_op jit(solution)/shard_map/while
  93.6 3.1 %copy-start.10 = (f32[1,512]{1,0:T(1,128)}, f32[1,512]{1,0:T(1,128)S(1)}, u32[]{:S(2)}) copy-start(f32[1,512]{1,0:T(1,128)S(1)} %get-tuple-element.363) | copy-start | bytes 6148 | tf_op jit(solution)/shard_map/while
  93.6 3.1 %copy-start.12 = (f32[1,512]{1,0:T(1,128)}, f32[1,512]{1,0:T(1,128)S(1)}, u32[]{:S(2)}) copy-start(f32[1,512]{1,0:T(1,128)S(1)} %get-tuple-element.364) | copy-start | bytes 6148 | tf_op jit(solution)/shard_map/while
  93.6 3.1 %copy-start.13 = (f32[1,512]{1,0:T(1,128)}, f32[1,512]{1,0:T(1,128)S(1)}, u32[]{:S(2)}) copy-start(f32[1,512]{1,0:T(1,128)S(1)} %get-tuple-element.366) | copy-start | bytes 6148 | tf_op jit(solution)/shard_map/while
  93.7 3.1 %copy-start.14 = (f32[1,512]{1,0:T(1,128)}, f32[1,512]{1,0:T(1,128)S(1)}, u32[]{:S(2)}) copy-start(f32[1,512]{1,0:T(1,128)S(1)} %get-tuple-element.367) | copy-start | bytes 6148 | tf_op jit(solution)/shard_map/while
  96.6 1.6 copy-start.46
  96.7 1.5 copy-start.7
  103.7 2.5 copy-start.58
  106.9 1.4 copy-start.59
  108.9 9.9 %copy-start.83 = (f32[2,3,256]{2,1,0:T(4,128)}, f32[2,3,256]{2,1,0:T(4,128)S(1)}, u32[]{:S(2)}) copy-start(f32[2,3,256]{2,1,0:T(4,128)S(1)} %get-tuple-element.416) | copy-start | bytes 18436 | tf_op jit(solution)/shard_map/while
  112.1 6.7 %copy-start.25 = (f32[256]{0:T(256)}, f32[256]{0:T(256)S(1)}, u32[]{:S(2)}) copy-start(f32[256]{0:T(256)S(1)} %get-tuple-element.362) | copy-start | bytes 3076 | tf_op jit(solution)/shard_map/while
  112.1 6.7 %copy-start.27 = (f32[256]{0:T(256)}, f32[256]{0:T(256)S(1)}, u32[]{:S(2)}) copy-start(f32[256]{0:T(256)S(1)} %get-tuple-element.365) | copy-start | bytes 3076 | tf_op jit(solution)/shard_map/while
  114.6 3.2 %copy-start.6 = (f32[9,512]{1,0:T(8,128)}, f32[9,512]{1,0:T(8,128)S(1)}, u32[]{:S(2)}) copy-start(f32[9,512]{1,0:T(8,128)S(1)} %select_bitcast_fusion.2) | copy-start | bytes 55300 | tf_op jit(solution)/shard_map/while
  115.8 3.1 %copy-start.10 = (f32[1,512]{1,0:T(1,128)}, f32[1,512]{1,0:T(1,128)S(1)}, u32[]{:S(2)}) copy-start(f32[1,512]{1,0:T(1,128)S(1)} %get-tuple-element.363) | copy-start | bytes 6148 | tf_op jit(solution)/shard_map/while
  115.8 3.1 %copy-start.12 = (f32[1,512]{1,0:T(1,128)}, f32[1,512]{1,0:T(1,128)S(1)}, u32[]{:S(2)}) copy-start(f32[1,512]{1,0:T(1,128)S(1)} %get-tuple-element.364) | copy-start | bytes 6148 | tf_op jit(solution)/shard_map/while
  115.8 3.1 %copy-start.13 = (f32[1,512]{1,0:T(1,128)}, f32[1,512]{1,0:T(1,128)S(1)}, u32[]{:S(2)}) copy-start(f32[1,512]{1,0:T(1,128)S(1)} %get-tuple-element.366) | copy-start | bytes 6148 | tf_op jit(solution)/shard_map/while
  115.8 3.1 %copy-start.14 = (f32[1,512]{1,0:T(1,128)}, f32[1,512]{1,0:T(1,128)S(1)}, u32[]{:S(2)}) copy-start(f32[1,512]{1,0:T(1,128)S(1)} %get-tuple-element.367) | copy-start | bytes 6148 | tf_op jit(solution)/shard_map/while
  118.8 1.6 copy-start.46
  118.9 1.5 copy-start.7
  125.8 2.5 copy-start.58
  129.0 1.4 copy-start.59
  179.6 2.2 copy-start.37
  181.8 0.9 copy-start.39
  181.8 1.0 copy-start.41
  181.8 1.0 copy-start.48
  181.8 1.0 copy-start.49
  181.8 1.0 copy-start.71
  181.8 1.0 copy-start.72
  181.8 1.0 copy-start.73
  181.8 1.0 copy-start.74
  186.5 4.5 %copy-start.15 = (f32[1,2048]{1,0:T(1,128)}, f32[1,2048]{1,0:T(1,128)S(1)}, u32[]{:S(2)}) copy-start(f32[1,2048]{1,0:T(1,128)S(1)} %get-tuple-element.189) | copy-start | bytes 24580
  186.5 4.5 %copy-start.17 = (f32[1,2048]{1,0:T(1,128)}, f32[1,2048]{1,0:T(1,128)S(1)}, u32[]{:S(2)}) copy-start(f32[1,2048]{1,0:T(1,128)S(1)} %get-tuple-element.191) | copy-start | bytes 24580
  186.5 4.5 %copy-start.19 = (f32[1,2048]{1,0:T(1,128)}, f32[1,2048]{1,0:T(1,128)S(1)}, u32[]{:S(2)}) copy-start(f32[1,2048]{1,0:T(1,128)S(1)} %get-tuple-element.181) | copy-start | bytes 24580
  186.5 4.5 %copy-start.21 = (f32[1,2048]{1,0:T(1,128)}, f32[1,2048]{1,0:T(1,128)S(1)}, u32[]{:S(2)}) copy-start(f32[1,2048]{1,0:T(1,128)S(1)} %get-tuple-element.183) | copy-start | bytes 24580
  186.5 4.5 %copy-start.23 = (f32[1,2048]{1,0:T(1,128)}, f32[1,2048]{1,0:T(1,128)S(1)}, u32[]{:S(2)}) copy-start(f32[1,2048]{1,0:T(1,128)S(1)} %get-tuple-element.185) | copy-start | bytes 24580
  193.2 1.3 copy-start.68
  194.5 1.0 copy-start.55
  197.8 4.7 %copy-start.1 = (f32[1,2048]{0,1:T(8,128)S(1)}, f32[1,2048]{0,1:T(8,128)}, u32[]{:S(2)}) copy-start(f32[1,2048]{0,1:T(8,128)} %get-tuple-element.236) | copy-start | bytes 24580
  200.0 2.8 %copy-start = (f32[1,2048]{0,1:T(8,128)S(1)}, f32[1,2048]{0,1:T(8,128)}, u32[]{:S(2)}) copy-start(f32[1,2048]{0,1:T(8,128)} %get-tuple-element.240) | copy-start | bytes 24580
  202.8 0.9 copy-start.9
  202.8 0.9 copy-start.16
  202.8 0.9 copy-start.18
  210.2 5.9 %copy-start.5 = (f32[3,16,2048]{2,1,0:T(8,128)S(1)}, f32[3,16,2048]{2,1,0:T(8,128)}, u32[]{:S(2)}) copy-start(f32[3,16,2048]{2,1,0:T(8,128)} %get-tuple-element.269) | copy-start | bytes 1179652
  215.2 0.9 copy-start.33
  (53 other events, 38.6 us)
Sparse Core Ops, SparseCore 0:
  217.1 44.4 all-reduce.25
where the time goes:
time: 275 us; the launch traced here: 270 us
  local copies, waits for them, and re-layouts  74.7 us (27%)
  other arithmetic  74 us (27%)
  waiting for transfers between devices  55.9 us (20%)
  starting transfers between devices  18.8 us (7%)
  blocking collectives  17.6 us (6%)
  between operations  14.9 us (5%)
  matrix products  8.49 us (3%)
  loops' own time  6 us (2%)
    psum x1, waiting for transfers between devices, sum_views(): return lax.psum(local_grad, 'view')  44.6 us
    unnamed x158, local copies, waits for them, and re-layouts  23.1 us
    all_to_all x1, starting transfers between devices, local(): lax.all_to_all(outgoing, 'cell', split_axis=1, concat_axis=1, tiled=True)  18.6 us
    all_to_all x1, blocking collectives, local(): lax.all_to_all(slot_grads, 'cell', split_axis=1, concat_axis=1, tiled=True)  17.6 us
    scatter-add x1, other arithmetic, local(): jnp.zeros((returned.shape[0], params.shape[1]), jnp.float32)  12 us
    all_to_all x1, waiting for transfers between devices, local(): lax.all_to_all(outgoing, 'cell', split_axis=1, concat_axis=1, tiled=True)  11.3 us
    dot_general x6, matrix products, shade_tile(): jnp.einsum('cl,pl->cp', feature_block[6:9], weights, precision=lax.Precis...  8.49 us
    scatter-add x1, other arithmetic, local(): slot_grads = jnp.zeros_like(received).at[:, flat_entries].add(flat_grads)  7.43 us
  transfers between devices with their start and end apart: 2, of which 2 were waited for; matrix products, arithmetic and copies ran while one was open for 0% of the time, Pallas kernels for 0%

commit v1 on v0

v1 whole, which is shorter than its diff:
```python
import functools

import jax
import jax.numpy as jnp
from jax import lax
from jax.experimental import pallas as pl
from jax.experimental.pallas import tpu as pltpu
from jax.sharding import PartitionSpec as P

TILE_SIDE = 16
TILE_COLS = 32
LANES = 128
Y_DEVS = 8
ZC_DEVS = 16
VIEW_DEVS = 4
FEATS = 9
F32 = jnp.float32
BF16 = jnp.bfloat16

focal_length = 800.0
dilation = 0.3
sh_first = 0.28209479177387814
sh_second = 0.4886025119029199
sh_third = (
    1.0925484305920792,
    -1.0925484305920792,
    0.31539156525252005,
    -1.0925484305920792,
    0.5462742152960396,
)
sh_fourth = (
    -0.5900435899266435,
    2.890611442640554,
    -0.4570457994644658,
    0.3731763325901154,
    -0.4570457994644658,
    1.445305721320277,
    -0.5900435899266435,
)


def split2(value):
    high = value.astype(BF16)
    return high, (value - high.astype(F32)).astype(BF16)


def split3(value):
    high = value.astype(BF16).astype(F32)
    rest = value - high
    mid = rest.astype(BF16).astype(F32)
    return high, mid, rest - mid


def dot_nt(lhs, rhs):
    return lax.dot_general(lhs, rhs, (((1,), (1,)), ((), ())), preferred_element_type=F32)


def dot_nn(lhs, rhs):
    return lax.dot_general(lhs, rhs, (((1,), (0,)), ((), ())), preferred_element_type=F32)


def rotation_of(q_w, q_x, q_y, q_z):
    return [
        1.0 - 2.0 * (q_y * q_y + q_z * q_z),
        2.0 * (q_x * q_y - q_w * q_z),
        2.0 * (q_x * q_z + q_w * q_y),
        2.0 * (q_x * q_y + q_w * q_z),
        1.0 - 2.0 * (q_x * q_x + q_z * q_z),
        2.0 * (q_y * q_z - q_w * q_x),
        2.0 * (q_x * q_z - q_w * q_y),
        2.0 * (q_y * q_z + q_w * q_x),
        1.0 - 2.0 * (q_x * q_x + q_y * q_y),
    ]


def unit_quaternion(quaternion):
    total = sum(part * part for part in quaternion[1:]) + quaternion[0] * quaternion[0]
    inverse = lax.rsqrt(total)
    return [part * inverse for part in quaternion], inverse


def shape_matrix(log_scales, quaternion):
    scales = [jnp.exp(part) for part in log_scales]
    unit, inverse = unit_quaternion(quaternion)
    rotation = rotation_of(*unit)
    matrix = [rotation[3 * i + j] * scales[j] for i in range(3) for j in range(3)]
    return matrix, scales, unit, inverse


def harmonics(x, y, z):
    xx, yy, zz = x * x, y * y, z * z
    rim = 4.0 * zz - xx - yy
    gap = xx - yy
    return [
        -sh_second * y,
        sh_second * z,
        -sh_second * x,
        sh_third[0] * (x * y),
        sh_third[1] * (y * z),
        sh_third[2] * (2.0 * zz - xx - yy),
        sh_third[3] * (x * z),
        sh_third[4] * gap,
        sh_fourth[0] * (y * (3.0 * xx - yy)),
        sh_fourth[1] * (x * y * z),
        sh_fourth[2] * (y * rim),
        sh_fourth[3] * (z * (2.0 * zz - 3.0 * xx - 3.0 * yy)),
        sh_fourth[4] * (x * rim),
        sh_fourth[5] * (z * gap),
        sh_fourth[6] * (x * (xx - 3.0 * yy)),
    ]


def geometry(pos, matrix):
    x, y, z = pos
    inv_z = 1.0 / z
    jac = focal_length * inv_z
    screen_x = x * jac
    screen_y = y * jac
    jac_x = -screen_x * inv_z
    jac_y = -screen_y * inv_z
    row_u = [jac * matrix[j] + jac_x * matrix[6 + j] for j in range(3)]
    row_v = [jac * matrix[3 + j] + jac_y * matrix[6 + j] for j in range(3)]
    cov_a = row_u[0] * row_u[0] + row_u[1] * row_u[1] + row_u[2] * row_u[2] + dilation
    cov_c = row_v[0] * row_v[0] + row_v[1] * row_v[1] + row_v[2] * row_v[2] + dilation
    cov_b = row_u[0] * row_v[0] + row_u[1] * row_v[1] + row_u[2] * row_v[2]
    inv_det = 1.0 / (cov_a * cov_c - cov_b * cov_b)
    return inv_z, jac, screen_x, screen_y, jac_x, jac_y, row_u, row_v, cov_a, cov_b, cov_c, inv_det


def direction(pos):
    x, y, z = pos
    inverse = lax.rsqrt(x * x + y * y + z * z)
    return [x * inverse, y * inverse, z * inverse], inverse


def raw_colour(load, channel, basis):
    total = load(11 + 16 * channel) * sh_first
    for j in range(15):
        total = total + load(12 + 16 * channel + j) * basis[j]
    return total + 0.5


def lane_gather(source, index):
    return jnp.take_along_axis(source, index, axis=1, mode="promise_in_bounds")


def gather_chunk(table, high, low):
    shape = (8, LANES)
    low = jnp.broadcast_to(low, shape)
    high = jnp.broadcast_to(high, shape)
    top = bottom = jnp.zeros(shape, F32)
    for chunk in range(16):
        here = high == chunk
        top = jnp.where(here, lane_gather(table[pl.ds(16 * chunk, 8), :], low), top)
        bottom = jnp.where(here, lane_gather(table[pl.ds(16 * chunk + 8, 8), :], low), bottom)
    return top, bottom


def project_kernel(camera, params, slots, dense, outgoing, packed, table):
    rows = params.shape[0]
    for group in range(0, rows, 8):
        size = min(8, rows - group)
        for chunk in range(16):
            packed[pl.ds(group * 16 + chunk * 8, size), :] = params[
                pl.ds(group, size), pl.ds(chunk * LANES, LANES)
            ]
    for row in range(rows):
        dense[row] = packed[pl.ds((row // 8) * 128 + row % 8, 16, stride=8), :]
    table[...] = jnp.zeros_like(table)

    load = lambda row: dense[row]
    pos = [load(i) - camera[0, i] for i in range(3)]
    matrix, _, _, _ = shape_matrix([load(3 + i) for i in range(3)], [load(6 + i) for i in range(4)])
    _, _, screen_x, screen_y, _, _, _, _, cov_a, cov_b, cov_c, inv_det = geometry(pos, matrix)
    unit, _ = direction(pos)
    basis = harmonics(*unit)
    features = [
        screen_x,
        screen_y,
        cov_c * inv_det,
        -cov_b * inv_det,
        cov_a * inv_det,
        1.0 / (1.0 + jnp.exp(-load(10))),
    ]
    features += [jnp.maximum(raw_colour(load, channel, basis), 0.0) for channel in range(3)]
    for i, feature in enumerate(features):
        table[pl.ds(i, 16, stride=16), :] = feature

    def one_chunk(chunk, carry):
        index = slots[0, :, pl.ds(pl.multiple_of(chunk * LANES, LANES), LANES)]
        top, bottom = gather_chunk(table, index >> 7, index & 127)
        outgoing[chunk, pl.ds(0, 8), :] = top
        outgoing[chunk, pl.ds(8, 1), :] = bottom[0:1]
        return carry

    lax.fori_loop(0, 16, one_chunk, 0, unroll=2)


def project_call(camera, params, slots):
    rows = params.shape[0]
    return pl.pallas_call(
        project_kernel,
        out_shape=(
            jax.ShapeDtypeStruct((rows, 16, LANES), F32),
            jax.ShapeDtypeStruct((16, FEATS, LANES), F32),
        ),
        in_specs=[
            pl.BlockSpec(memory_space=pltpu.SMEM),
            pl.BlockSpec(memory_space=pltpu.VMEM),
            pl.BlockSpec(memory_space=pltpu.VMEM),
        ],
        out_specs=(pl.BlockSpec(memory_space=pltpu.VMEM),) * 2,
        scratch_shapes=[pltpu.VMEM((64 * 16, LANES), F32), pltpu.VMEM((256, LANES), F32)],
        compiler_params=pltpu.CompilerParams(vmem_limit_bytes=24 * 2**20),
        name="project",
    )(camera, params, slots)


def block_transpose(rows):
    group = lax.broadcasted_iota(jnp.int32, rows[0].shape, 1) // 16
    for step in (1, 2, 4):
        odd = (group & step) != 0
        fresh = list(rows)
        for i in range(8):
            if i & step:
                continue
            first, second = rows[i], rows[i + step]
            fresh[i] = jnp.where(odd, pltpu.roll(second, 16 * step, 1), first)
            fresh[i + step] = jnp.where(odd, second, pltpu.roll(first, LANES - 16 * step, 1))
        rows = fresh
    return rows


def greet(my_y, my_zc):
    barrier = pltpu.get_barrier_semaphore()
    for k in range(1, Y_DEVS):
        pl.semaphore_signal(
            barrier,
            inc=1,
            device_id={"cell": lax.rem(my_y + k, Y_DEVS) * ZC_DEVS + my_zc},
            device_id_type=pl.DeviceIdType.MESH,
        )
    for k in range(1, ZC_DEVS):
        pl.semaphore_signal(
            barrier,
            inc=1,
            device_id={"cell": my_y * ZC_DEVS + lax.rem(my_zc + k, ZC_DEVS)},
            device_id_type=pl.DeviceIdType.MESH,
        )
    return barrier


def forward_kernel(outgoing, received, landed, staged, send_y, recv_y, send_zc, recv_zc):
    cell = lax.axis_index("cell")
    my_y, my_zc = cell // ZC_DEVS, lax.rem(cell, ZC_DEVS)
    barrier = greet(my_y, my_zc)
    pl.semaphore_wait(barrier, Y_DEVS + ZC_DEVS - 2)
    copies = []
    for k in range(1, Y_DEVS):
        peer = lax.rem(my_y + k, Y_DEVS)
        copy = pltpu.make_async_remote_copy(
            src_ref=outgoing.at[pl.ds(2 * peer, 2)],
            dst_ref=landed.at[my_y],
            send_sem=send_y.at[k - 1],
            recv_sem=recv_y.at[k - 1],
            device_id={"cell": peer * ZC_DEVS + my_zc},
            device_id_type=pl.DeviceIdType.MESH,
        )
        copy.start()
        copies.append(copy)
    landed[my_y] = outgoing[pl.ds(2 * my_y, 2)]
    for copy in copies:
        copy.wait()
    for half in range(2):
        rows = block_transpose([landed[y, half] for y in range(Y_DEVS)])
        for i in range(8):
            staged[8 * half + i] = rows[i]
    copies = []
    for k in range(1, ZC_DEVS):
        peer = lax.rem(my_zc + k, ZC_DEVS)
        copy = pltpu.make_async_remote_copy(
            src_ref=staged.at[peer],
            dst_ref=received.at[my_zc],
            send_sem=send_zc.at[k - 1],
            recv_sem=recv_zc.at[k - 1],
            device_id={"cell": my_y * ZC_DEVS + peer},
            device_id_type=pl.DeviceIdType.MESH,
        )
        copy.start()
        copies.append(copy)
    received[my_zc] = staged[my_zc]
    for copy in copies:
        copy.wait()


def backward_kernel(slot_grads, returned, landed, staged, send_y, recv_y, send_zc, recv_zc):
    cell = lax.axis_index("cell")
    my_y, my_zc = cell // ZC_DEVS, lax.rem(cell, ZC_DEVS)
    barrier = greet(my_y, my_zc)
    pl.semaphore_wait(barrier, Y_DEVS + ZC_DEVS - 2)
    copies = []
    for k in range(1, ZC_DEVS):
        peer = lax.rem(my_zc + k, ZC_DEVS)
        copy = pltpu.make_async_remote_copy(
            src_ref=slot_grads.at[peer],
            dst_ref=landed.at[my_zc],
            send_sem=send_zc.at[k - 1],
            recv_sem=recv_zc.at[k - 1],
            device_id={"cell": my_y * ZC_DEVS + peer},
            device_id_type=pl.DeviceIdType.MESH,
        )
        copy.start()
        copies.append(copy)
    landed[my_zc] = slot_grads[my_zc]
    for copy in copies:
        copy.wait()
    for half in range(2):
        rows = block_transpose([landed[8 * half + i] for i in range(8)])
        for y in range(Y_DEVS):
            staged[y, half] = rows[y]
    copies = []
    for k in range(1, Y_DEVS):
        peer = lax.rem(my_y + k, Y_DEVS)
        copy = pltpu.make_async_remote_copy(
            src_ref=staged.at[peer],
            dst_ref=returned.at[pl.ds(2 * my_y, 2)],
            send_sem=send_y.at[k - 1],
            recv_sem=recv_y.at[k - 1],
            device_id={"cell": peer * ZC_DEVS + my_zc},
            device_id_type=pl.DeviceIdType.MESH,
        )
        copy.start()
        copies.append(copy)
    returned[pl.ds(2 * my_y, 2)] = staged[my_y]
    for copy in copies:
        copy.wait()


def exchange_call(kernel, collective_id, operand, name):
    by_y = pltpu.VMEM((Y_DEVS, 2, FEATS, LANES), F32)
    by_zc = pltpu.VMEM((ZC_DEVS, FEATS, LANES), F32)
    buffers = [by_y, by_zc] if kernel is forward_kernel else [by_zc, by_y]
    return pl.pallas_call(
        kernel,
        out_shape=jax.ShapeDtypeStruct((16, FEATS, LANES), F32),
        in_specs=[pl.BlockSpec(memory_space=pltpu.VMEM)],
        out_specs=pl.BlockSpec(memory_space=pltpu.VMEM),
        scratch_shapes=buffers
        + [
            pltpu.SemaphoreType.DMA((Y_DEVS - 1,)),
            pltpu.SemaphoreType.DMA((Y_DEVS - 1,)),
            pltpu.SemaphoreType.DMA((ZC_DEVS - 1,)),
            pltpu.SemaphoreType.DMA((ZC_DEVS - 1,)),
        ],
        compiler_params=pltpu.CompilerParams(
            collective_id=collective_id, has_side_effects=True, vmem_limit_bytes=16 * 2**20
        ),
        name=name,
    )(operand)


def scatter_operands(values, high, low, left, right, column):
    columns = pl.ds(pl.multiple_of(column, LANES), LANES)
    shape = (16, LANES)
    here = jnp.broadcast_to(high, shape) == lax.broadcasted_iota(jnp.int32, shape, 0)
    for piece, rows in enumerate(split3(values)):
        for f in range(FEATS):
            spread = jnp.where(here, jnp.broadcast_to(rows[f : f + 1], shape), 0.0)
            left[pl.ds((piece * FEATS + f) * 16, 16), columns] = spread.astype(BF16)
    shape = (LANES, LANES)
    hot = jnp.broadcast_to(low, shape) == lax.broadcasted_iota(jnp.int32, shape, 0)
    right[:, columns] = jnp.where(hot, 1.0, 0.0).astype(BF16)


def scatter_product(left, right):
    size = FEATS * 16
    total = dot_nt(left[...], right[...])
    return total[0:size] + total[size : 2 * size] + total[2 * size : 3 * size]


def tile_kernel(
    tile_ids, tile_len, received, lists, targets, pictures, slot_grads,
    table, feats, alpha, before, weight, weight_hi, weight_lo, part_hi, part_lo, upper, grads, left, right, spread,
):
    tiles, entries = lists.shape[1], lists.shape[2]
    chunks = entries // LANES
    pixels = TILE_SIDE * TILE_SIDE
    half = entries // 2
    table[...] = jnp.zeros_like(table)
    for chunk in range(16):
        table[pl.ds(16 * chunk, FEATS), :] = received[chunk]
    row = lax.broadcasted_iota(jnp.int32, (entries, entries), 0)
    col = lax.broadcasted_iota(jnp.int32, (entries, entries), 1)
    upper[...] = jnp.where(row < col, 1.0, 0.0).astype(BF16)
    grads[...] = jnp.zeros_like(grads)

    def slot_of(tile, chunk):
        index = lists[0, pl.ds(tile, 1), pl.ds(chunk * LANES, LANES)]
        return (index >> 4) & 15, ((index >> 8) << 4) | (index & 15)

    for tile in range(tiles):
        for chunk in range(chunks):
            high, low = slot_of(tile, chunk)
            top, bottom = gather_chunk(table, high, low)
            feats[pl.ds(0, 8), pl.ds(chunk * LANES, LANES)] = top
            feats[pl.ds(8, 8), pl.ds(chunk * LANES, LANES)] = bottom
        number = tile_ids[0, tile]
        length = tile_len[0, tile]
        left_x = (TILE_SIDE * lax.rem(number, TILE_COLS)).astype(F32) + 0.5
        top_y = (TILE_SIDE * (number // TILE_COLS)).astype(F32) + 0.5
        shape = (TILE_SIDE, LANES)
        pixel_x = lax.broadcasted_iota(jnp.int32, shape, 0).astype(F32) + left_x

        def feature(f, chunk):
            return jnp.broadcast_to(feats[pl.ds(f, 1), pl.ds(chunk * LANES, LANES)], (8, LANES))

        def twice(rows):
            return jnp.concatenate([rows, rows], axis=0)

        for chunk in range(chunks):
            lanes = pl.ds(chunk * LANES, LANES)
            lane = lax.broadcasted_iota(jnp.int32, (8, LANES), 1) + chunk * LANES
            opacity = twice(jnp.where(lane < length, feature(5, chunk), 0.0))
            delta_x = twice(feature(0, chunk)) - pixel_x
            part_x = twice(-0.5 * feature(2, chunk)) * delta_x * delta_x
            cross = twice(-feature(3, chunk)) * delta_x
            screen_y = feature(1, chunk)
            conic_c = -0.5 * feature(4, chunk)

            def one_row(y, carry):
                rows = pl.ds(pl.multiple_of(y * TILE_SIDE, TILE_SIDE), TILE_SIDE)
                delta_y = screen_y - (top_y + y.astype(F32))
                part_y = conic_c * delta_y * delta_y
                value = opacity * jnp.exp(part_x + cross * twice(delta_y) + twice(part_y))
                alpha[rows, lanes] = value
                part_hi[rows, lanes], part_lo[rows, lanes] = split2(jnp.log(1.0 - value))
                return carry

            lax.fori_loop(0, TILE_SIDE, one_row, 0, unroll=4)

        def prefix(part):
            first = dot_nn(part[:, pl.ds(0, half)], upper[pl.ds(0, half), :])
            second = dot_nn(part[:, pl.ds(half, half)], upper[pl.ds(half, half), pl.ds(half, half)])
            return first[:, :half], first[:, half:] + second

        high_left, high_right = prefix(part_hi)
        low_left, low_right = prefix(part_lo)
        before[:, pl.ds(0, half)] = high_left + low_left
        before[:, pl.ds(half, half)] = high_right + low_right

        def one_weight(y, carry):
            rows = pl.ds(pl.multiple_of(y * TILE_SIDE, TILE_SIDE), TILE_SIDE)
            value = jnp.exp(before[rows, :]) * alpha[rows, :]
            weight[rows, :] = value
            weight_hi[rows, :], weight_lo[rows, :] = split2(value)
            return carry

        lax.fori_loop(0, TILE_SIDE, one_weight, 0, unroll=2)

        colours = jnp.concatenate([feats[pl.ds(6, 3), :], jnp.zeros((5, entries), F32)], axis=0)
        colour_hi = colours.astype(BF16).astype(F32)
        colour_lo = (colours - colour_hi).astype(BF16).astype(F32)
        both = jnp.concatenate([colour_hi, colour_lo], axis=0).astype(BF16)
        product = dot_nt(both, weight_hi[...])
        picture = product[0:8] + product[8:16] + dot_nt(both, weight_lo[...])[0:8]
        pictures[0, tile] = picture[0:3]
        residual = picture - jnp.concatenate([targets[0, tile], jnp.zeros((5, pixels), F32)], axis=0)
        residual_hi = residual.astype(BF16).astype(F32)
        residual_lo = (residual - residual_hi).astype(BF16).astype(F32)

        pair = jnp.concatenate([residual_hi, residual_lo], axis=0).astype(BF16)
        product = dot_nn(pair, weight_hi[...])
        colour_grad = product[0:8] + product[8:16] + dot_nn(pair, weight_lo[...])[0:8]

        stack = jnp.concatenate(
            [residual_hi, residual_lo, residual_hi, jnp.zeros((104, pixels), F32)], axis=0
        )
        columns = jnp.transpose(stack).astype(BF16)
        rows24 = jnp.concatenate(
            [colour_hi, colour_hi, colour_lo, jnp.zeros((104, entries), F32)], axis=0
        ).astype(BF16)
        before[...] = dot_nn(columns, rows24)

        def one_share(y, carry):
            rows = pl.ds(pl.multiple_of(y * TILE_SIDE, TILE_SIDE), TILE_SIDE)
            value = before[rows, :] * weight[rows, :]
            weight[rows, :] = value
            part_hi[rows, :], part_lo[rows, :] = split2(value)
            return carry

        lax.fori_loop(0, TILE_SIDE, one_share, 0, unroll=2)

        def suffix(part):
            first = dot_nt(part[:, pl.ds(0, half)], upper[pl.ds(0, half), pl.ds(0, half)])
            second = dot_nt(part[:, pl.ds(half, half)], upper[:, pl.ds(half, half)])
            return first + second[:, :half], second[:, half:]

        high_left, high_right = suffix(part_hi)
        low_left, low_right = suffix(part_lo)
        before[:, pl.ds(0, half)] = high_left + low_left
        before[:, pl.ds(half, half)] = high_right + low_right

        for chunk in range(chunks):
            lanes = pl.ds(chunk * LANES, LANES)
            screen_y = feature(1, chunk)

            def one_row(y, carry):
                rows = pl.ds(pl.multiple_of(y * TILE_SIDE, TILE_SIDE), TILE_SIDE)
                sum_0, sum_1, sum_2 = carry
                delta_y = twice(screen_y - (top_y + y.astype(F32)))
                value = alpha[rows, lanes]
                grad = weight[rows, lanes] - before[rows, lanes] * (value / (1.0 - value))
                slope = grad * delta_y
                return sum_0 + grad, sum_1 + slope, sum_2 + slope * delta_y

            zero = jnp.zeros(shape, F32)
            sum_0, sum_1, sum_2 = lax.fori_loop(0, TILE_SIDE, one_row, (zero, zero, zero), unroll=4)
            delta_x = twice(feature(0, chunk)) - pixel_x
            over = lambda rows: jnp.sum(rows, axis=0, keepdims=True)
            first_x = over(delta_x * sum_0)
            first_y = over(sum_1)
            row_of = lambda f: feats[pl.ds(f, 1), lanes]
            out = pl.ds(tile * entries + chunk * LANES, LANES)
            grads[pl.ds(0, 1), out] = -row_of(2) * first_x - row_of(3) * first_y
            grads[pl.ds(1, 1), out] = -row_of(4) * first_y - row_of(3) * first_x
            grads[pl.ds(2, 1), out] = -0.5 * over(delta_x * delta_x * sum_0)
            grads[pl.ds(3, 1), out] = -over(delta_x * sum_1)
            grads[pl.ds(4, 1), out] = -0.5 * over(sum_2)
            grads[pl.ds(5, 1), out] = over(sum_0)
        grads[pl.ds(6, 3), pl.ds(tile * entries, entries)] = colour_grad[0:3]

        for chunk in range(chunks):
            high, low = slot_of(tile, chunk)
            column = tile * entries + chunk * LANES
            scatter_operands(grads[:, pl.ds(column, LANES)], high, low, left, right, column)

    total = scatter_product(left, right)
    for f in range(FEATS):
        spread[pl.ds(f, 16, stride=16), :] = total[16 * f : 16 * f + 16]
    for chunk in range(16):
        slot_grads[chunk] = spread[pl.ds(16 * chunk, FEATS), :]


def tile_call(tile_ids, tile_len, received, lists, targets):
    tiles, entries = lists.shape[1], lists.shape[2]
    pixels = TILE_SIDE * TILE_SIDE
    smem = pl.BlockSpec(memory_space=pltpu.SMEM)
    vmem = pl.BlockSpec(memory_space=pltpu.VMEM)
    plane = pltpu.VMEM((pixels, entries), F32)
    thin = pltpu.VMEM((pixels, entries), BF16)
    return pl.pallas_call(
        tile_kernel,
        out_shape=(
            jax.ShapeDtypeStruct(targets.shape, F32),
            jax.ShapeDtypeStruct((16, FEATS, LANES), F32),
        ),
        in_specs=[smem, smem, vmem, vmem, vmem],
        out_specs=(vmem, vmem),
        scratch_shapes=[
            pltpu.VMEM((256, LANES), F32),
            pltpu.VMEM((16, entries), F32),
            plane,
            plane,
            plane,
            thin,
            thin,
            thin,
            thin,
            pltpu.VMEM((entries, entries), BF16),
            pltpu.VMEM((16, tiles * entries), F32),
            pltpu.VMEM((3 * FEATS * 16, tiles * entries), BF16),
            pltpu.VMEM((LANES, tiles * entries), BF16),
            pltpu.VMEM((256, LANES), F32),
        ],
        compiler_params=pltpu.CompilerParams(vmem_limit_bytes=32 * 2**20),
        name="tiles",
    )(tile_ids, tile_len, received, lists, targets)


VIEW_ROWS = FEATS * 16 + 8


def gauss_kernel(camera, returned, slots, out, left, right):
    def one_chunk(chunk, carry):
        column = pl.multiple_of(chunk * LANES, LANES)
        index = slots[0, :, pl.ds(column, LANES)]
        scatter_operands(returned[chunk], index >> 7, index & 127, left, right, column)
        return carry

    lax.fori_loop(0, 16, one_chunk, 0)
    out[pl.ds(0, FEATS * 16), :] = scatter_product(left, right)
    row = lax.broadcasted_iota(jnp.int32, (8, LANES), 0)
    shift = jnp.where(row == 0, camera[0, 0], jnp.where(row == 1, camera[0, 1], camera[0, 2]))
    out[pl.ds(FEATS * 16, 8), :] = shift


def gauss_call(camera, returned, slots):
    vmem = pl.BlockSpec(memory_space=pltpu.VMEM)
    return pl.pallas_call(
        gauss_kernel,
        out_shape=jax.ShapeDtypeStruct((VIEW_ROWS, LANES), F32),
        in_specs=[pl.BlockSpec(memory_space=pltpu.SMEM), vmem, vmem],
        out_specs=vmem,
        scratch_shapes=[
            pltpu.VMEM((3 * FEATS * 16, 2048), BF16),
            pltpu.VMEM((LANES, 2048), BF16),
        ],
        compiler_params=pltpu.CompilerParams(vmem_limit_bytes=24 * 2**20),
        name="gauss",
    )(camera, returned, slots)


def views_kernel(mine, every, send_sem, recv_sem):
    view = lax.axis_index("view")
    barrier = pltpu.get_barrier_semaphore()
    for k in range(1, VIEW_DEVS):
        pl.semaphore_signal(
            barrier,
            inc=1,
            device_id={"view": lax.rem(view + k, VIEW_DEVS)},
            device_id_type=pl.DeviceIdType.MESH,
        )
    pl.semaphore_wait(barrier, VIEW_DEVS - 1)
    copies = []
    for k in range(1, VIEW_DEVS):
        copy = pltpu.make_async_remote_copy(
            src_ref=mine,
            dst_ref=every.at[view],
            send_sem=send_sem.at[k - 1],
            recv_sem=recv_sem.at[k - 1],
            device_id={"view": lax.rem(view + k, VIEW_DEVS)},
            device_id_type=pl.DeviceIdType.MESH,
        )
        copy.start()
        copies.append(copy)
    every[view] = mine[...]
    for copy in copies:
        copy.wait()


def views_call(mine):
    vmem = pl.BlockSpec(memory_space=pltpu.VMEM)
    return pl.pallas_call(
        views_kernel,
        out_shape=jax.ShapeDtypeStruct((VIEW_DEVS, VIEW_ROWS, LANES), F32),
        in_specs=[vmem],
        out_specs=vmem,
        scratch_shapes=[
            pltpu.SemaphoreType.DMA((VIEW_DEVS - 1,)),
            pltpu.SemaphoreType.DMA((VIEW_DEVS - 1,)),
        ],
        compiler_params=pltpu.CompilerParams(
            collective_id=2, has_side_effects=True, vmem_limit_bytes=16 * 2**20
        ),
        name="views",
    )(mine)


def param_kernel(dense, every, gradient, packed):
    rows = gradient.shape[0]

    def one_half(half, carry):
        part = pl.ds(pl.multiple_of(half * 8, 8), 8)
        load = lambda row: dense[row, part, :]

        def store(row, value):
            packed[pl.ds((row // 8) * 128 + row % 8 + half * 64, 8, stride=8), :] = value

        def add(row, value, view):
            if view:
                where = pl.ds((row // 8) * 128 + row % 8 + half * 64, 8, stride=8)
                packed[where, :] = packed[where, :] + value
            else:
                store(row, value)

        quaternion = [load(6 + i) for i in range(4)]
        matrix, scales, unit_q, inv_norm = shape_matrix([load(3 + i) for i in range(3)], quaternion)
        grad_matrix = [0.0] * 9
        grad_pos = [0.0] * 3
        grad_log = 0.0
        for view in range(VIEW_DEVS):
            slot = lambda f: every[view, pl.ds(pl.multiple_of(f * 16 + half * 8, 8), 8), :]
            shift = lambda i: jnp.broadcast_to(every[view, pl.ds(FEATS * 16 + i, 1), :], (8, LANES))
            pos = [load(i) - shift(i) for i in range(3)]
            inv_z, jac, screen_x, screen_y, jac_x, jac_y, row_u, row_v, cov_a, cov_b, cov_c, inv_det = geometry(
                pos, matrix
            )
            g_a, g_b, g_c = slot(2), slot(3), slot(4)
            g_det = -(g_a * cov_c - g_b * cov_b + g_c * cov_a) * inv_det * inv_det
            d_a = g_c * inv_det + g_det * cov_c
            d_c = g_a * inv_det + g_det * cov_a
            d_b = -g_b * inv_det - 2.0 * g_det * cov_b
            d_a, d_c = 2.0 * d_a, 2.0 * d_c
            g_u = [d_a * row_u[j] + d_b * row_v[j] for j in range(3)]
            g_v = [d_c * row_v[j] + d_b * row_u[j] for j in range(3)]
            for j in range(3):
                grad_matrix[j] = grad_matrix[j] + jac * g_u[j]
                grad_matrix[3 + j] = grad_matrix[3 + j] + jac * g_v[j]
                grad_matrix[6 + j] = grad_matrix[6 + j] + jac_x * g_u[j] + jac_y * g_v[j]
            g_jac = sum(g_u[j] * matrix[j] + g_v[j] * matrix[3 + j] for j in range(3))
            g_jac_x = sum(g_u[j] * matrix[6 + j] for j in range(3))
            g_jac_y = sum(g_v[j] * matrix[6 + j] for j in range(3))
            g_sx = slot(0) - inv_z * g_jac_x
            g_sy = slot(1) - inv_z * g_jac_y
            g_inv = (
                focal_length * (g_jac + pos[0] * g_sx + pos[1] * g_sy) - screen_x * g_jac_x - screen_y * g_jac_y
            )
            g_pos = [jac * g_sx, jac * g_sy, -inv_z * inv_z * g_inv]

            unit, inv_len = direction(pos)
            basis, pull = jax.vjp(harmonics, *unit)
            g_basis = [0.0] * 15
            for channel in range(3):
                colour = raw_colour(load, channel, basis)
                g_colour = slot(6 + channel)
                g_colour = jnp.where(colour > 0.0, g_colour, jnp.where(colour < 0.0, 0.0, 0.5 * g_colour))
                add(11 + 16 * channel, sh_first * g_colour, view)
                for j in range(15):
                    add(12 + 16 * channel + j, basis[j] * g_colour, view)
                    g_basis[j] = g_basis[j] + load(12 + 16 * channel + j) * g_colour
            g_unit = pull(g_basis)
            along = unit[0] * g_unit[0] + unit[1] * g_unit[1] + unit[2] * g_unit[2]
            for i in range(3):
                grad_pos[i] = grad_pos[i] + g_pos[i] + inv_len * (g_unit[i] - unit[i] * along)
            grad_log = grad_log + slot(5)

        for i in range(3):
            store(i, grad_pos[i])
            store(3 + i, sum(grad_matrix[3 * k + i] * matrix[3 * k + i] for k in range(3)))
        rotation, pull = jax.vjp(rotation_of, *unit_q)
        g_unit = pull([grad_matrix[3 * i + j] * scales[j] for i in range(3) for j in range(3)])
        along = sum(unit_q[i] * g_unit[i] for i in range(4))
        for i in range(4):
            store(6 + i, inv_norm * (g_unit[i] - unit_q[i] * along))
        store(10, grad_log * (1.0 / (1.0 + jnp.exp(load(10)))))
        return carry

    lax.fori_loop(0, 2, one_half, 0)
    for group in range(0, rows, 8):
        size = min(8, rows - group)
        for chunk in range(16):
            gradient[pl.ds(group, size), pl.ds(chunk * LANES, LANES)] = packed[
                pl.ds(group * 16 + chunk * 8, size), :
            ]


def param_call(dense, every):
    vmem = pl.BlockSpec(memory_space=pltpu.VMEM)
    return pl.pallas_call(
        param_kernel,
        out_shape=jax.ShapeDtypeStruct((dense.shape[0], 2048), F32),
        in_specs=[vmem, vmem],
        out_specs=vmem,
        scratch_shapes=[pltpu.VMEM((64 * 16, LANES), F32)],
        compiler_params=pltpu.CompilerParams(vmem_limit_bytes=24 * 2**20),
        name="params",
    )(dense, every)


def local(params, cameras, targets, tile_ids, send_slots, tile_lists, tile_len):
    dense, outgoing = project_call(cameras, params, send_slots)
    received = exchange_call(forward_kernel, 0, outgoing, "forward")
    pictures, slot_grads = tile_call(tile_ids, tile_len, received, tile_lists, targets)
    returned = exchange_call(backward_kernel, 1, slot_grads, "backward")
    mine = gauss_call(cameras, returned, send_slots)
    every = views_call(mine)
    return pictures, param_call(dense, every)


def solution(mesh):
    return jax.shard_map(
        local,
        mesh=mesh,
        in_specs=(
            P(None, "cell"),
            P("view", None),
            P("view", "cell", None, None),
            P("view", "cell"),
            P("view", "cell", None),
            P("view", "cell", None),
            P("view", "cell"),
        ),
        out_specs=(P("view", "cell", None, None), P(None, "cell")),
        check_vma=False,
    )
```

time: 275 us -> 63.2 us (0.23); the launches traced: 270 us -> 62.7 us
  other arithmetic: 74 us -> 0 us
  local copies, waits for them, and re-layouts: 74.7 us -> 2.37 us
  Pallas kernels: 0 us -> 59.6 us
  waiting for transfers between devices: 55.9 us -> 0 us
  starting transfers between devices: 18.8 us -> 0 us
  blocking collectives: 17.6 us -> 0 us
  between operations: 14.9 us -> 0.75 us
  matrix products: 8.49 us -> 0 us
  loops' own time: 6 us -> 0 us
    pallas_call x0 -> x7, Pallas kernels: none -> 59.6 us  [the longest x2 39.1 us: exchange_call(): pl.pallas_call(kernel, out_shape=jax.ShapeDtypeStruct((16, FEATS, LANES),...]
    psum x1 -> x0, waiting for transfers between devices: 44.6 us -> none  [sum_views(): return lax.psum(local_grad, 'view')]
    unnamed x158 -> x14, local copies, waits for them, and re-layouts: 23.1 us -> 2.37 us
    scatter-add x2 -> x0, other arithmetic: 19.4 us -> none  [the longest x1 12 us: local(): jnp.zeros((returned.shape[0], params.shape[1]), jnp.float32)]
    add_any x11 -> x0, other arithmetic: 19.3 us -> none  [the longest x1 3.3 us: project(): inv_depth = 1.0 / depth_cam]
    all_to_all x1 -> x0, starting transfers between devices: 18.6 us -> none  [local(): lax.all_to_all(outgoing, 'cell', split_axis=1, concat_axis=1, tiled=True)]
    all_to_all x1 -> x0, blocking collectives: 17.6 us -> none  [local(): lax.all_to_all(slot_grads, 'cell', split_axis=1, concat_axis=1, tiled=True)]
    mul x18 -> x0, other arithmetic: 14.3 us -> none  [the longest x2 3.77 us: project(): colors = jnp.maximum(jnp.sum(coeffs * sh_basis[None], axis=1) + 0.5, 0.0)]
  transfers between devices with their start and end apart: 2 -> 0, of which waited for: 2 -> 0; matrix products, arithmetic and copies ran while one was open for 0% -> 0% of each run, Pallas kernels for 0% -> 0%
where the time goes in v1:
time: 63.2 us; the launch traced here: 62.7 us
  Pallas kernels  59.6 us (94%)
  local copies, waits for them, and re-layouts  2.37 us (4%)
  between operations  0.75 us (1%)
    pallas_call x2, Pallas kernels, exchange_call(): pl.pallas_call(kernel, out_shape=jax.ShapeDtypeStruct((16, FEATS, LANES),...  39.1 us
    pallas_call x1, Pallas kernels, views_call(): pl.pallas_call(views_kernel, out_shape=jax.ShapeDtypeStruct((VIEW_DEVS, V...  7.58 us
    pallas_call x1, Pallas kernels, tile_call(): pl.pallas_call(tile_kernel, out_shape=(jax.ShapeDtypeStruct(targets.shape...  7.18 us
    unnamed x14, local copies, waits for them, and re-layouts  2.37 us
    pallas_call x1, Pallas kernels, param_call(): pl.pallas_call(param_kernel, out_shape=jax.ShapeDtypeStruct((dense.shape[...  1.97 us
    pallas_call x1, Pallas kernels, project_call(): pl.pallas_call(project_kernel, out_shape=(jax.ShapeDtypeStruct((rows, 16,...  1.9 us
    pallas_call x1, Pallas kernels, gauss_call(): pl.pallas_call(gauss_kernel, out_shape=jax.ShapeDtypeStruct((VIEW_ROWS, L...  1.9 us

profile of v1, /device:TPU:1, one launch (start us, length us, event | category | flops | bytes accessed | tf_op | source)
XLA Modules:
  0.0 62.7 jit_solution(12310998680700926545)
XLA Ops:
  0.6 0.0 copy-start.1
  0.6 0.0 copy-start.3
  0.7 0.7 %copy.9.targets = f32[1,2,3,256]{3,2,1,0:T(4,128)S(1)} copy(f32[1,2,3,256]{3,1,2,0:T(2,128)} %param.9) | data formatting | bytes 12288 | tf_op args[2]
  1.4 0.0 copy-done.1
  1.4 0.0 copy-done.3
  1.4 0.0 copy-start
  1.4 1.0 %copy-done = f32[59,2048]{1,0:T(8,128)S(1)} copy-done((f32[59,2048]{1,0:T(8,128)S(1)}, f32[59,2048]{1,0:T(8,128)}, u32[]{:S(2)}) %copy-start) | copy-done | bytes 483352
  2.4 1.9 %project.1 = (f32[59,16,128]{2,1,0:T(8,128)S(1)}, f32[16,9,128]{2,1,0:T(8,128)S(1)}) custom-call(f32[1,3]{1,0:T(1,128)S(1)} %copy-done.3, f32[59,2048]{1,0:T(8,128)S(1)} %copy-done, s32[1,1,2048]{2,1,0:T(1,128)S(1)} %copy-done.1), custom_call_target="tpu_custom_call" | custom-call | tf_op jit(solution)/shard_map/project/pallas_call | solution.py:201
  4.3 0.0 copy-start.2
  4.3 0.0 copy-start.4
  4.3 0.0 copy-start.5
  4.4 25.6 %forward.1.received = f32[16,9,128]{2,1,0:T(8,128)S(1)} custom-call(f32[16,9,128]{2,1,0:T(8,128)S(1)} %get-tuple-element.6.outgoing), custom_call_target="tpu_custom_call" | custom-call | tf_op jit(solution)/shard_map/forward/pallas_call | solution.py:343
  29.9 0.0 copy-done.2
  29.9 0.0 copy-done.4
  29.9 0.0 copy-done.5
  29.9 7.2 %tiles.1 = (f32[1,2,3,256]{3,2,1,0:T(4,128)S(1)}, f32[16,9,128]{2,1,0:T(8,128)S(1)}) custom-call(s32[1,2]{1,0:T(1,128)S(1)} %copy-done.4, s32[1,2]{1,0:T(1,128)S(1)} %copy-done.5, f32[16,9,128]{2,1,0:T(8,128)S(1)} %forward.1.received, s32[1,2,512]{2,1,0:T(2,128)S(1)} %copy-done.2, f32[1,2,3,256]{3,2,1,0:T(4,128)S(1)} %copy.9.targets), custom_call_target="tpu_custom_call" | custom-call | tf_op jit(solution)/shard_map/tiles/pallas_call | solution.py:551
  37.1 0.6 copy.10
  37.7 13.5 %backward.1.returned = f32[16,9,128]{2,1,0:T(8,128)S(1)} custom-call(f32[16,9,128]{2,1,0:T(8,128)S(1)} %get-tuple-element.9.slot_grads), custom_call_target="tpu_custom_call" | custom-call | tf_op jit(solution)/shard_map/backward/pallas_call | solution.py:343
  51.3 1.9 %gauss.1.mine = f32[152,128]{1,0:T(8,128)S(1)} custom-call(f32[1,3]{1,0:T(1,128)S(1)} %copy-done.3, f32[16,9,128]{2,1,0:T(8,128)S(1)} %backward.1.returned, s32[1,1,2048]{2,1,0:T(1,128)S(1)} %copy-done.1), custom_call_target="tpu_custom_call" | custom-call | tf_op jit(solution)/shard_map/gauss/pallas_call | solution.py:599
  53.2 7.6 %views.1.every = f32[4,152,128]{2,1,0:T(8,128)S(1)} custom-call(f32[152,128]{1,0:T(8,128)S(1)} %gauss.1.mine), custom_call_target="tpu_custom_call" | custom-call | tf_op jit(solution)/shard_map/views/pallas_call | solution.py:643
  60.8 2.0 %params.3 = f32[59,2048]{1,0:T(8,128)} custom-call(f32[59,16,128]{2,1,0:T(8,128)S(1)} %get-tuple-element.8.dense, f32[4,152,128]{2,1,0:T(8,128)S(1)} %views.1.every), custom_call_target="tpu_custom_call" | custom-call | tf_op jit(solution)/shard_map/params/pallas_call | solution.py:749
Async XLA Ops:
  0.6 0.7 %copy-start.1 = (s32[1,1,2048]{2,1,0:T(1,128)S(1)}, s32[1,1,2048]{2,1,0:T(1,128)}, u32[]{:S(2)}) copy-start(s32[1,1,2048]{2,1,0:T(1,128)} %slots.3) | copy-start | bytes 24580
  0.6 0.7 %copy-start.3 = (f32[1,3]{1,0:T(1,128)S(1)}, f32[1,3]{1,0:T(1,128)}, u32[]{:S(2)}) copy-start(f32[1,3]{1,0:T(1,128)} %camera.3) | copy-start | bytes 40
  1.4 1.0 %copy-start = (f32[59,2048]{1,0:T(8,128)S(1)}, f32[59,2048]{1,0:T(8,128)}, u32[]{:S(2)}) copy-start(f32[59,2048]{1,0:T(8,128)} %params.2) | copy-start | bytes 1449988
  4.3 25.6 %copy-start.2 = (s32[1,2,512]{2,1,0:T(2,128)S(1)}, s32[1,2,512]{2,1,0:T(2,128)}, u32[]{:S(2)}) copy-start(s32[1,2,512]{2,1,0:T(2,128)} %lists.1) | copy-start | bytes 12292
  4.3 25.6 %copy-start.4 = (s32[1,2]{1,0:T(1,128)S(1)}, s32[1,2]{1,0:T(1,128)}, u32[]{:S(2)}) copy-start(s32[1,2]{1,0:T(1,128)} %tile_ids.1) | copy-start | bytes 28
  4.3 25.6 %copy-start.5 = (s32[1,2]{1,0:T(1,128)S(1)}, s32[1,2]{1,0:T(1,128)}, u32[]{:S(2)}) copy-start(s32[1,2]{1,0:T(1,128)} %tile_len.1) | copy-start | bytes 28

commit v2 on v1

--- a/solution.py
+++ b/solution.py
@@ -14,6 +14,9 @@
 ZC_DEVS = 16
 VIEW_DEVS = 4
 FEATS = 9
+Y_ORDER = (4, 3, 5, 2, 6, 1, 7)
+ZC_ORDER = (8, 9, 7, 6, 10, 5, 11, 4, 12, 3, 13, 2, 14, 1, 15)
+VIEW_ORDER = (2, 1, 3)
 F32 = jnp.float32
 BF16 = jnp.bfloat16
 
@@ -156,7 +159,7 @@
     return top, bottom
 
 
-def project_kernel(camera, params, slots, dense, outgoing, packed, table):
+def project_body(camera, params, slots, dense, outgoing, packed, table):
     rows = params.shape[0]
     for group in range(0, rows, 8):
         size = min(8, rows - group)
@@ -196,26 +199,6 @@
     lax.fori_loop(0, 16, one_chunk, 0, unroll=2)
 
 
-def project_call(camera, params, slots):
-    rows = params.shape[0]
-    return pl.pallas_call(
-        project_kernel,
-        out_shape=(
-            jax.ShapeDtypeStruct((rows, 16, LANES), F32),
-            jax.ShapeDtypeStruct((16, FEATS, LANES), F32),
-        ),
-        in_specs=[
-            pl.BlockSpec(memory_space=pltpu.SMEM),
-            pl.BlockSpec(memory_space=pltpu.VMEM),
-            pl.BlockSpec(memory_space=pltpu.VMEM),
-        ],
-        out_specs=(pl.BlockSpec(memory_space=pltpu.VMEM),) * 2,
-        scratch_shapes=[pltpu.VMEM((64 * 16, LANES), F32), pltpu.VMEM((256, LANES), F32)],
-        compiler_params=pltpu.CompilerParams(vmem_limit_bytes=24 * 2**20),
-        name="project",
-    )(camera, params, slots)
-
-
 def block_transpose(rows):
     group = lax.broadcasted_iota(jnp.int32, rows[0].shape, 1) // 16
     for step in (1, 2, 4):
@@ -231,132 +214,80 @@
     return rows
 
 
-def greet(my_y, my_zc):
+def remote(src_ref, dst_ref, send_sem, recv_sem, k, device_id):
+    copy = pltpu.make_async_remote_copy(
+        src_ref=src_ref,
+        dst_ref=dst_ref,
+        send_sem=send_sem.at[k - 1],
+        recv_sem=recv_sem.at[k - 1],
+        device_id=device_id,
+        device_id_type=pl.DeviceIdType.MESH,
+    )
+    copy.start()
+    return copy
+
+
+def y_peer(my_y, my_zc, k):
+    peer = lax.rem(my_y + k, Y_DEVS)
+    return peer, {"cell": peer * ZC_DEVS + my_zc}
+
+
+def zc_peer(my_y, my_zc, k):
+    peer = lax.rem(my_zc + k, ZC_DEVS)
+    return peer, {"cell": my_y * ZC_DEVS + peer}
+
+
+def view_peer(view, k):
+    return {"view": lax.rem(view + k, VIEW_DEVS)}
+
+
+def greet(my_y, my_zc, view):
     barrier = pltpu.get_barrier_semaphore()
-    for k in range(1, Y_DEVS):
-        pl.semaphore_signal(
-            barrier,
-            inc=1,
-            device_id={"cell": lax.rem(my_y + k, Y_DEVS) * ZC_DEVS + my_zc},
-            device_id_type=pl.DeviceIdType.MESH,
+    peers = [y_peer(my_y, my_zc, k)[1] for k in Y_ORDER]
+    peers += [zc_peer(my_y, my_zc, k)[1] for k in ZC_ORDER]
+    peers += [view_peer(view, k) for k in VIEW_ORDER]
+    for peer in peers:
+        pl.semaphore_signal(barrier, inc=1, device_id=peer, device_id_type=pl.DeviceIdType.MESH)
+    return barrier, len(peers)
+
+
+def over_y(source, target, my_y, my_zc, sems):
+    copies = []
+    for k in Y_ORDER:
+        peer, device_id = y_peer(my_y, my_zc, k)
+        copies.append(
+            remote(source.at[pl.ds(2 * peer, 2)], target.at[pl.ds(2 * my_y, 2)], *sems, k, device_id)
         )
-    for k in range(1, ZC_DEVS):
-        pl.semaphore_signal(
-            barrier,
-            inc=1,
-            device_id={"cell": my_y * ZC_DEVS + lax.rem(my_zc + k, ZC_DEVS)},
-            device_id_type=pl.DeviceIdType.MESH,
-        )
-    return barrier
-
-
-def forward_kernel(outgoing, received, landed, staged, send_y, recv_y, send_zc, recv_zc):
-    cell = lax.axis_index("cell")
-    my_y, my_zc = cell // ZC_DEVS, lax.rem(cell, ZC_DEVS)
-    barrier = greet(my_y, my_zc)
-    pl.semaphore_wait(barrier, Y_DEVS + ZC_DEVS - 2)
+    target[pl.ds(2 * my_y, 2)] = source[pl.ds(2 * my_y, 2)]
+    return copies
+
+
+def over_zc(source, target, my_y, my_zc, sems):
     copies = []
-    for k in range(1, Y_DEVS):
-        peer = lax.rem(my_y + k, Y_DEVS)
-        copy = pltpu.make_async_remote_copy(
-            src_ref=outgoing.at[pl.ds(2 * peer, 2)],
-            dst_ref=landed.at[my_y],
-            send_sem=send_y.at[k - 1],
-            recv_sem=recv_y.at[k - 1],
-            device_id={"cell": peer * ZC_DEVS + my_zc},
-            device_id_type=pl.DeviceIdType.MESH,
-        )
-        copy.start()
-        copies.append(copy)
-    landed[my_y] = outgoing[pl.ds(2 * my_y, 2)]
+    for k in ZC_ORDER:
+        peer, device_id = zc_peer(my_y, my_zc, k)
+        copies.append(remote(source.at[peer], target.at[my_zc], *sems, k, device_id))
+    target[my_zc] = source[my_zc]
+    return copies
+
+
+def wait_all(copies):
     for copy in copies:
         copy.wait()
+
+
+def regroup_by_zc(source, target):
     for half in range(2):
-        rows = block_transpose([landed[y, half] for y in range(Y_DEVS)])
+        rows = block_transpose([source[2 * y + half] for y in range(Y_DEVS)])
         for i in range(8):
-            staged[8 * half + i] = rows[i]
-    copies = []
-    for k in range(1, ZC_DEVS):
-        peer = lax.rem(my_zc + k, ZC_DEVS)
-        copy = pltpu.make_async_remote_copy(
-            src_ref=staged.at[peer],
-            dst_ref=received.at[my_zc],
-            send_sem=send_zc.at[k - 1],
-            recv_sem=recv_zc.at[k - 1],
-            device_id={"cell": my_y * ZC_DEVS + peer},
-            device_id_type=pl.DeviceIdType.MESH,
-        )
-        copy.start()
-        copies.append(copy)
-    received[my_zc] = staged[my_zc]
-    for copy in copies:
-        copy.wait()
-
-
-def backward_kernel(slot_grads, returned, landed, staged, send_y, recv_y, send_zc, recv_zc):
-    cell = lax.axis_index("cell")
-    my_y, my_zc = cell // ZC_DEVS, lax.rem(cell, ZC_DEVS)
-    barrier = greet(my_y, my_zc)
-    pl.semaphore_wait(barrier, Y_DEVS + ZC_DEVS - 2)
-    copies = []
-    for k in range(1, ZC_DEVS):
-        peer = lax.rem(my_zc + k, ZC_DEVS)
-        copy = pltpu.make_async_remote_copy(
-            src_ref=slot_grads.at[peer],
-            dst_ref=landed.at[my_zc],
-            send_sem=send_zc.at[k - 1],
-            recv_sem=recv_zc.at[k - 1],
-            device_id={"cell": my_y * ZC_DEVS + peer},
-            device_id_type=pl.DeviceIdType.MESH,
-        )
-        copy.start()
-        copies.append(copy)
-    landed[my_zc] = slot_grads[my_zc]
-    for copy in copies:
-        copy.wait()
+            target[8 * half + i] = rows[i]
+
+
+def regroup_by_y(source, target):
     for half in range(2):
-        rows = block_transpose([landed[8 * half + i] for i in range(8)])
+        rows = block_transpose([source[8 * half + i] for i in range(8)])
         for y in range(Y_DEVS):
-            staged[y, half] = rows[y]
-    copies = []
-    for k in range(1, Y_DEVS):
-        peer = lax.rem(my_y + k, Y_DEVS)
-        copy = pltpu.make_async_remote_copy(
-            src_ref=staged.at[peer],
-            dst_ref=returned.at[pl.ds(2 * my_y, 2)],
-            send_sem=send_y.at[k - 1],
-            recv_sem=recv_y.at[k - 1],
-            device_id={"cell": peer * ZC_DEVS + my_zc},
-            device_id_type=pl.DeviceIdType.MESH,
-        )
-        copy.start()
-        copies.append(copy)
-    returned[pl.ds(2 * my_y, 2)] = staged[my_y]
-    for copy in copies:
-        copy.wait()
-
-
-def exchange_call(kernel, collective_id, operand, name):
-    by_y = pltpu.VMEM((Y_DEVS, 2, FEATS, LANES), F32)
-    by_zc = pltpu.VMEM((ZC_DEVS, FEATS, LANES), F32)
-    buffers = [by_y, by_zc] if kernel is forward_kernel else [by_zc, by_y]
-    return pl.pallas_call(
-        kernel,
-        out_shape=jax.ShapeDtypeStruct((16, FEATS, LANES), F32),
-        in_specs=[pl.BlockSpec(memory_space=pltpu.VMEM)],
-        out_specs=pl.BlockSpec(memory_space=pltpu.VMEM),
-        scratch_shapes=buffers
-        + [
-            pltpu.SemaphoreType.DMA((Y_DEVS - 1,)),
-            pltpu.SemaphoreType.DMA((Y_DEVS - 1,)),
-            pltpu.SemaphoreType.DMA((ZC_DEVS - 1,)),
-            pltpu.SemaphoreType.DMA((ZC_DEVS - 1,)),
-        ],
-        compiler_params=pltpu.CompilerParams(
-            collective_id=collective_id, has_side_effects=True, vmem_limit_bytes=16 * 2**20
-        ),
-        name=name,
-    )(operand)
+            target[2 * y + half] = rows[y]
 
 
 def scatter_operands(values, high, low, left, right, column):
@@ -378,7 +309,7 @@
     return total[0:size] + total[size : 2 * size] + total[2 * size : 3 * size]
 
 
-def tile_kernel(
+def tile_body(
     tile_ids, tile_len, received, lists, targets, pictures, slot_grads,
     table, feats, alpha, before, weight, weight_hi, weight_lo, part_hi, part_lo, upper, grads, left, right, spread,
 ):
@@ -463,8 +394,8 @@
         both = jnp.concatenate([colour_hi, colour_lo], axis=0).astype(BF16)
         product = dot_nt(both, weight_hi[...])
         picture = product[0:8] + product[8:16] + dot_nt(both, weight_lo[...])[0:8]
-        pictures[0, tile] = picture[0:3]
-        residual = picture - jnp.concatenate([targets[0, tile], jnp.zeros((5, pixels), F32)], axis=0)
+        pictures[0, :, tile, :] = picture[0:3]
+        residual = picture - jnp.concatenate([targets[0, :, tile, :], jnp.zeros((5, pixels), F32)], axis=0)
         residual_hi = residual.astype(BF16).astype(F32)
         residual_lo = (residual - residual_hi).astype(BF16).astype(F32)
 
@@ -541,23 +472,81 @@
         slot_grads[chunk] = spread[pl.ds(16 * chunk, FEATS), :]
 
 
-def tile_call(tile_ids, tile_len, received, lists, targets):
+VIEW_ROWS = FEATS * 16 + 8
+
+
+def gauss_body(camera, returned, slots, out, left, right):
+    def one_chunk(chunk, carry):
+        column = pl.multiple_of(chunk * LANES, LANES)
+        index = slots[0, :, pl.ds(column, LANES)]
+        scatter_operands(returned[chunk], index >> 7, index & 127, left, right, column)
+        return carry
+
+    lax.fori_loop(0, 16, one_chunk, 0)
+    out[pl.ds(0, FEATS * 16), :] = scatter_product(left, right)
+    row = lax.broadcasted_iota(jnp.int32, (8, LANES), 0)
+    shift = jnp.where(row == 0, camera[0, 0], jnp.where(row == 1, camera[0, 1], camera[0, 2]))
+    out[pl.ds(FEATS * 16, 8), :] = shift
+
+
+def render_kernel(
+    camera, tile_ids, tile_len, params, slots, lists, targets,
+    pictures, dense, every,
+    packed, table, outgoing, landed, staged, received, slot_grads, landed_back, staged_back, returned, mine,
+    feats, alpha, before, weight, weight_hi, weight_lo, part_hi, part_lo, upper, grads, tile_left, tile_right, spread,
+    left, right, *sems,
+):
+    cell, view = lax.axis_index("cell"), lax.axis_index("view")
+    my_y, my_zc = cell // ZC_DEVS, lax.rem(cell, ZC_DEVS)
+    barrier, greetings = greet(my_y, my_zc, view)
+    project_body(camera, params, slots, dense, outgoing, packed, table)
+    pl.semaphore_wait(barrier, greetings)
+
+    wait_all(over_y(outgoing, landed, my_y, my_zc, sems[0:2]))
+    regroup_by_zc(landed, staged)
+    wait_all(over_zc(staged, received, my_y, my_zc, sems[2:4]))
+    tile_body(
+        tile_ids, tile_len, received, lists, targets, pictures, slot_grads,
+        table, feats, alpha, before, weight, weight_hi, weight_lo, part_hi, part_lo, upper, grads,
+        tile_left, tile_right, spread,
+    )
+    wait_all(over_zc(slot_grads, landed_back, my_y, my_zc, sems[4:6]))
+    regroup_by_y(landed_back, staged_back)
+    wait_all(over_y(staged_back, returned, my_y, my_zc, sems[6:8]))
+    gauss_body(camera, returned, slots, mine, left, right)
+    copies = [remote(mine, every.at[view], sems[8], sems[9], k, view_peer(view, k)) for k in VIEW_ORDER]
+    every[view] = mine[...]
+    wait_all(copies)
+
+
+def render_call(camera, tile_ids, tile_len, params, slots, lists, targets):
+    rows = params.shape[0]
     tiles, entries = lists.shape[1], lists.shape[2]
     pixels = TILE_SIDE * TILE_SIDE
     smem = pl.BlockSpec(memory_space=pltpu.SMEM)
     vmem = pl.BlockSpec(memory_space=pltpu.VMEM)
     plane = pltpu.VMEM((pixels, entries), F32)
     thin = pltpu.VMEM((pixels, entries), BF16)
+    blocks = pltpu.VMEM((16, FEATS, LANES), F32)
+    pair = [pltpu.SemaphoreType.DMA((Y_DEVS - 1,))] * 2
+    many = [pltpu.SemaphoreType.DMA((ZC_DEVS - 1,))] * 2
+    few = [pltpu.SemaphoreType.DMA((VIEW_DEVS - 1,))] * 2
     return pl.pallas_call(
-        tile_kernel,
+        render_kernel,
         out_shape=(
             jax.ShapeDtypeStruct(targets.shape, F32),
-            jax.ShapeDtypeStruct((16, FEATS, LANES), F32),
+            jax.ShapeDtypeStruct((rows, 16, LANES), F32),
+            jax.ShapeDtypeStruct((VIEW_DEVS, VIEW_ROWS, LANES), F32),
         ),
-        in_specs=[smem, smem, vmem, vmem, vmem],
-        out_specs=(vmem, vmem),
+        in_specs=[smem, smem, smem, vmem, vmem, vmem, vmem],
+        out_specs=(vmem, vmem, vmem),
         scratch_shapes=[
+            pltpu.VMEM((64 * 16, LANES), F32),
             pltpu.VMEM((256, LANES), F32),
+        ]
+        + [blocks] * 8
+        + [
+            pltpu.VMEM((VIEW_ROWS, LANES), F32),
             pltpu.VMEM((16, entries), F32),
             plane,
             plane,
@@ -571,92 +560,19 @@
             pltpu.VMEM((3 * FEATS * 16, tiles * entries), BF16),
             pltpu.VMEM((LANES, tiles * entries), BF16),
             pltpu.VMEM((256, LANES), F32),
-        ],
-        compiler_params=pltpu.CompilerParams(vmem_limit_bytes=32 * 2**20),
-        name="tiles",
-    )(tile_ids, tile_len, received, lists, targets)
-
-
-VIEW_ROWS = FEATS * 16 + 8
-
-
-def gauss_kernel(camera, returned, slots, out, left, right):
-    def one_chunk(chunk, carry):
-        column = pl.multiple_of(chunk * LANES, LANES)
-        index = slots[0, :, pl.ds(column, LANES)]
-        scatter_operands(returned[chunk], index >> 7, index & 127, left, right, column)
-        return carry
-
-    lax.fori_loop(0, 16, one_chunk, 0)
-    out[pl.ds(0, FEATS * 16), :] = scatter_product(left, right)
-    row = lax.broadcasted_iota(jnp.int32, (8, LANES), 0)
-    shift = jnp.where(row == 0, camera[0, 0], jnp.where(row == 1, camera[0, 1], camera[0, 2]))
-    out[pl.ds(FEATS * 16, 8), :] = shift
-
-
-def gauss_call(camera, returned, slots):
-    vmem = pl.BlockSpec(memory_space=pltpu.VMEM)
-    return pl.pallas_call(
-        gauss_kernel,
-        out_shape=jax.ShapeDtypeStruct((VIEW_ROWS, LANES), F32),
-        in_specs=[pl.BlockSpec(memory_space=pltpu.SMEM), vmem, vmem],
-        out_specs=vmem,
-        scratch_shapes=[
             pltpu.VMEM((3 * FEATS * 16, 2048), BF16),
             pltpu.VMEM((LANES, 2048), BF16),
-        ],
-        compiler_params=pltpu.CompilerParams(vmem_limit_bytes=24 * 2**20),
-        name="gauss",
-    )(camera, returned, slots)
-
-
-def views_kernel(mine, every, send_sem, recv_sem):
-    view = lax.axis_index("view")
-    barrier = pltpu.get_barrier_semaphore()
-    for k in range(1, VIEW_DEVS):
-        pl.semaphore_signal(
-            barrier,
-            inc=1,
-            device_id={"view": lax.rem(view + k, VIEW_DEVS)},
-            device_id_type=pl.DeviceIdType.MESH,
-        )
-    pl.semaphore_wait(barrier, VIEW_DEVS - 1)
-    copies = []
-    for k in range(1, VIEW_DEVS):
-        copy = pltpu.make_async_remote_copy(
-            src_ref=mine,
-            dst_ref=every.at[view],
-            send_sem=send_sem.at[k - 1],
-            recv_sem=recv_sem.at[k - 1],
-            device_id={"view": lax.rem(view + k, VIEW_DEVS)},
-            device_id_type=pl.DeviceIdType.MESH,
-        )
-        copy.start()
-        copies.append(copy)
-    every[view] = mine[...]
-    for copy in copies:
-        copy.wait()
-
-
-def views_call(mine):
-    vmem = pl.BlockSpec(memory_space=pltpu.VMEM)
-    return pl.pallas_call(
-        views_kernel,
-        out_shape=jax.ShapeDtypeStruct((VIEW_DEVS, VIEW_ROWS, LANES), F32),
-        in_specs=[vmem],
-        out_specs=vmem,
-        scratch_shapes=[
-            pltpu.SemaphoreType.DMA((VIEW_DEVS - 1,)),
-            pltpu.SemaphoreType.DMA((VIEW_DEVS - 1,)),
-        ],
+        ]
+        + pair + many + many + pair + few,
         compiler_params=pltpu.CompilerParams(
-            collective_id=2, has_side_effects=True, vmem_limit_bytes=16 * 2**20
+            collective_id=0, has_side_effects=True, vmem_limit_bytes=40 * 2**20
         ),
-        name="views",
-    )(mine)
-
-
-def param_kernel(dense, every, gradient, packed):
+        name="render",
+    )(camera, tile_ids, tile_len, params, slots, lists, targets)
+
+
+def param_kernel(pictures_in, dense, every, pictures, gradient, packed):
+    pictures[...] = pictures_in[...]
     rows = gradient.shape[0]
 
     def one_half(half, carry):
@@ -744,27 +660,28 @@
             ]
 
 
-def param_call(dense, every):
+def param_call(pictures, dense, every):
     vmem = pl.BlockSpec(memory_space=pltpu.VMEM)
     return pl.pallas_call(
         param_kernel,
-        out_shape=jax.ShapeDtypeStruct((dense.shape[0], 2048), F32),
-        in_specs=[vmem, vmem],
-        out_specs=vmem,
+        out_shape=(
+            jax.ShapeDtypeStruct(pictures.shape, F32),
+            jax.ShapeDtypeStruct((dense.shape[0], 2048), F32),
+        ),
+        in_specs=[vmem, vmem, vmem],
+        out_specs=(vmem, vmem),
         scratch_shapes=[pltpu.VMEM((64 * 16, LANES), F32)],
         compiler_params=pltpu.CompilerParams(vmem_limit_bytes=24 * 2**20),
         name="params",
-    )(dense, every)
+    )(pictures, dense, every)
 
 
 def local(params, cameras, targets, tile_ids, send_slots, tile_lists, tile_len):
-    dense, outgoing = project_call(cameras, params, send_slots)
-    received = exchange_call(forward_kernel, 0, outgoing, "forward")
-    pictures, slot_grads = tile_call(tile_ids, tile_len, received, tile_lists, targets)
-    returned = exchange_call(backward_kernel, 1, slot_grads, "backward")
-    mine = gauss_call(cameras, returned, send_slots)
-    every = views_call(mine)
-    return pictures, param_call(dense, every)
+    pictures, dense, every = render_call(
+        cameras, tile_ids, tile_len, params, send_slots, tile_lists, jnp.transpose(targets, (0, 2, 1, 3))
+    )
+    pictures, gradient = param_call(pictures, dense, every)
+    return jnp.transpose(pictures, (0, 2, 1, 3)), gradient
 
 
 def solution(mesh):

time: 63.2 us -> 54.7 us (0.87)
  Pallas kernels: 59.6 us -> 50 us
  local copies, waits for them, and re-layouts: 2.37 us -> 3.78 us
    pallas_call x7 -> x2, Pallas kernels: 59.6 us -> 50 us  [the longest x1 48 us: render_call(): pl.pallas_call(render_kernel, out_shape=(jax.ShapeDtypeStruct(targets.sha...]
    unnamed x14, local copies, waits for them, and re-layouts: 2.37 us -> 3.78 us
where the time goes in v2:
time: 54.7 us; the launch traced here: 54.5 us
  Pallas kernels  50 us (91%)
  local copies, waits for them, and re-layouts  3.78 us (7%)
  between operations  0.67 us (1%)
    pallas_call x1, Pallas kernels, render_call(): pl.pallas_call(render_kernel, out_shape=(jax.ShapeDtypeStruct(targets.sha...  48 us
    unnamed x14, local copies, waits for them, and re-layouts  3.78 us
    pallas_call x1, Pallas kernels, param_call(): pl.pallas_call(param_kernel, out_shape=(jax.ShapeDtypeStruct(pictures.sha...  1.99 us

profile of v2, /device:TPU:1, one launch (start us, length us, event | category | flops | bytes accessed | tf_op | source)
XLA Modules:
  0.0 54.5 jit_solution(3938145831358692080)
XLA Ops:
  0.6 0.0 copy-start.6
  0.6 0.0 copy-start.5
  0.7 0.0 copy-start.4
  0.7 0.6 %copy-done.6 = s32[1,2]{1,0:T(1,128)S(1)} copy-done((s32[1,2]{1,0:T(1,128)S(1)}, s32[1,2]{1,0:T(1,128)}, u32[]{:S(2)}) %copy-start.6) | copy-done | bytes 32
  1.3 0.0 copy-done.5
  1.3 0.0 copy-done.4
  1.3 0.0 copy-start
  1.3 1.0 %copy-done = f32[59,2048]{1,0:T(8,128)S(1)} copy-done((f32[59,2048]{1,0:T(8,128)S(1)}, f32[59,2048]{1,0:T(8,128)}, u32[]{:S(2)}) %copy-start) | copy-done | bytes 483352
  2.4 0.0 copy-start.1
  2.4 0.7 %copy-done.1 = s32[1,1,2048]{2,1,0:T(1,128)S(1)} copy-done((s32[1,1,2048]{2,1,0:T(1,128)S(1)}, s32[1,1,2048]{2,1,0:T(1,128)}, u32[]{:S(2)}) %copy-start.1) | copy-done | bytes 8216
  3.1 0.0 copy-start.2
  3.1 0.7 %copy-done.2 = f32[1,2,3,256]{3,1,2,0:T(2,128)S(1)} copy-done((f32[1,2,3,256]{3,1,2,0:T(2,128)S(1)}, f32[1,2,3,256]{3,1,2,0:T(2,128)}, u32[]{:S(2)}) %copy-start.2) | copy-done | bytes 6168
  3.8 0.0 copy-start.3
  3.8 0.7 %copy-done.3 = s32[1,2,512]{2,1,0:T(2,128)S(1)} copy-done((s32[1,2,512]{2,1,0:T(2,128)S(1)}, s32[1,2,512]{2,1,0:T(2,128)}, u32[]{:S(2)}) %copy-start.3) | copy-done | bytes 4120
  4.4 48.0 %render.1 = (f32[1,3,2,256]{3,2,1,0:T(2,128)S(1)}, f32[59,16,128]{2,1,0:T(8,128)S(1)}, f32[4,152,128]{2,1,0:T(8,128)S(1)}) custom-call(f32[1,3]{1,0:T(1,128)S(1)} %copy-done.4, s32[1,2]{1,0:T(1,128)S(1)} %copy-done.5, s32[1,2]{1,0:T(1,128)S(1)} %copy-done.6, f32[59,2048]{1,0:T(8,128)S(1)} %copy-done, s32[1,1,2048]{2,1,0:T(1,128)S(1)} %copy-done.1, ...), custom_call_target="tpu_custom_call" | custom-call | tf_op jit(solution)/shard_map/render/pallas_call | solution.py:534
  52.5 2.0 %params.3 = (f32[1,3,2,256]{3,2,1,0:T(2,128)}, f32[59,2048]{1,0:T(8,128)}) custom-call(f32[1,3,2,256]{3,2,1,0:T(2,128)S(1)} %get-tuple-element.7.pictures_in, f32[59,16,128]{2,1,0:T(8,128)S(1)} %get-tuple-element.8.dense, f32[4,152,128]{2,1,0:T(8,128)S(1)} %get-tuple-element.9.every), custom_call_target="tpu_custom_call" | custom-call | tf_op jit(solution)/shard_map/params/pallas_call | solution.py:665
Async XLA Ops:
  0.6 0.7 %copy-start.6 = (s32[1,2]{1,0:T(1,128)S(1)}, s32[1,2]{1,0:T(1,128)}, u32[]{:S(2)}) copy-start(s32[1,2]{1,0:T(1,128)} %tile_len.1) | copy-start | bytes 28
  0.6 0.7 %copy-start.5 = (s32[1,2]{1,0:T(1,128)S(1)}, s32[1,2]{1,0:T(1,128)}, u32[]{:S(2)}) copy-start(s32[1,2]{1,0:T(1,128)} %tile_ids.1) | copy-start | bytes 28
  0.7 0.7 %copy-start.4 = (f32[1,3]{1,0:T(1,128)S(1)}, f32[1,3]{1,0:T(1,128)}, u32[]{:S(2)}) copy-start(f32[1,3]{1,0:T(1,128)} %camera.1) | copy-start | bytes 40
  1.3 1.0 %copy-start = (f32[59,2048]{1,0:T(8,128)S(1)}, f32[59,2048]{1,0:T(8,128)}, u32[]{:S(2)}) copy-start(f32[59,2048]{1,0:T(8,128)} %params.2) | copy-start | bytes 1449988
  2.4 0.7 %copy-start.1 = (s32[1,1,2048]{2,1,0:T(1,128)S(1)}, s32[1,1,2048]{2,1,0:T(1,128)}, u32[]{:S(2)}) copy-start(s32[1,1,2048]{2,1,0:T(1,128)} %slots.1) | copy-start | bytes 24580
  3.1 0.7 %copy-start.2 = (f32[1,2,3,256]{3,1,2,0:T(2,128)S(1)}, f32[1,2,3,256]{3,1,2,0:T(2,128)}, u32[]{:S(2)}) copy-start(f32[1,2,3,256]{3,1,2,0:T(2,128)} %param.9) | copy-start | bytes 18436
  3.8 0.7 %copy-start.3 = (s32[1,2,512]{2,1,0:T(2,128)S(1)}, s32[1,2,512]{2,1,0:T(2,128)}, u32[]{:S(2)}) copy-start(s32[1,2,512]{2,1,0:T(2,128)} %lists.1) | copy-start | bytes 12292

commit v3 on v0

v3 whole, which is shorter than its diff:
```python
import jax
import jax.numpy as jnp
from jax import lax
from jax.experimental import pallas as pl
from jax.experimental.pallas import tpu as pltpu
from jax.sharding import PartitionSpec as P

TILE_SIDE = 16
TILE_COLS = 32
LANES = 128
Y_DEVS = 8
ZC_DEVS = 16
VIEW_DEVS = 4
FEATS = 9
Y_ORDER = (4, 3, 5, 2, 6, 1, 7)
ZC_ORDER = (8, 9, 7, 6, 10, 5, 11, 4, 12, 3, 13, 2, 14, 1, 15)
VIEW_ORDER = (2, 1, 3)
ENTRIES = 512
TILES_DEV = 2
PIXELS = 256
ROWS = 59
G_DEV = 2048
LOG2_E = 1.4426950408889634
F32 = jnp.float32
BF16 = jnp.bfloat16

focal_length = 800.0
dilation = 0.3
sh_first = 0.28209479177387814
sh_second = 0.4886025119029199
sh_third = (
    1.0925484305920792,
    -1.0925484305920792,
    0.31539156525252005,
    -1.0925484305920792,
    0.5462742152960396,
)
sh_fourth = (
    -0.5900435899266435,
    2.890611442640554,
    -0.4570457994644658,
    0.3731763325901154,
    -0.4570457994644658,
    1.445305721320277,
    -0.5900435899266435,
)


def split2(value):
    high = value.astype(BF16)
    return high, (value - high.astype(F32)).astype(BF16)


def dot_nt(lhs, rhs):
    return lax.dot_general(lhs, rhs, (((1,), (1,)), ((), ())), preferred_element_type=F32)


def dot_nn(lhs, rhs):
    return lax.dot_general(lhs, rhs, (((1,), (0,)), ((), ())), preferred_element_type=F32)


def rotation_of(q_w, q_x, q_y, q_z):
    return [
        1.0 - 2.0 * (q_y * q_y + q_z * q_z),
        2.0 * (q_x * q_y - q_w * q_z),
        2.0 * (q_x * q_z + q_w * q_y),
        2.0 * (q_x * q_y + q_w * q_z),
        1.0 - 2.0 * (q_x * q_x + q_z * q_z),
        2.0 * (q_y * q_z - q_w * q_x),
        2.0 * (q_x * q_z - q_w * q_y),
        2.0 * (q_y * q_z + q_w * q_x),
        1.0 - 2.0 * (q_x * q_x + q_y * q_y),
    ]


def unit_quaternion(quaternion):
    total = sum(part * part for part in quaternion[1:]) + quaternion[0] * quaternion[0]
    inverse = lax.rsqrt(total)
    return [part * inverse for part in quaternion], inverse


def shape_matrix(log_scales, quaternion):
    scales = [jnp.exp(part) for part in log_scales]
    unit, inverse = unit_quaternion(quaternion)
    rotation = rotation_of(*unit)
    matrix = [rotation[3 * i + j] * scales[j] for i in range(3) for j in range(3)]
    return matrix, scales, unit, inverse


def harmonics(x, y, z):
    xx, yy, zz = x * x, y * y, z * z
    rim = 4.0 * zz - xx - yy
    gap = xx - yy
    return [
        -sh_second * y,
        sh_second * z,
        -sh_second * x,
        sh_third[0] * (x * y),
        sh_third[1] * (y * z),
        sh_third[2] * (2.0 * zz - xx - yy),
        sh_third[3] * (x * z),
        sh_third[4] * gap,
        sh_fourth[0] * (y * (3.0 * xx - yy)),
        sh_fourth[1] * (x * y * z),
        sh_fourth[2] * (y * rim),
        sh_fourth[3] * (z * (2.0 * zz - 3.0 * xx - 3.0 * yy)),
        sh_fourth[4] * (x * rim),
        sh_fourth[5] * (z * gap),
        sh_fourth[6] * (x * (xx - 3.0 * yy)),
    ]


def geometry(pos, matrix):
    x, y, z = pos
    inv_z = 1.0 / z
    jac = focal_length * inv_z
    screen_x = x * jac
    screen_y = y * jac
    jac_x = -screen_x * inv_z
    jac_y = -screen_y * inv_z
    row_u = [jac * matrix[j] + jac_x * matrix[6 + j] for j in range(3)]
    row_v = [jac * matrix[3 + j] + jac_y * matrix[6 + j] for j in range(3)]
    cov_a = row_u[0] * row_u[0] + row_u[1] * row_u[1] + row_u[2] * row_u[2] + dilation
    cov_c = row_v[0] * row_v[0] + row_v[1] * row_v[1] + row_v[2] * row_v[2] + dilation
    cov_b = row_u[0] * row_v[0] + row_u[1] * row_v[1] + row_u[2] * row_v[2]
    inv_det = 1.0 / (cov_a * cov_c - cov_b * cov_b)
    return inv_z, jac, screen_x, screen_y, jac_x, jac_y, row_u, row_v, cov_a, cov_b, cov_c, inv_det


def direction(pos):
    x, y, z = pos
    inverse = lax.rsqrt(x * x + y * y + z * z)
    return [x * inverse, y * inverse, z * inverse], inverse


def raw_colour(load, channel, basis):
    total = load(11 + 16 * channel) * sh_first
    for j in range(15):
        total = total + load(12 + 16 * channel + j) * basis[j]
    return total + 0.5


KEPT = 40
SHAPE_ROWS = 17


def keep_view(load, shift, matrix, saved, base):
    pos = [load(i) - shift[i] for i in range(3)]
    inv_z, jac, screen_x, screen_y, jac_x, jac_y, row_u, row_v, cov_a, cov_b, cov_c, inv_det = geometry(pos, matrix)
    unit, inv_len = direction(pos)
    basis = harmonics(*unit)
    raw = [raw_colour(load, channel, basis) for channel in range(3)]
    gates = [jnp.where(value > 0.0, 1.0, jnp.where(value < 0.0, 0.0, 0.5)) for value in raw]
    values = [pos[0], pos[1], inv_z, jac, screen_x, screen_y, jac_x, jac_y]
    values += row_u + row_v + [cov_a, cov_b, cov_c, inv_det] + unit + [inv_len] + basis + gates
    for i, value in enumerate(values):
        saved[base + i] = value
    features = [screen_x, screen_y, cov_c * inv_det, -cov_b * inv_det, cov_a * inv_det]
    features.append(1.0 / (1.0 + jnp.exp(-load(10))))
    return features + [jnp.maximum(value, 0.0) for value in raw]


def pull_view(load, slot, matrix, saved, base, totals, total_base, first, colour, colour_base):
    kept = lambda i: saved[base + i]
    inv_z, jac, screen_x, screen_y, jac_x, jac_y = [kept(2 + i) for i in range(6)]
    row_u, row_v = [kept(8 + i) for i in range(3)], [kept(11 + i) for i in range(3)]
    cov_a, cov_b, cov_c, inv_det = [kept(14 + i) for i in range(4)]
    g_a, g_b, g_c = slot(2), slot(3), slot(4)
    g_det = -(g_a * cov_c - g_b * cov_b + g_c * cov_a) * inv_det * inv_det
    d_a = 2.0 * (g_c * inv_det + g_det * cov_c)
    d_c = 2.0 * (g_a * inv_det + g_det * cov_a)
    d_b = -g_b * inv_det - 2.0 * g_det * cov_b
    g_u = [d_a * row_u[j] + d_b * row_v[j] for j in range(3)]
    g_v = [d_c * row_v[j] + d_b * row_u[j] for j in range(3)]
    g_matrix = [jac * g_u[j] for j in range(3)] + [jac * g_v[j] for j in range(3)]
    g_matrix += [jac_x * g_u[j] + jac_y * g_v[j] for j in range(3)]
    g_jac = sum(g_u[j] * matrix[j] + g_v[j] * matrix[3 + j] for j in range(1, 3)) + (
        g_u[0] * matrix[0] + g_v[0] * matrix[3]
    )
    g_jac_x = g_u[0] * matrix[6] + g_u[1] * matrix[7] + g_u[2] * matrix[8]
    g_jac_y = g_v[0] * matrix[6] + g_v[1] * matrix[7] + g_v[2] * matrix[8]
    g_sx = slot(0) - inv_z * g_jac_x
    g_sy = slot(1) - inv_z * g_jac_y
    g_inv = focal_length * (g_jac + kept(0) * g_sx + kept(1) * g_sy) - screen_x * g_jac_x - screen_y * g_jac_y
    g_pos = [jac * g_sx, jac * g_sy, -inv_z * inv_z * g_inv]

    g_basis = None
    for channel in range(3):
        g_colour = slot(6 + channel) * kept(37 + channel)
        colour[colour_base + channel] = g_colour
        terms = [load(12 + 16 * channel + j) * g_colour for j in range(15)]
        g_basis = terms if g_basis is None else [a + b for a, b in zip(g_basis, terms)]
    unit, inv_len = [kept(18 + i) for i in range(3)], kept(21)
    _, pull = jax.vjp(harmonics, *unit)
    g_unit = pull(g_basis)
    along = unit[0] * g_unit[0] + unit[1] * g_unit[1] + unit[2] * g_unit[2]
    for i in range(3):
        g_pos[i] = g_pos[i] + inv_len * (g_unit[i] - unit[i] * along)
    for i, value in enumerate(g_pos + g_matrix + [slot(5)]):
        totals[total_base + i] = value if first else totals[total_base + i] + value


def lane_gather(source, index):
    return jnp.take_along_axis(source, index, axis=1, mode="promise_in_bounds")


def gather_chunk(table, index):
    shape = (8, LANES)
    low = jnp.broadcast_to(index & 127, shape)
    high = jnp.broadcast_to(index >> 7, shape)
    top = bottom = jnp.zeros(shape, F32)
    for chunk in range(16):
        here = high == chunk
        top = jnp.where(here, lane_gather(table[pl.ds(16 * chunk, 8), :], low), top)
        bottom = jnp.where(here, lane_gather(table[pl.ds(16 * chunk + 8, 8), :], low), bottom)
    return top, bottom


def block_transpose(rows):
    group = lax.broadcasted_iota(jnp.int32, rows[0].shape, 1) // 16
    for step in (1, 2, 4):
        odd = (group & step) != 0
        fresh = list(rows)
        for i in range(8):
            if i & step:
                continue
            first, second = rows[i], rows[i + step]
            fresh[i] = jnp.where(odd, pltpu.roll(second, 16 * step, 1), first)
            fresh[i + step] = jnp.where(odd, second, pltpu.roll(first, LANES - 16 * step, 1))
        rows = fresh
    return rows


def remote(src_ref, dst_ref, send_sem, recv_sem, device_id):
    copy = pltpu.make_async_remote_copy(
        src_ref=src_ref,
        dst_ref=dst_ref,
        send_sem=send_sem,
        recv_sem=recv_sem,
        device_id=device_id,
        device_id_type=pl.DeviceIdType.MESH,
    )
    copy.start()
    return copy


def y_peer(my_y, my_zc, k):
    peer = lax.rem(my_y + k, Y_DEVS)
    return peer, {"cell": peer * ZC_DEVS + my_zc}


def zc_peer(my_y, my_zc, k):
    peer = lax.rem(my_zc + k, ZC_DEVS)
    return peer, {"cell": my_y * ZC_DEVS + peer}


def view_peer(view, k):
    return {"view": lax.rem(view + k, VIEW_DEVS)}


def greet(my_y, my_zc, view):
    barrier = pltpu.get_barrier_semaphore()
    peers = [y_peer(my_y, my_zc, k)[1] for k in Y_ORDER]
    peers += [zc_peer(my_y, my_zc, k)[1] for k in ZC_ORDER]
    peers += [view_peer(view, k) for k in VIEW_ORDER]
    for peer in peers:
        pl.semaphore_signal(barrier, inc=1, device_id=peer, device_id_type=pl.DeviceIdType.MESH)
    return barrier, len(peers)


def regroup(load, store):
    for half in range(2):
        for j, rows in enumerate(block_transpose([load(i, half) for i in range(8)])):
            store(j, half, rows)


def part_lanes(chunk):
    base = (chunk // 2) * 512 + (chunk % 2) * LANES
    return pl.ds(base, LANES), pl.ds(base + 256, LANES)


def fill_triangles(upper, lower):
    row = lax.broadcasted_iota(jnp.int32, (256, 256), 0)
    col = lax.broadcasted_iota(jnp.int32, (256, 256), 1)
    above = jnp.where(row < col, 1.0, 0.0).astype(BF16)
    below = jnp.where(row > col, 1.0, 0.0).astype(BF16)
    ones = jnp.ones((256, 256), BF16)
    for i in range(4):
        upper[pl.ds(256 * i, 256), :] = ones if i < 2 else above
        lower[pl.ds(256 * i, 256), :] = below if i < 2 else ones


def entry_slot(lists, tile, chunk):
    index = lists[0, pl.ds(tile, 1), pl.ds(chunk * LANES, LANES)]
    return (index >> 4) & 15, ((index >> 8) << 4) | (index & 15)


def hot_rows(index, count):
    shape = (count, LANES)
    return jnp.where(
        jnp.broadcast_to(index, shape) == lax.broadcasted_iota(jnp.int32, shape, 0), 1.0, 0.0
    ).astype(BF16)


def fill_masks(high, count, masks, base):
    high = jnp.broadcast_to(high, (16, LANES))
    for value in range(count):
        masks[pl.ds(base + 16 * value, 16), :] = jnp.where(high == value, 1.0, 0.0).astype(BF16)


def spread(values, count, masks, base, left, column):
    for i, piece in enumerate(split2(values)):
        for value in range(count):
            left[pl.ds((i * count + value) * 16, 16), pl.ds(column, LANES)] = (
                masks[pl.ds(base + 16 * value, 16), :] * piece
            )


def tile_body(
    tile_ids, tile_len, targets, pictures, slot_grads,
    feats, alpha, ratio, plane, weight, part, upper, lower, grads, masks, left, right,
):
    chunks = ENTRIES // LANES
    half = ENTRIES // 2
    for tile in range(TILES_DEV):
        number = tile_ids[0, tile]
        length = tile_len[0, tile]
        left_x = (TILE_SIDE * lax.rem(number, TILE_COLS)).astype(F32) + 0.5
        top_y = (TILE_SIDE * (number // TILE_COLS)).astype(F32) + 0.5
        shape = (TILE_SIDE, LANES)
        pixel_x = lax.broadcasted_iota(jnp.int32, shape, 0).astype(F32) + left_x
        whole = pl.ds(tile * ENTRIES, ENTRIES)

        def row_of(f, chunk):
            return feats[pl.ds(f, 1), pl.ds(tile * ENTRIES + chunk * LANES, LANES)]

        def feature(f, chunk):
            return jnp.broadcast_to(row_of(f, chunk), (8, LANES))

        def twice(rows):
            return jnp.concatenate([rows, rows], axis=0)

        def pixels_of(y):
            return pl.ds(pl.multiple_of(y * TILE_SIDE, TILE_SIDE), TILE_SIDE)

        for chunk in range(chunks):
            lanes = pl.ds(chunk * LANES, LANES)
            high, low = part_lanes(chunk)
            lane = lax.broadcasted_iota(jnp.int32, (8, LANES), 1) + chunk * LANES
            log_opacity = jnp.where(lane < length, jnp.log2(feature(5, chunk)), -1e30)
            delta_x = twice(feature(0, chunk)) - pixel_x
            part_x = twice((-0.5 * LOG2_E) * feature(2, chunk)) * delta_x * delta_x + twice(log_opacity)
            cross = twice(-LOG2_E * feature(3, chunk)) * delta_x
            screen_y = feature(1, chunk) - top_y
            conic_c = (-0.5 * LOG2_E) * feature(4, chunk)

            def one_row(y, carry):
                rows = pixels_of(y)
                delta_y = screen_y - y.astype(F32)
                part_y = conic_c * delta_y * delta_y
                value = jnp.exp2(part_x + cross * twice(delta_y) + twice(part_y))
                keep = jnp.log2(1.0 - value)
                alpha[rows, lanes] = value
                ratio[rows, lanes] = value * jnp.exp2(-keep)
                part[rows, high], part[rows, low] = split2(keep)
                return carry

            lax.fori_loop(0, TILE_SIDE, one_row, 0, unroll=TILE_SIDE)

        plane[:, pl.ds(0, half)] = dot_nn(part[:, pl.ds(0, 512)], upper[pl.ds(512, 512), :])
        plane[:, pl.ds(half, half)] = dot_nn(part[...], upper[...])

        for chunk in range(chunks):
            lanes = pl.ds(chunk * LANES, LANES)
            high, low = part_lanes(chunk)

            def one_weight(y, carry):
                rows = pixels_of(y)
                value = jnp.exp2(plane[rows, lanes]) * alpha[rows, lanes]
                weight[rows, lanes] = value
                part[rows, high], part[rows, low] = split2(value)
                return carry

            lax.fori_loop(0, TILE_SIDE, one_weight, 0, unroll=TILE_SIDE)

        colours = jnp.concatenate([feats[pl.ds(6, 3), whole], jnp.zeros((5, ENTRIES), F32)], axis=0)
        colour_hi = colours.astype(BF16).astype(F32)
        colour_lo = (colours - colour_hi).astype(BF16).astype(F32)
        both = jnp.concatenate([colour_hi, colour_lo], axis=0)
        both = jnp.concatenate([both[:, :half], both[:, :half], both[:, half:], both[:, half:]], axis=1)
        product = dot_nt(both.astype(BF16), part[...])
        picture = product[0:8] + product[8:16]
        pictures[0, :, tile, :] = picture[0:3]
        residual = picture - jnp.concatenate([targets[0, :, tile, :], jnp.zeros((5, PIXELS), F32)], axis=0)
        residual_hi = residual.astype(BF16).astype(F32)
        residual_lo = (residual - residual_hi).astype(BF16).astype(F32)
        pair = jnp.concatenate([residual_hi, residual_lo], axis=0).astype(BF16)
        product = dot_nn(pair, part[...])
        product = product[0:8] + product[8:16]
        grads[pl.ds(6, 3), whole] = jnp.concatenate(
            [product[0:3, 0:256] + product[0:3, 256:512], product[0:3, 512:768] + product[0:3, 768:1024]], axis=1
        )
        stack = jnp.concatenate([residual_hi, residual_lo, residual_hi, jnp.zeros((104, PIXELS), F32)], axis=0)
        rows24 = jnp.concatenate([colour_hi, colour_hi, colour_lo, jnp.zeros((104, ENTRIES), F32)], axis=0)
        plane[...] = dot_nn(jnp.transpose(stack).astype(BF16), rows24.astype(BF16))

        for chunk in range(chunks):
            lanes = pl.ds(chunk * LANES, LANES)
            high, low = part_lanes(chunk)

            def one_share(y, carry):
                rows = pixels_of(y)
                value = plane[rows, lanes] * weight[rows, lanes]
                weight[rows, lanes] = value
                part[rows, high], part[rows, low] = split2(value)
                return carry

            lax.fori_loop(0, TILE_SIDE, one_share, 0, unroll=TILE_SIDE)

        plane[:, pl.ds(0, half)] = dot_nn(part[...], lower[...])
        plane[:, pl.ds(half, half)] = dot_nn(part[:, pl.ds(512, 512)], lower[pl.ds(0, 512), :])

        for chunk in range(chunks):
            lanes = pl.ds(chunk * LANES, LANES)
            screen_y = feature(1, chunk) - top_y

            def one_sum(y, carry):
                rows = pixels_of(y)
                sum_0, sum_1, sum_2 = carry
                delta_y = twice(screen_y - y.astype(F32))
                grad = weight[rows, lanes] - plane[rows, lanes] * ratio[rows, lanes]
                slope = grad * delta_y
                return sum_0 + grad, sum_1 + slope, sum_2 + slope * delta_y

            zero = jnp.zeros(shape, F32)
            sum_0, sum_1, sum_2 = lax.fori_loop(0, TILE_SIDE, one_sum, (zero, zero, zero), unroll=TILE_SIDE)
            delta_x = twice(feature(0, chunk)) - pixel_x
            over = lambda rows: jnp.sum(rows, axis=0, keepdims=True)
            first_x = over(delta_x * sum_0)
            first_y = over(sum_1)
            out = pl.ds(tile * ENTRIES + chunk * LANES, LANES)
            grads[pl.ds(0, 1), out] = -row_of(2, chunk) * first_x - row_of(3, chunk) * first_y
            grads[pl.ds(1, 1), out] = -row_of(4, chunk) * first_y - row_of(3, chunk) * first_x
            grads[pl.ds(2, 1), out] = -0.5 * over(delta_x * delta_x * sum_0)
            grads[pl.ds(3, 1), out] = -over(delta_x * sum_1)
            grads[pl.ds(4, 1), out] = -0.5 * over(sum_2)
            grads[pl.ds(5, 1), out] = over(sum_0)

    for n in range(TILES_DEV * chunks):
        spread(grads[:, pl.ds(n * LANES, LANES)], 16, masks, n * 256, left, n * LANES)
    total = dot_nt(left[...], right[...])
    for zc in range(16):
        slot_grads[zc] = total[16 * zc : 16 * zc + FEATS] + total[256 + 16 * zc : 256 + 16 * zc + FEATS]


Y_ARRIVAL = (0, 1, 7, 2, 6, 3, 5, 4)
ZC_ARRIVAL = (0, 1, 15, 2, 14, 3, 13, 4, 12, 5, 11, 6, 10, 7, 9, 8)
LAST = 7 * 256


def render_kernel(
    camera, tile_ids, tile_len, params_hbm, slots_hbm, lists_hbm, targets_hbm,
    pictures_hbm, gradient_hbm,
    params, packed, dense, lists, targets, pictures, slots, cams,
    table, outgoing, landed, staged, received, slot_grads, landed_back, staged_back, returned, every,
    feats, alpha, ratio, plane, weight, part, upper, lower, grads, masks, left, right,
    view_masks, view_left, view_right, view_grads, saved, shape_rows, totals, colour,
    load_sem, store_sem, send_y, recv_y, send_zc, recv_zc, send_zc2, recv_zc2, send_y2, recv_y2,
    send_slots, recv_slots, send_cams, recv_cams, send_view, recv_view,
):
    cell, view = lax.axis_index("cell"), lax.axis_index("view")
    my_y, my_zc = cell // ZC_DEVS, lax.rem(cell, ZC_DEVS)
    barrier, greetings = greet(my_y, my_zc, view)

    loads = [
        pltpu.make_async_copy(source, target, load_sem.at[i])
        for i, (source, target) in enumerate(
            (
                (params_hbm.at[pl.ds(0, 16)], params.at[pl.ds(0, 16)]),
                (params_hbm.at[pl.ds(16, ROWS - 16)], params.at[pl.ds(16, ROWS - 16)]),
                (slots_hbm, slots.at[0]),
                (lists_hbm, lists),
                (targets_hbm, targets),
            )
        )
    ]
    for load in loads:
        load.start()
    table[...] = jnp.zeros_like(table)
    feats[...] = jnp.zeros_like(feats)
    grads[...] = jnp.zeros_like(grads)
    shift_row = lax.broadcasted_iota(jnp.int32, (8, LANES), 0)
    cams[0] = jnp.where(shift_row == 0, camera[0, 0], jnp.where(shift_row == 1, camera[0, 1], camera[0, 2]))

    def unpack(first, last):
        for group in range(first, last, 8):
            size = min(8, last - group)
            for chunk in range(16):
                packed[pl.ds(group * 16 + chunk * 8, size), :] = params[
                    pl.ds(group, size), pl.ds(chunk * LANES, LANES)
                ]
        for row in range(first, last):
            for half in range(2):
                dense[2 * row + half] = packed[pl.ds((row // 8) * 128 + half * 8 + row % 8, 8, stride=16), :]

    def loader(half):
        return lambda row: dense[2 * row + half]

    loads[0].wait()
    unpack(0, 16)
    loads[1].wait()
    unpack(16, ROWS)

    for half in range(2):
        load = loader(half)
        matrix, scales, unit_q, inv_norm = shape_matrix([load(3 + i) for i in range(3)], [load(6 + i) for i in range(4)])
        for i, value in enumerate(matrix + scales + unit_q + [inv_norm]):
            shape_rows[half * SHAPE_ROWS + i] = value
        features = keep_view(load, [camera[0, i] for i in range(3)], matrix, saved, half * KEPT)
        for f, feature in enumerate(features):
            table[pl.ds(half * 16 + f, 8, stride=32), :] = feature

    loads[2].wait()
    pl.semaphore_wait(barrier, greetings)
    y_sends = {}
    for k in Y_ORDER + (0,):
        peer, device_id = y_peer(my_y, my_zc, k)
        for half in range(2):
            chunk = 2 * peer + half
            top, bottom = gather_chunk(table, slots[0, pl.ds(chunk, 1), :])
            outgoing[chunk, pl.ds(0, 8), :] = top
            outgoing[chunk, pl.ds(8, 1), :] = bottom[0:1]
        if k:
            y_sends[k] = remote(
                outgoing.at[pl.ds(2 * peer, 2)], landed.at[pl.ds(2 * my_y, 2)],
                send_y.at[k - 1], recv_y.at[k - 1], device_id,
            )
    landed[pl.ds(2 * my_y, 2)] = outgoing[pl.ds(2 * my_y, 2)]
    side_sends = []
    for k in VIEW_ORDER:
        peer = view_peer(view, k)
        side_sends.append(remote(slots.at[0], slots.at[k], send_slots.at[k - 1], recv_slots.at[k - 1], peer))
        side_sends.append(remote(cams.at[0], cams.at[k], send_cams.at[k - 1], recv_cams.at[k - 1], peer))

    fill_triangles(upper, lower)
    loads[3].wait()
    loads[4].wait()
    for tile in range(TILES_DEV):
        for chunk in range(ENTRIES // LANES):
            n = tile * (ENTRIES // LANES) + chunk
            high, low = entry_slot(lists, tile, chunk)
            fill_masks(high, 16, masks, n * 256)
            right[:, pl.ds(n * LANES, LANES)] = hot_rows(low, LANES)

    def view_factors(k):
        for p, step in enumerate(Y_ARRIVAL):
            for half in range(2):
                n = 2 * p + half
                index = slots[k, pl.ds(2 * lax.rem(my_y + Y_DEVS - step, Y_DEVS) + half, 1), :]
                fill_masks(index >> 8, 8, view_masks, (k * 16 + n) * 128)
                view_right[k, :, pl.ds(n * LANES, LANES)] = hot_rows(index & 255, 256)

    view_factors(0)
    for k in Y_ORDER:
        y_sends[k].wait()

    def to_zc(j, half, rows):
        staged[8 * half + j] = rows

    regroup(lambda i, half: landed[2 * i + half], to_zc)
    zc_sends = {}
    for k in ZC_ORDER:
        peer, device_id = zc_peer(my_y, my_zc, k)
        zc_sends[k] = remote(
            staged.at[peer], received.at[my_zc], send_zc.at[k - 1], recv_zc.at[k - 1], device_id
        )
    received[my_zc] = staged[my_zc]

    for copy in side_sends:
        copy.wait()
    for k in range(1, VIEW_DEVS):
        for half in range(2):
            shift = [jnp.broadcast_to(cams[k, pl.ds(i, 1), :], (8, LANES)) for i in range(3)]
            matrix = [shape_rows[half * SHAPE_ROWS + i] for i in range(9)]
            keep_view(loader(half), shift, matrix, saved, (2 * k + half) * KEPT)
        view_factors(k)

    places = [entry_slot(lists, n // 4, n % 4) for n in range(8)]
    places = [(jnp.broadcast_to(high, (8, LANES)), jnp.broadcast_to(low, (8, LANES))) for high, low in places]
    tops = [jnp.zeros((8, LANES), F32)] * 8
    bottoms = [jnp.zeros((8, LANES), F32)] * 8
    for k in ZC_ARRIVAL:
        if k:
            zc_sends[k].wait()
        source = lax.rem(my_zc + ZC_DEVS - k, ZC_DEVS)
        top = received[source, pl.ds(0, 8), :]
        bottom = jnp.broadcast_to(received[source, pl.ds(8, 1), :], (8, LANES))
        for n, (high, low) in enumerate(places):
            here = high == source
            tops[n] = jnp.where(here, lane_gather(top, low), tops[n])
            bottoms[n] = jnp.where(here, lane_gather(bottom, low), bottoms[n])
    for n in range(8):
        feats[pl.ds(0, 8), pl.ds(n * LANES, LANES)] = tops[n]
        feats[pl.ds(8, 8), pl.ds(n * LANES, LANES)] = bottoms[n]

    tile_body(
        tile_ids, tile_len, targets, pictures, slot_grads,
        feats, alpha, ratio, plane, weight, part, upper, lower, grads, masks, left, right,
    )
    store_pictures = pltpu.make_async_copy(pictures, pictures_hbm, store_sem.at[0])
    store_pictures.start()

    for k in ZC_ORDER:
        peer, device_id = zc_peer(my_y, my_zc, k)
        zc_sends[k] = remote(
            slot_grads.at[peer], landed_back.at[my_zc], send_zc2.at[k - 1], recv_zc2.at[k - 1], device_id
        )
    landed_back[my_zc] = slot_grads[my_zc]
    for k in ZC_ORDER[::-1]:
        zc_sends[k].wait()

    def to_y(j, half, rows):
        staged_back[2 * j + half] = rows

    regroup(lambda i, half: landed_back[8 * half + i], to_y)
    for k in Y_ORDER:
        peer, device_id = y_peer(my_y, my_zc, k)
        y_sends[k] = remote(
            staged_back.at[pl.ds(2 * peer, 2)], returned.at[pl.ds(2 * my_y, 2)],
            send_y2.at[k - 1], recv_y2.at[k - 1], device_id,
        )
    returned[pl.ds(2 * my_y, 2)] = staged_back[pl.ds(2 * my_y, 2)]

    def add_left(k, p, block):
        for half in range(2):
            n = 2 * p + half
            values = jnp.concatenate(
                [block(half, 0, 8), jnp.broadcast_to(block(half, 8, 1), (8, LANES))], axis=0
            )
            spread(values, 8, view_masks, (k * 16 + n) * 128, view_left.at[k], n * LANES)

    def scatter(k, columns, first):
        product = dot_nt(view_left[k, :, columns], view_right[k, :, columns])
        for half in range(2):
            lanes = slice(half * LANES, (half + 1) * LANES)
            rows = pl.ds((2 * k + half) * 128, 128)
            value = product[0:128, lanes] + product[128:256, lanes]
            view_grads[rows, :] = value if first else view_grads[rows, :] + value

    def pull(k):
        for half in range(2):
            matrix = [shape_rows[half * SHAPE_ROWS + i] for i in range(9)]
            slot = lambda f: view_grads[pl.ds((2 * k + half) * 128 + f, 8, stride=16), :]
            pull_view(
                loader(half), slot, matrix, saved, (2 * k + half) * KEPT, totals, half * 13, k == 0,
                colour, (2 * k + half) * 3,
            )

    view_sends = {}
    for p, step in enumerate(Y_ARRIVAL):
        if step:
            y_sends[step].wait()
        y = lax.rem(my_y + Y_DEVS - step, Y_DEVS)
        for k in VIEW_ORDER:
            view_sends[k, p] = remote(
                returned.at[pl.ds(2 * y, 2)], every.at[k, pl.ds(2 * p, 2)],
                send_view.at[k - 1, p], recv_view.at[k - 1, p], view_peer(view, k),
            )
        add_left(0, p, lambda half, row, size, y=y: returned[2 * y + half, pl.ds(row, size), :])
    scatter(0, pl.ds(0, G_DEV), True)
    pull(0)
    for p in range(8):
        for k in (1, 3, 2):
            view_sends[k, p].wait()
            add_left(k, p, lambda half, row, size: every[k, 2 * p + half, pl.ds(row, size), :])
            if p == 6:
                scatter(k, pl.ds(0, LAST), True)
            if p == 7:
                scatter(k, pl.ds(LAST, 256), False)
                pull(k)

    def put(row, half, value):
        packed[pl.ds((row // 8) * 128 + half * 8 + row % 8, 8, stride=16), :] = value

    def pack(first, last):
        for group in range(first, last, 8):
            size = min(8, last - group)
            for chunk in range(16):
                params[pl.ds(group, size), pl.ds(chunk * LANES, LANES)] = packed[
                    pl.ds(group * 16 + chunk * 8, size), :
                ]

    for half in range(2):
        kept = lambda k, i: saved[(2 * k + half) * KEPT + i]
        for channel in range(3):
            parts = [colour[(2 * k + half) * 3 + channel] for k in range(VIEW_DEVS)]
            put(11 + 16 * channel, half, sh_first * (parts[0] + parts[1] + parts[2] + parts[3]))
            for j in range(15):
                terms = [kept(k, 22 + j) * parts[k] for k in range(VIEW_DEVS)]
                put(12 + 16 * channel + j, half, terms[0] + terms[1] + terms[2] + terms[3])
    pack(16, ROWS)
    store_tail = pltpu.make_async_copy(
        params.at[pl.ds(16, ROWS - 16)], gradient_hbm.at[pl.ds(16, ROWS - 16)], store_sem.at[1]
    )
    store_tail.start()
    for half in range(2):
        total = [totals[half * 13 + i] for i in range(13)]
        shape = [shape_rows[half * SHAPE_ROWS + i] for i in range(SHAPE_ROWS)]
        matrix, scales, unit_q, inv_norm = shape[0:9], shape[9:12], shape[12:16], shape[16]
        for i in range(3):
            put(i, half, total[i])
            put(3 + i, half, sum(total[3 + 3 * r + i] * matrix[3 * r + i] for r in range(1, 3)) + total[3 + i] * matrix[i])
        _, pull_back = jax.vjp(rotation_of, *unit_q)
        g_unit = pull_back([total[3 + 3 * i + j] * scales[j] for i in range(3) for j in range(3)])
        along = unit_q[0] * g_unit[0] + unit_q[1] * g_unit[1] + unit_q[2] * g_unit[2] + unit_q[3] * g_unit[3]
        for i in range(4):
            put(6 + i, half, inv_norm * (g_unit[i] - unit_q[i] * along))
        put(10, half, total[12] * (1.0 / (1.0 + jnp.exp(dense[20 + half]))))
    pack(0, 16)
    store_head = pltpu.make_async_copy(params.at[pl.ds(0, 16)], gradient_hbm.at[pl.ds(0, 16)], store_sem.at[2])
    store_head.start()
    store_pictures.wait()
    store_tail.wait()
    store_head.wait()


def render_call(camera, tile_ids, tile_len, params, slots, lists, targets):
    smem = pl.BlockSpec(memory_space=pltpu.SMEM)
    anywhere = pl.BlockSpec(memory_space=pl.ANY)
    plane = pltpu.VMEM((PIXELS, ENTRIES), F32)
    blocks = pltpu.VMEM((16, FEATS, LANES), F32)
    tile = (8, LANES)
    y_sems = [pltpu.SemaphoreType.DMA((Y_DEVS - 1,))] * 2
    zc_sems = [pltpu.SemaphoreType.DMA((ZC_DEVS - 1,))] * 2
    view_sems = [pltpu.SemaphoreType.DMA((VIEW_DEVS - 1,))] * 2
    return pl.pallas_call(
        render_kernel,
        out_shape=(
            jax.ShapeDtypeStruct(targets.shape, F32),
            jax.ShapeDtypeStruct(params.shape, F32),
        ),
        in_specs=[smem, smem, smem, anywhere, anywhere, anywhere, anywhere],
        out_specs=(anywhere, anywhere),
        scratch_shapes=[
            pltpu.VMEM((ROWS, G_DEV), F32),
            pltpu.VMEM((64 * 16, LANES), F32),
            pltpu.VMEM((2 * ROWS,) + tile, F32),
            pltpu.VMEM(lists.shape, jnp.int32),
            pltpu.VMEM(targets.shape, F32),
            pltpu.VMEM(targets.shape, F32),
            pltpu.VMEM((VIEW_DEVS, 16, LANES), jnp.int32),
            pltpu.VMEM((VIEW_DEVS,) + tile, F32),
            pltpu.VMEM((256, LANES), F32),
        ]
        + [blocks] * 8
        + [
            pltpu.VMEM((VIEW_DEVS, 16, FEATS, LANES), F32),
            pltpu.VMEM((16, TILES_DEV * ENTRIES), F32),
            plane,
            plane,
            plane,
            plane,
            pltpu.VMEM((PIXELS, 2 * ENTRIES), BF16),
            pltpu.VMEM((1024, 256), BF16),
            pltpu.VMEM((1024, 256), BF16),
            pltpu.VMEM((16, TILES_DEV * ENTRIES), F32),
            pltpu.VMEM((8 * 256, LANES), BF16),
            pltpu.VMEM((512, TILES_DEV * ENTRIES), BF16),
            pltpu.VMEM((LANES, TILES_DEV * ENTRIES), BF16),
            pltpu.VMEM((VIEW_DEVS * 16 * 128, LANES), BF16),
            pltpu.VMEM((VIEW_DEVS, 256, G_DEV), BF16),
            pltpu.VMEM((VIEW_DEVS, 256, G_DEV), BF16),
            pltpu.VMEM((VIEW_DEVS * 256, LANES), F32),
            pltpu.VMEM((VIEW_DEVS * 2 * KEPT,) + tile, F32),
            pltpu.VMEM((2 * SHAPE_ROWS,) + tile, F32),
            pltpu.VMEM((2 * 13,) + tile, F32),
            pltpu.VMEM((VIEW_DEVS * 2 * 3,) + tile, F32),
            pltpu.SemaphoreType.DMA((5,)),
            pltpu.SemaphoreType.DMA((3,)),
        ]
        + y_sems + zc_sems + zc_sems + y_sems + view_sems + view_sems
        + [pltpu.SemaphoreType.DMA((VIEW_DEVS - 1, 8))] * 2,
        compiler_params=pltpu.CompilerParams(
            collective_id=0, has_side_effects=True, vmem_limit_bytes=58 * 2**20
        ),
        name="render",
    )(camera, tile_ids, tile_len, params, slots, lists, targets)


def local(params, cameras, targets, tile_ids, send_slots, tile_lists, tile_len):
    pictures, gradient = render_call(
        cameras, tile_ids, tile_len, params, send_slots.reshape(16, LANES), tile_lists,
        jnp.transpose(targets, (0, 2, 1, 3)),
    )
    return jnp.transpose(pictures, (0, 2, 1, 3)), gradient


def solution(mesh):
    return jax.shard_map(
        local,
        mesh=mesh,
        in_specs=(
            P(None, "cell"),
            P("view", None),
            P("view", "cell", None, None),
            P("view", "cell"),
            P("view", "cell", None),
            P("view", "cell", None),
            P("view", "cell"),
        ),
        out_specs=(P("view", "cell", None, None), P(None, "cell")),
        check_vma=False,
    )
```

time: 275 us -> 52.4 us (0.19); the launches traced: 270 us -> 52.2 us
  other arithmetic: 74 us -> 0 us
  local copies, waits for them, and re-layouts: 74.7 us -> 3.16 us
  waiting for transfers between devices: 55.9 us -> 0 us
  Pallas kernels: 0 us -> 48.4 us
  starting transfers between devices: 18.8 us -> 0 us
  blocking collectives: 17.6 us -> 0 us
  between operations: 14.9 us -> 0.64 us
  matrix products: 8.49 us -> 0 us
  loops' own time: 6 us -> 0 us
    pallas_call x0 -> x1, Pallas kernels: none -> 48.4 us  [render_call(): pl.pallas_call(render_kernel, out_shape=(jax.ShapeDtypeStruct(targets.sha...]
    psum x1 -> x0, waiting for transfers between devices: 44.6 us -> none  [sum_views(): return lax.psum(local_grad, 'view')]
    unnamed x158 -> x2, local copies, waits for them, and re-layouts: 23.1 us -> 3.16 us
    scatter-add x2 -> x0, other arithmetic: 19.4 us -> none  [the longest x1 12 us: local(): jnp.zeros((returned.shape[0], params.shape[1]), jnp.float32)]
    add_any x11 -> x0, other arithmetic: 19.3 us -> none  [the longest x1 3.3 us: project(): inv_depth = 1.0 / depth_cam]
    all_to_all x1 -> x0, starting transfers between devices: 18.6 us -> none  [local(): lax.all_to_all(outgoing, 'cell', split_axis=1, concat_axis=1, tiled=True)]
    all_to_all x1 -> x0, blocking collectives: 17.6 us -> none  [local(): lax.all_to_all(slot_grads, 'cell', split_axis=1, concat_axis=1, tiled=True)]
    mul x18 -> x0, other arithmetic: 14.3 us -> none  [the longest x2 3.77 us: project(): colors = jnp.maximum(jnp.sum(coeffs * sh_basis[None], axis=1) + 0.5, 0.0)]
  transfers between devices with their start and end apart: 2 -> 0, of which waited for: 2 -> 0; matrix products, arithmetic and copies ran while one was open for 0% -> 0% of each run, Pallas kernels for 0% -> 0%
where the time goes in v3:
time: 52.4 us; the launch traced here: 52.2 us
  Pallas kernels  48.4 us (92%)
  local copies, waits for them, and re-layouts  3.16 us (6%)
  between operations  0.64 us (1%)
    pallas_call x1, Pallas kernels, render_call(): pl.pallas_call(render_kernel, out_shape=(jax.ShapeDtypeStruct(targets.sha...  48.4 us
    unnamed x2, local copies, waits for them, and re-layouts  3.16 us

profile of v3, /device:TPU:1, one launch (start us, length us, event | category | flops | bytes accessed | tf_op | source)
XLA Modules:
  0.0 52.2 jit_solution(16202778237203348049)
XLA Ops:
  0.6 48.4 %render.1 = (f32[1,3,2,256]{3,2,1,0:T(2,128)}, f32[59,2048]{1,0:T(8,128)}) custom-call(f32[1,3]{1,0:T(1,128)} %camera.1, s32[1,2]{1,0:T(1,128)} %tile_ids.1, s32[1,2]{1,0:T(1,128)} %tile_len.1, f32[59,2048]{1,0:T(8,128)} %params_hbm.1, s32[16,128]{1,0:T(8,128)} %bitcast.3, s32[1,2,512]{2,1,0:T(2,128)} %lists_hbm.1, f32[1,3,2,256]{3,2,1,0:T(2,128)} %bitcast.4), custom_call_target="tpu_custom_call" | custom-call | tf_op jit(solution)/shard_map/render/pallas_call | solution.py:736
  49.0 1.3 %copy.11 = f32[1,2,3,256]{3,1,2,0:T(2,128)} copy(f32[1,2,3,256]{3,1,2,0:T(2,128)} %bitcast.5) | data formatting | bytes 12288
  50.3 1.9 %copy.12 = f32[59,2048]{1,0:T(8,128)} copy(f32[59,2048]{1,0:T(8,128)} %get-tuple-element.9) | data formatting | bytes 966656

commit v4 on v3

--- a/solution.py
+++ b/solution.py
@@ -16,6 +16,8 @@
 ZC_ORDER = (8, 9, 7, 6, 10, 5, 11, 4, 12, 3, 13, 2, 14, 1, 15)
 VIEW_ORDER = (2, 1, 3)
 ENTRIES = 512
+CHUNKS = ENTRIES // LANES
+HALF = ENTRIES // 2
 TILES_DEV = 2
 PIXELS = 256
 ROWS = 59
@@ -316,137 +318,162 @@
             )
 
 
-def tile_body(
-    tile_ids, tile_len, targets, pictures, slot_grads,
-    feats, alpha, ratio, plane, weight, part, upper, lower, grads, masks, left, right,
-):
-    chunks = ENTRIES // LANES
-    half = ENTRIES // 2
-    for tile in range(TILES_DEV):
-        number = tile_ids[0, tile]
-        length = tile_len[0, tile]
+class Tile:
+    def __init__(self, tile, number, length, feats, grads, alpha, ratio, plane, weight, part):
+        self.tile, self.length, self.feats, self.grads = tile, length, feats, grads
+        self.alpha, self.ratio, self.plane, self.weight, self.part = alpha, ratio, plane, weight, part
+        self.whole = pl.ds(tile * ENTRIES, ENTRIES)
         left_x = (TILE_SIDE * lax.rem(number, TILE_COLS)).astype(F32) + 0.5
-        top_y = (TILE_SIDE * (number // TILE_COLS)).astype(F32) + 0.5
-        shape = (TILE_SIDE, LANES)
-        pixel_x = lax.broadcasted_iota(jnp.int32, shape, 0).astype(F32) + left_x
-        whole = pl.ds(tile * ENTRIES, ENTRIES)
-
-        def row_of(f, chunk):
-            return feats[pl.ds(f, 1), pl.ds(tile * ENTRIES + chunk * LANES, LANES)]
-
-        def feature(f, chunk):
-            return jnp.broadcast_to(row_of(f, chunk), (8, LANES))
-
-        def twice(rows):
-            return jnp.concatenate([rows, rows], axis=0)
-
-        def pixels_of(y):
-            return pl.ds(pl.multiple_of(y * TILE_SIDE, TILE_SIDE), TILE_SIDE)
-
-        for chunk in range(chunks):
+        self.top_y = (TILE_SIDE * (number // TILE_COLS)).astype(F32) + 0.5
+        self.pixel_x = lax.broadcasted_iota(jnp.int32, (TILE_SIDE, LANES), 0).astype(F32) + left_x
+
+    def row_of(self, f, chunk):
+        return self.feats[pl.ds(f, 1), pl.ds(self.tile * ENTRIES + chunk * LANES, LANES)]
+
+    def feature(self, f, chunk):
+        return jnp.broadcast_to(self.row_of(f, chunk), (8, LANES))
+
+    def each_row(self, body, carry):
+        def one_row(y, carry):
+            rows = pl.ds(pl.multiple_of(y * TILE_SIDE, TILE_SIDE), TILE_SIDE)
+            return body(y.astype(F32), rows, carry)
+
+        return lax.fori_loop(0, TILE_SIDE, one_row, carry, unroll=TILE_SIDE)
+
+    def opacities(self):
+        for chunk in range(CHUNKS):
             lanes = pl.ds(chunk * LANES, LANES)
             high, low = part_lanes(chunk)
             lane = lax.broadcasted_iota(jnp.int32, (8, LANES), 1) + chunk * LANES
-            log_opacity = jnp.where(lane < length, jnp.log2(feature(5, chunk)), -1e30)
-            delta_x = twice(feature(0, chunk)) - pixel_x
-            part_x = twice((-0.5 * LOG2_E) * feature(2, chunk)) * delta_x * delta_x + twice(log_opacity)
-            cross = twice(-LOG2_E * feature(3, chunk)) * delta_x
-            screen_y = feature(1, chunk) - top_y
-            conic_c = (-0.5 * LOG2_E) * feature(4, chunk)
-
-            def one_row(y, carry):
-                rows = pixels_of(y)
-                delta_y = screen_y - y.astype(F32)
+            log_opacity = jnp.where(lane < self.length, jnp.log2(self.feature(5, chunk)), -1e30)
+            delta_x = twice(self.feature(0, chunk)) - self.pixel_x
+            part_x = twice((-0.5 * LOG2_E) * self.feature(2, chunk)) * delta_x * delta_x + twice(log_opacity)
+            cross = twice(-LOG2_E * self.feature(3, chunk)) * delta_x
+            screen_y = self.feature(1, chunk) - self.top_y
+            conic_c = (-0.5 * LOG2_E) * self.feature(4, chunk)
+
+            def body(y, rows, carry):
+                delta_y = screen_y - y
                 part_y = conic_c * delta_y * delta_y
                 value = jnp.exp2(part_x + cross * twice(delta_y) + twice(part_y))
                 keep = jnp.log2(1.0 - value)
-                alpha[rows, lanes] = value
-                ratio[rows, lanes] = value * jnp.exp2(-keep)
-                part[rows, high], part[rows, low] = split2(keep)
+                self.alpha[rows, lanes] = value
+                self.ratio[rows, lanes] = value * jnp.exp2(-keep)
+                self.part[rows, high], self.part[rows, low] = split2(keep)
                 return carry
 
-            lax.fori_loop(0, TILE_SIDE, one_row, 0, unroll=TILE_SIDE)
-
-        plane[:, pl.ds(0, half)] = dot_nn(part[:, pl.ds(0, 512)], upper[pl.ds(512, 512), :])
-        plane[:, pl.ds(half, half)] = dot_nn(part[...], upper[...])
-
-        for chunk in range(chunks):
+            self.each_row(body, 0)
+
+    def log_transmittance(self, upper):
+        self.plane[:, pl.ds(0, HALF)] = dot_nn(self.part[:, pl.ds(0, 512)], upper[pl.ds(512, 512), :])
+        self.plane[:, pl.ds(HALF, HALF)] = dot_nn(self.part[...], upper[...])
+
+    def weights(self):
+        for chunk in range(CHUNKS):
             lanes = pl.ds(chunk * LANES, LANES)
             high, low = part_lanes(chunk)
 
-            def one_weight(y, carry):
-                rows = pixels_of(y)
-                value = jnp.exp2(plane[rows, lanes]) * alpha[rows, lanes]
-                weight[rows, lanes] = value
-                part[rows, high], part[rows, low] = split2(value)
+            def body(y, rows, carry):
+                value = jnp.exp2(self.plane[rows, lanes]) * self.alpha[rows, lanes]
+                self.weight[rows, lanes] = value
+                self.part[rows, high], self.part[rows, low] = split2(value)
                 return carry
 
-            lax.fori_loop(0, TILE_SIDE, one_weight, 0, unroll=TILE_SIDE)
-
-        colours = jnp.concatenate([feats[pl.ds(6, 3), whole], jnp.zeros((5, ENTRIES), F32)], axis=0)
+            self.each_row(body, 0)
+
+    def picture(self, targets, pictures):
+        colours = jnp.concatenate([self.feats[pl.ds(6, 3), self.whole], jnp.zeros((5, ENTRIES), F32)], axis=0)
         colour_hi = colours.astype(BF16).astype(F32)
         colour_lo = (colours - colour_hi).astype(BF16).astype(F32)
         both = jnp.concatenate([colour_hi, colour_lo], axis=0)
-        both = jnp.concatenate([both[:, :half], both[:, :half], both[:, half:], both[:, half:]], axis=1)
-        product = dot_nt(both.astype(BF16), part[...])
+        both = jnp.concatenate([both[:, :HALF], both[:, :HALF], both[:, HALF:], both[:, HALF:]], axis=1)
+        product = dot_nt(both.astype(BF16), self.part[...])
         picture = product[0:8] + product[8:16]
-        pictures[0, :, tile, :] = picture[0:3]
-        residual = picture - jnp.concatenate([targets[0, :, tile, :], jnp.zeros((5, PIXELS), F32)], axis=0)
+        pictures[0, :, self.tile, :] = picture[0:3]
+        residual = picture - jnp.concatenate([targets[0, :, self.tile, :], jnp.zeros((5, PIXELS), F32)], axis=0)
         residual_hi = residual.astype(BF16).astype(F32)
         residual_lo = (residual - residual_hi).astype(BF16).astype(F32)
         pair = jnp.concatenate([residual_hi, residual_lo], axis=0).astype(BF16)
-        product = dot_nn(pair, part[...])
+        product = dot_nn(pair, self.part[...])
         product = product[0:8] + product[8:16]
-        grads[pl.ds(6, 3), whole] = jnp.concatenate(
+        self.grads[pl.ds(6, 3), self.whole] = jnp.concatenate(
             [product[0:3, 0:256] + product[0:3, 256:512], product[0:3, 512:768] + product[0:3, 768:1024]], axis=1
         )
         stack = jnp.concatenate([residual_hi, residual_lo, residual_hi, jnp.zeros((104, PIXELS), F32)], axis=0)
         rows24 = jnp.concatenate([colour_hi, colour_hi, colour_lo, jnp.zeros((104, ENTRIES), F32)], axis=0)
-        plane[...] = dot_nn(jnp.transpose(stack).astype(BF16), rows24.astype(BF16))
-
-        for chunk in range(chunks):
+        self.plane[...] = dot_nn(jnp.transpose(stack).astype(BF16), rows24.astype(BF16))
+
+    def shares(self):
+        for chunk in range(CHUNKS):
             lanes = pl.ds(chunk * LANES, LANES)
             high, low = part_lanes(chunk)
 
-            def one_share(y, carry):
-                rows = pixels_of(y)
-                value = plane[rows, lanes] * weight[rows, lanes]
-                weight[rows, lanes] = value
-                part[rows, high], part[rows, low] = split2(value)
+            def body(y, rows, carry):
+                value = self.plane[rows, lanes] * self.weight[rows, lanes]
+                self.weight[rows, lanes] = value
+                self.part[rows, high], self.part[rows, low] = split2(value)
                 return carry
 
-            lax.fori_loop(0, TILE_SIDE, one_share, 0, unroll=TILE_SIDE)
-
-        plane[:, pl.ds(0, half)] = dot_nn(part[...], lower[...])
-        plane[:, pl.ds(half, half)] = dot_nn(part[:, pl.ds(512, 512)], lower[pl.ds(0, 512), :])
-
-        for chunk in range(chunks):
+            self.each_row(body, 0)
+
+    def later_shares(self, lower):
+        self.plane[:, pl.ds(0, HALF)] = dot_nn(self.part[...], lower[...])
+        self.plane[:, pl.ds(HALF, HALF)] = dot_nn(self.part[:, pl.ds(512, 512)], lower[pl.ds(0, 512), :])
+
+    def sums(self):
+        for chunk in range(CHUNKS):
             lanes = pl.ds(chunk * LANES, LANES)
-            screen_y = feature(1, chunk) - top_y
-
-            def one_sum(y, carry):
-                rows = pixels_of(y)
+            screen_y = self.feature(1, chunk) - self.top_y
+
+            def body(y, rows, carry):
                 sum_0, sum_1, sum_2 = carry
-                delta_y = twice(screen_y - y.astype(F32))
-                grad = weight[rows, lanes] - plane[rows, lanes] * ratio[rows, lanes]
+                delta_y = twice(screen_y - y)
+                grad = self.weight[rows, lanes] - self.plane[rows, lanes] * self.ratio[rows, lanes]
                 slope = grad * delta_y
                 return sum_0 + grad, sum_1 + slope, sum_2 + slope * delta_y
 
-            zero = jnp.zeros(shape, F32)
-            sum_0, sum_1, sum_2 = lax.fori_loop(0, TILE_SIDE, one_sum, (zero, zero, zero), unroll=TILE_SIDE)
-            delta_x = twice(feature(0, chunk)) - pixel_x
+            zero = jnp.zeros((TILE_SIDE, LANES), F32)
+            sum_0, sum_1, sum_2 = self.each_row(body, (zero, zero, zero))
+            delta_x = twice(self.feature(0, chunk)) - self.pixel_x
             over = lambda rows: jnp.sum(rows, axis=0, keepdims=True)
             first_x = over(delta_x * sum_0)
             first_y = over(sum_1)
-            out = pl.ds(tile * ENTRIES + chunk * LANES, LANES)
-            grads[pl.ds(0, 1), out] = -row_of(2, chunk) * first_x - row_of(3, chunk) * first_y
-            grads[pl.ds(1, 1), out] = -row_of(4, chunk) * first_y - row_of(3, chunk) * first_x
+            out = pl.ds(self.tile * ENTRIES + chunk * LANES, LANES)
+            grads, row_of = self.grads, lambda f: self.row_of(f, chunk)
+            grads[pl.ds(0, 1), out] = -row_of(2) * first_x - row_of(3) * first_y
+            grads[pl.ds(1, 1), out] = -row_of(4) * first_y - row_of(3) * first_x
             grads[pl.ds(2, 1), out] = -0.5 * over(delta_x * delta_x * sum_0)
             grads[pl.ds(3, 1), out] = -over(delta_x * sum_1)
             grads[pl.ds(4, 1), out] = -0.5 * over(sum_2)
             grads[pl.ds(5, 1), out] = over(sum_0)
 
-    for n in range(TILES_DEV * chunks):
+
+def twice(rows):
+    return jnp.concatenate([rows, rows], axis=0)
+
+
+def tile_body(
+    tile_ids, tile_len, targets, pictures, slot_grads, feats, planes, parts, upper, lower, grads, masks, left, right
+):
+    first, second = [
+        Tile(
+            tile, tile_ids[0, tile], tile_len[0, tile], feats, grads,
+            *[planes.at[4 * tile + i] for i in range(4)], parts.at[tile],
+        )
+        for tile in range(TILES_DEV)
+    ]
+    first.opacities()
+    second.opacities()
+    for tile in (first, second):
+        tile.log_transmittance(upper)
+        tile.weights()
+    for tile in (first, second):
+        tile.picture(targets, pictures)
+        tile.shares()
+    for tile in (first, second):
+        tile.later_shares(lower)
+        tile.sums()
+    for n in range(TILES_DEV * CHUNKS):
         spread(grads[:, pl.ds(n * LANES, LANES)], 16, masks, n * 256, left, n * LANES)
     total = dot_nt(left[...], right[...])
     for zc in range(16):
@@ -460,31 +487,30 @@
 
 def render_kernel(
     camera, tile_ids, tile_len, params_hbm, slots_hbm, lists_hbm, targets_hbm,
-    pictures_hbm, gradient_hbm,
-    params, packed, dense, lists, targets, pictures, slots, cams,
+    pictures, gradient,
+    params, packed, dense, lists, targets, slots, cams,
     table, outgoing, landed, staged, received, slot_grads, landed_back, staged_back, returned, every,
-    feats, alpha, ratio, plane, weight, part, upper, lower, grads, masks, left, right,
+    feats, planes, parts, upper, lower, grads, masks, left, right,
     view_masks, view_left, view_right, view_grads, saved, shape_rows, totals, colour,
-    load_sem, store_sem, send_y, recv_y, send_zc, recv_zc, send_zc2, recv_zc2, send_y2, recv_y2,
+    load_sem, send_y, recv_y, send_zc, recv_zc, send_zc2, recv_zc2, send_y2, recv_y2,
     send_slots, recv_slots, send_cams, recv_cams, send_view, recv_view,
 ):
     cell, view = lax.axis_index("cell"), lax.axis_index("view")
     my_y, my_zc = cell // ZC_DEVS, lax.rem(cell, ZC_DEVS)
     barrier, greetings = greet(my_y, my_zc, view)
 
+    pieces = [(first, min(8, ROWS - first)) for first in range(0, ROWS, 8)]
     loads = [
-        pltpu.make_async_copy(source, target, load_sem.at[i])
+        pltpu.make_async_copy(params_hbm.at[pl.ds(*piece)], params.at[pl.ds(*piece)], load_sem.at[i])
+        for i, piece in enumerate(pieces)
+    ]
+    side_loads = [
+        pltpu.make_async_copy(source, target, load_sem.at[8 + i])
         for i, (source, target) in enumerate(
-            (
-                (params_hbm.at[pl.ds(0, 16)], params.at[pl.ds(0, 16)]),
-                (params_hbm.at[pl.ds(16, ROWS - 16)], params.at[pl.ds(16, ROWS - 16)]),
-                (slots_hbm, slots.at[0]),
-                (lists_hbm, lists),
-                (targets_hbm, targets),
-            )
+            ((slots_hbm, slots.at[0]), (lists_hbm, lists), (targets_hbm, targets))
         )
     ]
-    for load in loads:
+    for load in loads + side_loads:
         load.start()
     table[...] = jnp.zeros_like(table)
     feats[...] = jnp.zeros_like(feats)
@@ -492,24 +518,19 @@
     shift_row = lax.broadcasted_iota(jnp.int32, (8, LANES), 0)
     cams[0] = jnp.where(shift_row == 0, camera[0, 0], jnp.where(shift_row == 1, camera[0, 1], camera[0, 2]))
 
-    def unpack(first, last):
-        for group in range(first, last, 8):
-            size = min(8, last - group)
-            for chunk in range(16):
-                packed[pl.ds(group * 16 + chunk * 8, size), :] = params[
-                    pl.ds(group, size), pl.ds(chunk * LANES, LANES)
-                ]
-        for row in range(first, last):
+    def unpack(group, size):
+        for chunk in range(16):
+            packed[pl.ds(group * 16 + chunk * 8, size), :] = params[pl.ds(group, size), pl.ds(chunk * LANES, LANES)]
+        for row in range(group, group + size):
             for half in range(2):
                 dense[2 * row + half] = packed[pl.ds((row // 8) * 128 + half * 8 + row % 8, 8, stride=16), :]
 
     def loader(half):
         return lambda row: dense[2 * row + half]
 
-    loads[0].wait()
-    unpack(0, 16)
-    loads[1].wait()
-    unpack(16, ROWS)
+    for load, piece in zip(loads, pieces):
+        load.wait()
+        unpack(*piece)
 
     for half in range(2):
         load = loader(half)
@@ -520,7 +541,7 @@
         for f, feature in enumerate(features):
             table[pl.ds(half * 16 + f, 8, stride=32), :] = feature
 
-    loads[2].wait()
+    side_loads[0].wait()
     pl.semaphore_wait(barrier, greetings)
     y_sends = {}
     for k in Y_ORDER + (0,):
@@ -543,8 +564,8 @@
         side_sends.append(remote(cams.at[0], cams.at[k], send_cams.at[k - 1], recv_cams.at[k - 1], peer))
 
     fill_triangles(upper, lower)
-    loads[3].wait()
-    loads[4].wait()
+    side_loads[1].wait()
+    side_loads[2].wait()
     for tile in range(TILES_DEV):
         for chunk in range(ENTRIES // LANES):
             n = tile * (ENTRIES // LANES) + chunk
@@ -560,8 +581,7 @@
                 fill_masks(index >> 8, 8, view_masks, (k * 16 + n) * 128)
                 view_right[k, :, pl.ds(n * LANES, LANES)] = hot_rows(index & 255, 256)
 
-    view_factors(0)
-    for k in Y_ORDER:
+    for k in Y_ORDER[::-1]:
         y_sends[k].wait()
 
     def to_zc(j, half, rows):
@@ -576,9 +596,11 @@
         )
     received[my_zc] = staged[my_zc]
 
+    view_factors(0)
     for copy in side_sends:
         copy.wait()
-    for k in range(1, VIEW_DEVS):
+
+    def view_forward(k):
         for half in range(2):
             shift = [jnp.broadcast_to(cams[k, pl.ds(i, 1), :], (8, LANES)) for i in range(3)]
             matrix = [shape_rows[half * SHAPE_ROWS + i] for i in range(9)]
@@ -605,10 +627,8 @@
 
     tile_body(
         tile_ids, tile_len, targets, pictures, slot_grads,
-        feats, alpha, ratio, plane, weight, part, upper, lower, grads, masks, left, right,
+        feats, planes, parts, upper, lower, grads, masks, left, right,
     )
-    store_pictures = pltpu.make_async_copy(pictures, pictures_hbm, store_sem.at[0])
-    store_pictures.start()
 
     for k in ZC_ORDER:
         peer, device_id = zc_peer(my_y, my_zc, k)
@@ -616,6 +636,8 @@
             slot_grads.at[peer], landed_back.at[my_zc], send_zc2.at[k - 1], recv_zc2.at[k - 1], device_id
         )
     landed_back[my_zc] = slot_grads[my_zc]
+    view_forward(1)
+    view_forward(2)
     for k in ZC_ORDER[::-1]:
         zc_sends[k].wait()
 
@@ -667,17 +689,22 @@
                 send_view.at[k - 1, p], recv_view.at[k - 1, p], view_peer(view, k),
             )
         add_left(0, p, lambda half, row, size, y=y: returned[2 * y + half, pl.ds(row, size), :])
+        if p == 0:
+            view_forward(3)
     scatter(0, pl.ds(0, G_DEV), True)
     pull(0)
     for p in range(8):
         for k in (1, 3, 2):
             view_sends[k, p].wait()
-            add_left(k, p, lambda half, row, size: every[k, 2 * p + half, pl.ds(row, size), :])
-            if p == 6:
+            if p < 7:
+                add_left(k, p, lambda half, row, size: every[k, 2 * p + half, pl.ds(row, size), :])
+        if p == 6:
+            for k in (1, 3, 2):
                 scatter(k, pl.ds(0, LAST), True)
-            if p == 7:
-                scatter(k, pl.ds(LAST, 256), False)
-                pull(k)
+    for k in (1, 3, 2):
+        add_left(k, 7, lambda half, row, size: every[k, 14 + half, pl.ds(row, size), :])
+        scatter(k, pl.ds(LAST, 256), False)
+        pull(k)
 
     def put(row, half, value):
         packed[pl.ds((row // 8) * 128 + half * 8 + row % 8, 8, stride=16), :] = value
@@ -686,7 +713,7 @@
         for group in range(first, last, 8):
             size = min(8, last - group)
             for chunk in range(16):
-                params[pl.ds(group, size), pl.ds(chunk * LANES, LANES)] = packed[
+                gradient[pl.ds(group, size), pl.ds(chunk * LANES, LANES)] = packed[
                     pl.ds(group * 16 + chunk * 8, size), :
                 ]
 
@@ -699,10 +726,6 @@
                 terms = [kept(k, 22 + j) * parts[k] for k in range(VIEW_DEVS)]
                 put(12 + 16 * channel + j, half, terms[0] + terms[1] + terms[2] + terms[3])
     pack(16, ROWS)
-    store_tail = pltpu.make_async_copy(
-        params.at[pl.ds(16, ROWS - 16)], gradient_hbm.at[pl.ds(16, ROWS - 16)], store_sem.at[1]
-    )
-    store_tail.start()
     for half in range(2):
         total = [totals[half * 13 + i] for i in range(13)]
         shape = [shape_rows[half * SHAPE_ROWS + i] for i in range(SHAPE_ROWS)]
@@ -717,17 +740,11 @@
             put(6 + i, half, inv_norm * (g_unit[i] - unit_q[i] * along))
         put(10, half, total[12] * (1.0 / (1.0 + jnp.exp(dense[20 + half]))))
     pack(0, 16)
-    store_head = pltpu.make_async_copy(params.at[pl.ds(0, 16)], gradient_hbm.at[pl.ds(0, 16)], store_sem.at[2])
-    store_head.start()
-    store_pictures.wait()
-    store_tail.wait()
-    store_head.wait()
 
 
 def render_call(camera, tile_ids, tile_len, params, slots, lists, targets):
     smem = pl.BlockSpec(memory_space=pltpu.SMEM)
     anywhere = pl.BlockSpec(memory_space=pl.ANY)
-    plane = pltpu.VMEM((PIXELS, ENTRIES), F32)
     blocks = pltpu.VMEM((16, FEATS, LANES), F32)
     tile = (8, LANES)
     y_sems = [pltpu.SemaphoreType.DMA((Y_DEVS - 1,))] * 2
@@ -736,17 +753,16 @@
     return pl.pallas_call(
         render_kernel,
         out_shape=(
-            jax.ShapeDtypeStruct(targets.shape, F32),
-            jax.ShapeDtypeStruct(params.shape, F32),
+            pltpu.VMEM(targets.shape, F32),
+            pltpu.VMEM(params.shape, F32),
         ),
         in_specs=[smem, smem, smem, anywhere, anywhere, anywhere, anywhere],
-        out_specs=(anywhere, anywhere),
+        out_specs=(pl.BlockSpec(memory_space=pltpu.VMEM), pl.BlockSpec(memory_space=pltpu.VMEM)),
         scratch_shapes=[
             pltpu.VMEM((ROWS, G_DEV), F32),
             pltpu.VMEM((64 * 16, LANES), F32),
             pltpu.VMEM((2 * ROWS,) + tile, F32),
             pltpu.VMEM(lists.shape, jnp.int32),
-            pltpu.VMEM(targets.shape, F32),
             pltpu.VMEM(targets.shape, F32),
             pltpu.VMEM((VIEW_DEVS, 16, LANES), jnp.int32),
             pltpu.VMEM((VIEW_DEVS,) + tile, F32),
@@ -756,11 +772,8 @@
         + [
             pltpu.VMEM((VIEW_DEVS, 16, FEATS, LANES), F32),
             pltpu.VMEM((16, TILES_DEV * ENTRIES), F32),
-            plane,
-            plane,
-            plane,
-            plane,
-            pltpu.VMEM((PIXELS, 2 * ENTRIES), BF16),
+            pltpu.VMEM((4 * TILES_DEV, PIXELS, ENTRIES), F32),
+            pltpu.VMEM((TILES_DEV, PIXELS, 2 * ENTRIES), BF16),
             pltpu.VMEM((1024, 256), BF16),
             pltpu.VMEM((1024, 256), BF16),
             pltpu.VMEM((16, TILES_DEV * ENTRIES), F32),
@@ -775,16 +788,45 @@
             pltpu.VMEM((2 * SHAPE_ROWS,) + tile, F32),
             pltpu.VMEM((2 * 13,) + tile, F32),
             pltpu.VMEM((VIEW_DEVS * 2 * 3,) + tile, F32),
-            pltpu.SemaphoreType.DMA((5,)),
-            pltpu.SemaphoreType.DMA((3,)),
+            pltpu.SemaphoreType.DMA((11,)),
         ]
         + y_sems + zc_sems + zc_sems + y_sems + view_sems + view_sems
         + [pltpu.SemaphoreType.DMA((VIEW_DEVS - 1, 8))] * 2,
         compiler_params=pltpu.CompilerParams(
-            collective_id=0, has_side_effects=True, vmem_limit_bytes=58 * 2**20
+            collective_id=0, has_side_effects=True, vmem_limit_bytes=40 * 2**20
         ),
         name="render",
-    )(camera, tile_ids, tile_len, params, slots, lists, targets)
+    )(
+        *[
+            pltpu.with_memory_space_constraint(operand, pltpu.HBM)
+            for operand in (camera, tile_ids, tile_len, params, slots, lists, targets)
+        ]
+    )
+
+
+def store_kernel(pictures, gradient, pictures_hbm, gradient_hbm, sems):
+    copies = [pltpu.make_async_copy(pictures, pictures_hbm, sems.at[0])]
+    for i, (first, size) in enumerate(((0, 16), (16, 16), (32, 16), (48, ROWS - 48))):
+        rows = pl.ds(first, size)
+        copies.append(pltpu.make_async_copy(gradient.at[rows], gradient_hbm.at[rows], sems.at[1 + i]))
+    for copy in copies:
+        copy.start()
+    for copy in copies:
+        copy.wait()
+
+
+def store_call(pictures, gradient):
+    vmem = pl.BlockSpec(memory_space=pltpu.VMEM)
+    anywhere = pl.BlockSpec(memory_space=pl.ANY)
+    return pl.pallas_call(
+        store_kernel,
+        out_shape=(jax.ShapeDtypeStruct(pictures.shape, F32), jax.ShapeDtypeStruct(gradient.shape, F32)),
+        in_specs=[vmem, vmem],
+        out_specs=(anywhere, anywhere),
+        scratch_shapes=[pltpu.SemaphoreType.DMA((5,))],
+        compiler_params=pltpu.CompilerParams(vmem_limit_bytes=8 * 2**20),
+        name="store",
+    )(pictures, gradient)
 
 
 def local(params, cameras, targets, tile_ids, send_slots, tile_lists, tile_len):
@@ -792,6 +834,7 @@
         cameras, tile_ids, tile_len, params, send_slots.reshape(16, LANES), tile_lists,
         jnp.transpose(targets, (0, 2, 1, 3)),
     )
+    pictures, gradient = store_call(pictures, gradient)
     return jnp.transpose(pictures, (0, 2, 1, 3)), gradient
 
 

time: 52.4 us -> 48.1 us (0.918)
  local copies, waits for them, and re-layouts: 3.16 us -> 0 us
  Pallas kernels: 48.4 us -> 47.3 us
    unnamed x2 -> x0, local copies, waits for them, and re-layouts: 3.16 us -> none
    pallas_call x1 -> x2, Pallas kernels: 48.4 us -> 47.3 us  [the longest x1 46.5 us: render_call(): pl.pallas_call(render_kernel, out_shape=(pltpu.VMEM(targets.shape, F32),...]
where the time goes in v4:
time: 48.1 us; the launch traced here: 48 us
  Pallas kernels  47.3 us (98%)
  between operations  0.64 us (1%)
    pallas_call x1, Pallas kernels, render_call(): pl.pallas_call(render_kernel, out_shape=(pltpu.VMEM(targets.shape, F32),...  46.5 us

profile of v4, /device:TPU:1, one launch (start us, length us, event | category | flops | bytes accessed | tf_op | source)
XLA Modules:
  0.0 48.0 jit_solution(4499469421757800553)
XLA Ops:
  0.6 46.5 %render.1 = (f32[1,3,2,256]{3,2,1,0:T(2,128)S(1)}, f32[59,2048]{1,0:T(8,128)S(1)}) custom-call(f32[1,3]{1,0:T(1,128)} %camera.1, s32[1,2]{1,0:T(1,128)} %tile_ids.1, s32[1,2]{1,0:T(1,128)} %tile_len.1, f32[59,2048]{1,0:T(8,128)} %params_hbm.1, s32[16,128]{1,0:T(8,128)} %bitcast.3, s32[1,2,512]{2,1,0:T(2,128)} %lists_hbm.1, f32[1,3,2,256]{3,2,1,0:T(2,128)} %bitcast.4), custom_call_target="tpu_custom_call" | custom-call | tf_op jit(solution)/shard_map/render/pallas_call | solution.py:753
  47.1 0.8 %store.1 = (f32[1,3,2,256]{3,2,1,0:T(2,128)}, f32[59,2048]{1,0:T(8,128)}) custom-call(f32[1,3,2,256]{3,2,1,0:T(2,128)S(1)} %get-tuple-element.6.pictures, f32[59,2048]{1,0:T(8,128)S(1)} %get-tuple-element.7.gradient), custom_call_target="tpu_custom_call" | custom-call | tf_op jit(solution)/shard_map/store/pallas_call | solution.py:821

commit v5 on v4

--- a/solution.py
+++ b/solution.py
@@ -15,6 +15,7 @@
 Y_ORDER = (4, 3, 5, 2, 6, 1, 7)
 ZC_ORDER = (8, 9, 7, 6, 10, 5, 11, 4, 12, 3, 13, 2, 14, 1, 15)
 VIEW_ORDER = (2, 1, 3)
+FAR_Y = 4
 ENTRIES = 512
 CHUNKS = ENTRIES // LANES
 HALF = ENTRIES // 2
@@ -146,23 +147,27 @@
 SHAPE_ROWS = 17
 
 
-def keep_view(load, shift, matrix, saved, base):
+def keep_geometry(load, shift, matrix, saved, base):
     pos = [load(i) - shift[i] for i in range(3)]
     inv_z, jac, screen_x, screen_y, jac_x, jac_y, row_u, row_v, cov_a, cov_b, cov_c, inv_det = geometry(pos, matrix)
     unit, inv_len = direction(pos)
-    basis = harmonics(*unit)
-    raw = [raw_colour(load, channel, basis) for channel in range(3)]
-    gates = [jnp.where(value > 0.0, 1.0, jnp.where(value < 0.0, 0.0, 0.5)) for value in raw]
     values = [pos[0], pos[1], inv_z, jac, screen_x, screen_y, jac_x, jac_y]
-    values += row_u + row_v + [cov_a, cov_b, cov_c, inv_det] + unit + [inv_len] + basis + gates
+    values += row_u + row_v + [cov_a, cov_b, cov_c, inv_det] + unit + [inv_len] + harmonics(*unit)
     for i, value in enumerate(values):
         saved[base + i] = value
-    features = [screen_x, screen_y, cov_c * inv_det, -cov_b * inv_det, cov_a * inv_det]
-    features.append(1.0 / (1.0 + jnp.exp(-load(10))))
-    return features + [jnp.maximum(value, 0.0) for value in raw]
-
-
-def pull_view(load, slot, matrix, saved, base, totals, total_base, first, colour, colour_base):
+    opacity = 1.0 / (1.0 + jnp.exp(-load(10)))
+    return [screen_x, screen_y, cov_c * inv_det, -cov_b * inv_det, cov_a * inv_det, opacity]
+
+
+def keep_colours(load, saved, base):
+    basis = [saved[base + 22 + j] for j in range(15)]
+    raw = [raw_colour(load, channel, basis) for channel in range(3)]
+    for channel, value in enumerate(raw):
+        saved[base + 37 + channel] = jnp.where(value > 0.0, 1.0, jnp.where(value < 0.0, 0.0, 0.5))
+    return [jnp.maximum(value, 0.0) for value in raw]
+
+
+def pull_view(load, slot, matrix, saved, base):
     kept = lambda i: saved[base + i]
     inv_z, jac, screen_x, screen_y, jac_x, jac_y = [kept(2 + i) for i in range(6)]
     row_u, row_v = [kept(8 + i) for i in range(3)], [kept(11 + i) for i in range(3)]
@@ -176,9 +181,9 @@
     g_v = [d_c * row_v[j] + d_b * row_u[j] for j in range(3)]
     g_matrix = [jac * g_u[j] for j in range(3)] + [jac * g_v[j] for j in range(3)]
     g_matrix += [jac_x * g_u[j] + jac_y * g_v[j] for j in range(3)]
-    g_jac = sum(g_u[j] * matrix[j] + g_v[j] * matrix[3 + j] for j in range(1, 3)) + (
-        g_u[0] * matrix[0] + g_v[0] * matrix[3]
-    )
+    g_jac = g_u[0] * matrix[0] + g_v[0] * matrix[3]
+    for j in (1, 2):
+        g_jac = g_jac + (g_u[j] * matrix[j] + g_v[j] * matrix[3 + j])
     g_jac_x = g_u[0] * matrix[6] + g_u[1] * matrix[7] + g_u[2] * matrix[8]
     g_jac_y = g_v[0] * matrix[6] + g_v[1] * matrix[7] + g_v[2] * matrix[8]
     g_sx = slot(0) - inv_z * g_jac_x
@@ -186,20 +191,18 @@
     g_inv = focal_length * (g_jac + kept(0) * g_sx + kept(1) * g_sy) - screen_x * g_jac_x - screen_y * g_jac_y
     g_pos = [jac * g_sx, jac * g_sy, -inv_z * inv_z * g_inv]
 
-    g_basis = None
-    for channel in range(3):
-        g_colour = slot(6 + channel) * kept(37 + channel)
-        colour[colour_base + channel] = g_colour
-        terms = [load(12 + 16 * channel + j) * g_colour for j in range(15)]
-        g_basis = terms if g_basis is None else [a + b for a, b in zip(g_basis, terms)]
+    g_colours = [slot(6 + channel) * kept(37 + channel) for channel in range(3)]
+    g_basis = []
+    for j in range(15):
+        terms = [load(12 + 16 * channel + j) * g_colours[channel] for channel in range(3)]
+        g_basis.append(terms[0] + terms[1] + terms[2])
     unit, inv_len = [kept(18 + i) for i in range(3)], kept(21)
     _, pull = jax.vjp(harmonics, *unit)
     g_unit = pull(g_basis)
     along = unit[0] * g_unit[0] + unit[1] * g_unit[1] + unit[2] * g_unit[2]
     for i in range(3):
         g_pos[i] = g_pos[i] + inv_len * (g_unit[i] - unit[i] * along)
-    for i, value in enumerate(g_pos + g_matrix + [slot(5)]):
-        totals[total_base + i] = value if first else totals[total_base + i] + value
+    return g_pos + g_matrix + [slot(5)], g_colours
 
 
 def lane_gather(source, index):
@@ -260,11 +263,16 @@
     return {"view": lax.rem(view + k, VIEW_DEVS)}
 
 
+def far_view_peer(my_y, my_zc, view, k):
+    return {**y_peer(my_y, my_zc, FAR_Y)[1], **view_peer(view, k)}
+
+
 def greet(my_y, my_zc, view):
     barrier = pltpu.get_barrier_semaphore()
     peers = [y_peer(my_y, my_zc, k)[1] for k in Y_ORDER]
     peers += [zc_peer(my_y, my_zc, k)[1] for k in ZC_ORDER]
     peers += [view_peer(view, k) for k in VIEW_ORDER]
+    peers += [far_view_peer(my_y, my_zc, view, k) for k in VIEW_ORDER]
     for peer in peers:
         pl.semaphore_signal(barrier, inc=1, device_id=peer, device_id_type=pl.DeviceIdType.MESH)
     return barrier, len(peers)
@@ -323,8 +331,8 @@
         self.tile, self.length, self.feats, self.grads = tile, length, feats, grads
         self.alpha, self.ratio, self.plane, self.weight, self.part = alpha, ratio, plane, weight, part
         self.whole = pl.ds(tile * ENTRIES, ENTRIES)
-        left_x = (TILE_SIDE * lax.rem(number, TILE_COLS)).astype(F32) + 0.5
-        self.top_y = (TILE_SIDE * (number // TILE_COLS)).astype(F32) + 0.5
+        left_x = twice((TILE_SIDE * (number & (TILE_COLS - 1))).astype(F32) + 0.5)
+        self.top_y = (TILE_SIDE * (number >> 5)).astype(F32) + 0.5
         self.pixel_x = lax.broadcasted_iota(jnp.int32, (TILE_SIDE, LANES), 0).astype(F32) + left_x
 
     def row_of(self, f, chunk):
@@ -448,6 +456,10 @@
             grads[pl.ds(5, 1), out] = over(sum_0)
 
 
+def wide(row, i):
+    return jnp.broadcast_to(row[:, pl.ds(i, 1)], (8, LANES))
+
+
 def twice(rows):
     return jnp.concatenate([rows, rows], axis=0)
 
@@ -457,7 +469,7 @@
 ):
     first, second = [
         Tile(
-            tile, tile_ids[0, tile], tile_len[0, tile], feats, grads,
+            tile, wide(tile_ids, tile), wide(tile_len, tile), feats, grads,
             *[planes.at[4 * tile + i] for i in range(4)], parts.at[tile],
         )
         for tile in range(TILES_DEV)
@@ -486,12 +498,11 @@
 
 
 def render_kernel(
-    camera, tile_ids, tile_len, params_hbm, slots_hbm, lists_hbm, targets_hbm,
-    pictures, gradient,
-    params, packed, dense, lists, targets, slots, cams,
+    camera_hbm, ids_hbm, len_hbm, params_hbm, slots_hbm, lists_hbm, targets_hbm,
+    pictures, view_grads, dense, saved, shape_rows, totals, colour,
+    camera, tile_ids, tile_len, params, packed, lists, targets, slots, cams,
     table, outgoing, landed, staged, received, slot_grads, landed_back, staged_back, returned, every,
-    feats, planes, parts, upper, lower, grads, masks, left, right,
-    view_masks, view_left, view_right, view_grads, saved, shape_rows, totals, colour,
+    feats, planes, parts, upper, lower, grads, masks, left, right, view_masks, view_left, view_right,
     load_sem, send_y, recv_y, send_zc, recv_zc, send_zc2, recv_zc2, send_y2, recv_y2,
     send_slots, recv_slots, send_cams, recv_cams, send_view, recv_view,
 ):
@@ -507,16 +518,21 @@
     side_loads = [
         pltpu.make_async_copy(source, target, load_sem.at[8 + i])
         for i, (source, target) in enumerate(
-            ((slots_hbm, slots.at[0]), (lists_hbm, lists), (targets_hbm, targets))
+            (
+                (camera_hbm, camera),
+                (slots_hbm, slots.at[0]),
+                (lists_hbm, lists),
+                (targets_hbm, targets),
+                (ids_hbm, tile_ids),
+                (len_hbm, tile_len),
+            )
         )
     ]
-    for load in loads + side_loads:
+    for load in loads[:2] + side_loads[:2] + loads[2:] + side_loads[2:]:
         load.start()
     table[...] = jnp.zeros_like(table)
     feats[...] = jnp.zeros_like(feats)
     grads[...] = jnp.zeros_like(grads)
-    shift_row = lax.broadcasted_iota(jnp.int32, (8, LANES), 0)
-    cams[0] = jnp.where(shift_row == 0, camera[0, 0], jnp.where(shift_row == 1, camera[0, 1], camera[0, 2]))
 
     def unpack(group, size):
         for chunk in range(16):
@@ -528,20 +544,31 @@
     def loader(half):
         return lambda row: dense[2 * row + half]
 
-    for load, piece in zip(loads, pieces):
-        load.wait()
-        unpack(*piece)
-
+    def load_pieces(first, last):
+        for load, piece in list(zip(loads, pieces))[first:last]:
+            load.wait()
+            unpack(*piece)
+
+    def put_features(first, features, half):
+        for f, feature in enumerate(features):
+            table[pl.ds(half * 16 + first + f, 8, stride=32), :] = feature
+
+    side_loads[0].wait()
+    shift = [wide(camera, i) for i in range(3)]
+    shift_row = lax.broadcasted_iota(jnp.int32, (8, LANES), 0)
+    cams[0] = jnp.where(shift_row == 0, shift[0], jnp.where(shift_row == 1, shift[1], shift[2]))
+    load_pieces(0, 2)
     for half in range(2):
         load = loader(half)
         matrix, scales, unit_q, inv_norm = shape_matrix([load(3 + i) for i in range(3)], [load(6 + i) for i in range(4)])
         for i, value in enumerate(matrix + scales + unit_q + [inv_norm]):
             shape_rows[half * SHAPE_ROWS + i] = value
-        features = keep_view(load, [camera[0, i] for i in range(3)], matrix, saved, half * KEPT)
-        for f, feature in enumerate(features):
-            table[pl.ds(half * 16 + f, 8, stride=32), :] = feature
-
-    side_loads[0].wait()
+        put_features(0, keep_geometry(load, shift, matrix, saved, half * KEPT), half)
+    load_pieces(2, 8)
+    for half in range(2):
+        put_features(6, keep_colours(loader(half), saved, half * KEPT), half)
+
+    side_loads[1].wait()
     pl.semaphore_wait(barrier, greetings)
     y_sends = {}
     for k in Y_ORDER + (0,):
@@ -564,8 +591,8 @@
         side_sends.append(remote(cams.at[0], cams.at[k], send_cams.at[k - 1], recv_cams.at[k - 1], peer))
 
     fill_triangles(upper, lower)
-    side_loads[1].wait()
-    side_loads[2].wait()
+    for load in side_loads[2:]:
+        load.wait()
     for tile in range(TILES_DEV):
         for chunk in range(ENTRIES // LANES):
             n = tile * (ENTRIES // LANES) + chunk
@@ -604,7 +631,8 @@
         for half in range(2):
             shift = [jnp.broadcast_to(cams[k, pl.ds(i, 1), :], (8, LANES)) for i in range(3)]
             matrix = [shape_rows[half * SHAPE_ROWS + i] for i in range(9)]
-            keep_view(loader(half), shift, matrix, saved, (2 * k + half) * KEPT)
+            keep_geometry(loader(half), shift, matrix, saved, (2 * k + half) * KEPT)
+            keep_colours(loader(half), saved, (2 * k + half) * KEPT)
         view_factors(k)
 
     places = [entry_slot(lists, n // 4, n % 4) for n in range(8)]
@@ -645,12 +673,20 @@
         staged_back[2 * j + half] = rows
 
     regroup(lambda i, half: landed_back[8 * half + i], to_y)
+    view_sends = {}
     for k in Y_ORDER:
         peer, device_id = y_peer(my_y, my_zc, k)
         y_sends[k] = remote(
             staged_back.at[pl.ds(2 * peer, 2)], returned.at[pl.ds(2 * my_y, 2)],
             send_y2.at[k - 1], recv_y2.at[k - 1], device_id,
         )
+        if k == FAR_Y:
+            for other in VIEW_ORDER:
+                view_sends[other, 7] = remote(
+                    staged_back.at[pl.ds(2 * peer, 2)], every.at[other, pl.ds(14, 2)],
+                    send_view.at[other - 1, 7], recv_view.at[other - 1, 7],
+                    far_view_peer(my_y, my_zc, view, other),
+                )
     returned[pl.ds(2 * my_y, 2)] = staged_back[pl.ds(2 * my_y, 2)]
 
     def add_left(k, p, block):
@@ -669,21 +705,11 @@
             value = product[0:128, lanes] + product[128:256, lanes]
             view_grads[rows, :] = value if first else view_grads[rows, :] + value
 
-    def pull(k):
-        for half in range(2):
-            matrix = [shape_rows[half * SHAPE_ROWS + i] for i in range(9)]
-            slot = lambda f: view_grads[pl.ds((2 * k + half) * 128 + f, 8, stride=16), :]
-            pull_view(
-                loader(half), slot, matrix, saved, (2 * k + half) * KEPT, totals, half * 13, k == 0,
-                colour, (2 * k + half) * 3,
-            )
-
-    view_sends = {}
     for p, step in enumerate(Y_ARRIVAL):
         if step:
             y_sends[step].wait()
         y = lax.rem(my_y + Y_DEVS - step, Y_DEVS)
-        for k in VIEW_ORDER:
+        for k in VIEW_ORDER if step != FAR_Y else ():
             view_sends[k, p] = remote(
                 returned.at[pl.ds(2 * y, 2)], every.at[k, pl.ds(2 * p, 2)],
                 send_view.at[k - 1, p], recv_view.at[k - 1, p], view_peer(view, k),
@@ -692,58 +718,129 @@
         if p == 0:
             view_forward(3)
     scatter(0, pl.ds(0, G_DEV), True)
-    pull(0)
+    for half in range(2):
+        matrix = [shape_rows[half * SHAPE_ROWS + i] for i in range(9)]
+        sums, colours = pull_view(loader(half), slot_rows(view_grads, 0, half), matrix, saved, half * KEPT)
+        for i, value in enumerate(sums):
+            totals[half * SUMS + i] = value
+        for i, value in enumerate(colours):
+            colour[half * 3 + i] = value
     for p in range(8):
         for k in (1, 3, 2):
             view_sends[k, p].wait()
-            if p < 7:
-                add_left(k, p, lambda half, row, size: every[k, 2 * p + half, pl.ds(row, size), :])
+            add_left(k, p, lambda half, row, size: every[k, 2 * p + half, pl.ds(row, size), :])
         if p == 6:
             for k in (1, 3, 2):
                 scatter(k, pl.ds(0, LAST), True)
     for k in (1, 3, 2):
-        add_left(k, 7, lambda half, row, size: every[k, 14 + half, pl.ds(row, size), :])
         scatter(k, pl.ds(LAST, 256), False)
-        pull(k)
+
+
+SUMS = 13
+
+
+def slot_rows(view_grads, view, half):
+    return lambda f: view_grads[pl.ds((2 * view + half) * 128 + f, 8, stride=16), :]
+
+
+def finish_kernel(
+    pictures, view_grads, dense, saved, shape_rows, totals, colour_mine,
+    pictures_hbm, gradient_hbm,
+    gradient, packed, colour, sums, sems,
+):
+    groups = [(first, min(8, ROWS - first)) for first in range(0, ROWS, 8)]
+    copies = [
+        pltpu.make_async_copy(gradient.at[pl.ds(*group)], gradient_hbm.at[pl.ds(*group)], sems.at[i])
+        for i, group in enumerate(groups)
+    ]
+    copies.append(pltpu.make_async_copy(pictures, pictures_hbm, sems.at[8]))
+    copies[8].start()
 
     def put(row, half, value):
         packed[pl.ds((row // 8) * 128 + half * 8 + row % 8, 8, stride=16), :] = value
 
-    def pack(first, last):
-        for group in range(first, last, 8):
-            size = min(8, last - group)
-            for chunk in range(16):
-                gradient[pl.ds(group, size), pl.ds(chunk * LANES, LANES)] = packed[
-                    pl.ds(group * 16 + chunk * 8, size), :
-                ]
+    def send(i):
+        first, size = groups[i]
+        for chunk in range(16):
+            gradient[pl.ds(first, size), pl.ds(chunk * LANES, LANES)] = packed[
+                pl.ds(first * 16 + chunk * 8, size), :
+            ]
+        copies[i].start()
+
+    def put_harmonic(row, half):
+        channel, j = divmod(row - 11, 16)
+        parts = [colour[(2 * k + half) * 3 + channel] for k in range(VIEW_DEVS)]
+        if j:
+            parts = [saved[(2 * k + half) * KEPT + 21 + j] * parts[k] for k in range(VIEW_DEVS)]
+        total = parts[0] + parts[1] + parts[2] + parts[3]
+        put(row, half, total if j else sh_first * total)
 
     for half in range(2):
-        kept = lambda k, i: saved[(2 * k + half) * KEPT + i]
-        for channel in range(3):
-            parts = [colour[(2 * k + half) * 3 + channel] for k in range(VIEW_DEVS)]
-            put(11 + 16 * channel, half, sh_first * (parts[0] + parts[1] + parts[2] + parts[3]))
-            for j in range(15):
-                terms = [kept(k, 22 + j) * parts[k] for k in range(VIEW_DEVS)]
-                put(12 + 16 * channel + j, half, terms[0] + terms[1] + terms[2] + terms[3])
-    pack(16, ROWS)
+        load = lambda row: dense[2 * row + half]
+        matrix = [shape_rows[half * SHAPE_ROWS + i] for i in range(9)]
+        total = [totals[half * SUMS + i] for i in range(SUMS)]
+        for i in range(3):
+            colour[half * 3 + i] = colour_mine[half * 3 + i]
+        for k in range(1, VIEW_DEVS):
+            place = 2 * k + half
+            values, colours = pull_view(load, slot_rows(view_grads, k, half), matrix, saved, place * KEPT)
+            total = [old + value for old, value in zip(total, values)]
+            for i, value in enumerate(colours):
+                colour[place * 3 + i] = value
+        for i, value in enumerate(total):
+            sums[half * SUMS + i] = value
+    for i in range(2, 8):
+        first, size = groups[i]
+        for row in range(first, first + size):
+            for half in range(2):
+                put_harmonic(row, half)
+        send(i)
     for half in range(2):
-        total = [totals[half * 13 + i] for i in range(13)]
+        total = [sums[half * SUMS + i] for i in range(SUMS)]
         shape = [shape_rows[half * SHAPE_ROWS + i] for i in range(SHAPE_ROWS)]
         matrix, scales, unit_q, inv_norm = shape[0:9], shape[9:12], shape[12:16], shape[16]
         for i in range(3):
             put(i, half, total[i])
-            put(3 + i, half, sum(total[3 + 3 * r + i] * matrix[3 * r + i] for r in range(1, 3)) + total[3 + i] * matrix[i])
+            put(3 + i, half, total[3 + i] * matrix[i] + total[6 + i] * matrix[3 + i] + total[9 + i] * matrix[6 + i])
         _, pull_back = jax.vjp(rotation_of, *unit_q)
         g_unit = pull_back([total[3 + 3 * i + j] * scales[j] for i in range(3) for j in range(3)])
         along = unit_q[0] * g_unit[0] + unit_q[1] * g_unit[1] + unit_q[2] * g_unit[2] + unit_q[3] * g_unit[3]
         for i in range(4):
             put(6 + i, half, inv_norm * (g_unit[i] - unit_q[i] * along))
         put(10, half, total[12] * (1.0 / (1.0 + jnp.exp(dense[20 + half]))))
-    pack(0, 16)
+        for row in range(11, 16):
+            put_harmonic(row, half)
+    send(0)
+    send(1)
+    for copy in copies:
+        copy.wait()
+
+
+def finish_call(operands):
+    vmem = pl.BlockSpec(memory_space=pltpu.VMEM)
+    anywhere = pl.BlockSpec(memory_space=pl.ANY)
+    tile = (8, LANES)
+    return pl.pallas_call(
+        finish_kernel,
+        out_shape=(
+            jax.ShapeDtypeStruct(operands[0].shape, F32),
+            jax.ShapeDtypeStruct((ROWS, G_DEV), F32),
+        ),
+        in_specs=[vmem] * len(operands),
+        out_specs=(anywhere, anywhere),
+        scratch_shapes=[
+            pltpu.VMEM((ROWS, G_DEV), F32),
+            pltpu.VMEM((64 * 16, LANES), F32),
+            pltpu.VMEM((VIEW_DEVS * 2 * 3,) + tile, F32),
+            pltpu.VMEM((2 * SUMS,) + tile, F32),
+            pltpu.SemaphoreType.DMA((9,)),
+        ],
+        compiler_params=pltpu.CompilerParams(vmem_limit_bytes=8 * 2**20),
+        name="finish",
+    )(*operands)
 
 
 def render_call(camera, tile_ids, tile_len, params, slots, lists, targets):
-    smem = pl.BlockSpec(memory_space=pltpu.SMEM)
     anywhere = pl.BlockSpec(memory_space=pl.ANY)
     blocks = pltpu.VMEM((16, FEATS, LANES), F32)
     tile = (8, LANES)
@@ -754,14 +851,21 @@
         render_kernel,
         out_shape=(
             pltpu.VMEM(targets.shape, F32),
-            pltpu.VMEM(params.shape, F32),
+            pltpu.VMEM((VIEW_DEVS * 256, LANES), F32),
+            pltpu.VMEM((2 * ROWS,) + tile, F32),
+            pltpu.VMEM((VIEW_DEVS * 2 * KEPT,) + tile, F32),
+            pltpu.VMEM((2 * SHAPE_ROWS,) + tile, F32),
+            pltpu.VMEM((2 * SUMS,) + tile, F32),
+            pltpu.VMEM((2 * 3,) + tile, F32),
         ),
-        in_specs=[smem, smem, smem, anywhere, anywhere, anywhere, anywhere],
-        out_specs=(pl.BlockSpec(memory_space=pltpu.VMEM), pl.BlockSpec(memory_space=pltpu.VMEM)),
+        in_specs=[anywhere] * 7,
+        out_specs=(pl.BlockSpec(memory_space=pltpu.VMEM),) * 7,
         scratch_shapes=[
+            pltpu.VMEM(camera.shape, F32),
+            pltpu.VMEM(tile_ids.shape, jnp.int32),
+            pltpu.VMEM(tile_len.shape, jnp.int32),
             pltpu.VMEM((ROWS, G_DEV), F32),
             pltpu.VMEM((64 * 16, LANES), F32),
-            pltpu.VMEM((2 * ROWS,) + tile, F32),
             pltpu.VMEM(lists.shape, jnp.int32),
             pltpu.VMEM(targets.shape, F32),
             pltpu.VMEM((VIEW_DEVS, 16, LANES), jnp.int32),
@@ -783,12 +887,7 @@
             pltpu.VMEM((VIEW_DEVS * 16 * 128, LANES), BF16),
             pltpu.VMEM((VIEW_DEVS, 256, G_DEV), BF16),
             pltpu.VMEM((VIEW_DEVS, 256, G_DEV), BF16),
-            pltpu.VMEM((VIEW_DEVS * 256, LANES), F32),
-            pltpu.VMEM((VIEW_DEVS * 2 * KEPT,) + tile, F32),
-            pltpu.VMEM((2 * SHAPE_ROWS,) + tile, F32),
-            pltpu.VMEM((2 * 13,) + tile, F32),
-            pltpu.VMEM((VIEW_DEVS * 2 * 3,) + tile, F32),
-            pltpu.SemaphoreType.DMA((11,)),
+            pltpu.SemaphoreType.DMA((14,)),
         ]
         + y_sems + zc_sems + zc_sems + y_sems + view_sems + view_sems
         + [pltpu.SemaphoreType.DMA((VIEW_DEVS - 1, 8))] * 2,
@@ -804,37 +903,12 @@
     )
 
 
-def store_kernel(pictures, gradient, pictures_hbm, gradient_hbm, sems):
-    copies = [pltpu.make_async_copy(pictures, pictures_hbm, sems.at[0])]
-    for i, (first, size) in enumerate(((0, 16), (16, 16), (32, 16), (48, ROWS - 48))):
-        rows = pl.ds(first, size)
-        copies.append(pltpu.make_async_copy(gradient.at[rows], gradient_hbm.at[rows], sems.at[1 + i]))
-    for copy in copies:
-        copy.start()
-    for copy in copies:
-        copy.wait()
-
-
-def store_call(pictures, gradient):
-    vmem = pl.BlockSpec(memory_space=pltpu.VMEM)
-    anywhere = pl.BlockSpec(memory_space=pl.ANY)
-    return pl.pallas_call(
-        store_kernel,
-        out_shape=(jax.ShapeDtypeStruct(pictures.shape, F32), jax.ShapeDtypeStruct(gradient.shape, F32)),
-        in_specs=[vmem, vmem],
-        out_specs=(anywhere, anywhere),
-        scratch_shapes=[pltpu.SemaphoreType.DMA((5,))],
-        compiler_params=pltpu.CompilerParams(vmem_limit_bytes=8 * 2**20),
-        name="store",
-    )(pictures, gradient)
-
-
 def local(params, cameras, targets, tile_ids, send_slots, tile_lists, tile_len):
-    pictures, gradient = render_call(
+    partial = render_call(
         cameras, tile_ids, tile_len, params, send_slots.reshape(16, LANES), tile_lists,
         jnp.transpose(targets, (0, 2, 1, 3)),
     )
-    pictures, gradient = store_call(pictures, gradient)
+    pictures, gradient = finish_call(partial)
     return jnp.transpose(pictures, (0, 2, 1, 3)), gradient
 
 

time: 48.1 us -> 48.1 us (level)
    pallas_call x1, Pallas kernels: 46.5 us -> 46 us  [render_call(): pl.pallas_call(render_kernel, out_shape=(pltpu.VMEM(targets.shape, F32),...]
where the time goes in v5:
time: 48.1 us; the launch traced here: 47.9 us
  Pallas kernels  47.2 us (98%)
  between operations  0.64 us (1%)
    pallas_call x1, Pallas kernels, render_call(): pl.pallas_call(render_kernel, out_shape=(pltpu.VMEM(targets.shape, F32),...  46 us
    pallas_call x1, Pallas kernels, finish_call(): pl.pallas_call(finish_kernel, out_shape=(jax.ShapeDtypeStruct(operands[0]...  1.25 us

profile of v5, /device:TPU:1, one launch (start us, length us, event | category | flops | bytes accessed | tf_op | source)
XLA Modules:
  0.0 47.9 jit_solution(6056971481025653973)
XLA Ops:
  0.6 46.0 %render.1 = (f32[1,3,2,256]{3,2,1,0:T(2,128)S(1)}, f32[1024,128]{1,0:T(8,128)S(1)}, f32[118,8,128]{2,1,0:T(8,128)S(1)}, f32[320,8,128]{2,1,0:T(8,128)S(1)}, f32[...) custom-call(f32[1,3]{1,0:T(1,128)} %camera_hbm.1, s32[1,2]{1,0:T(1,128)} %ids_hbm.1, ...), custom_call_target="tpu_custom_call" | custom-call | tf_op jit(solution)/shard_map/render/pallas_call | solution.py:850
  46.6 1.2 %finish.1 = (f32[1,3,2,256]{3,2,1,0:T(2,128)}, f32[59,2048]{1,0:T(8,128)}) custom-call(f32[1,3,2,256]{3,2,1,0:T(2,128)S(1)} %get-tuple-element.11.pictures, f32[1024,128]{1,0:T(8,128)S(1)} %get-tuple-element.12.view_grads, f32[118,8,128]{2,1,0:T(8,128)S(1)} %get-tuple-element.13.dense, f32[320,8,128]{2,1,0:T(8,128)S(1)} %get-tuple-element.14.saved, ...), custom_call_target="tpu_custom_call" | custom-call | tf_op jit(solution)/shard_map/finish/pallas_call | solution.py:823

commit v6 on v5

--- a/solution.py
+++ b/solution.py
@@ -15,7 +15,6 @@
 Y_ORDER = (4, 3, 5, 2, 6, 1, 7)
 ZC_ORDER = (8, 9, 7, 6, 10, 5, 11, 4, 12, 3, 13, 2, 14, 1, 15)
 VIEW_ORDER = (2, 1, 3)
-FAR_Y = 4
 ENTRIES = 512
 CHUNKS = ENTRIES // LANES
 HALF = ENTRIES // 2
@@ -263,16 +262,11 @@
     return {"view": lax.rem(view + k, VIEW_DEVS)}
 
 
-def far_view_peer(my_y, my_zc, view, k):
-    return {**y_peer(my_y, my_zc, FAR_Y)[1], **view_peer(view, k)}
-
-
 def greet(my_y, my_zc, view):
     barrier = pltpu.get_barrier_semaphore()
     peers = [y_peer(my_y, my_zc, k)[1] for k in Y_ORDER]
     peers += [zc_peer(my_y, my_zc, k)[1] for k in ZC_ORDER]
     peers += [view_peer(view, k) for k in VIEW_ORDER]
-    peers += [far_view_peer(my_y, my_zc, view, k) for k in VIEW_ORDER]
     for peer in peers:
         pl.semaphore_signal(barrier, inc=1, device_id=peer, device_id_type=pl.DeviceIdType.MESH)
     return barrier, len(peers)
@@ -300,9 +294,10 @@
         lower[pl.ds(256 * i, 256), :] = below if i < 2 else ones
 
 
-def entry_slot(lists, tile, chunk):
+def entry_slot(lists, my_y, tile, chunk):
     index = lists[0, pl.ds(tile, 1), pl.ds(chunk * LANES, LANES)]
-    return (index >> 4) & 15, ((index >> 8) << 4) | (index & 15)
+    steps = (my_y - (index >> 8)) & (Y_DEVS - 1)
+    return (index >> 4) & 15, (steps << 4) | (index & 15)
 
 
 def hot_rows(index, count):
@@ -580,10 +575,10 @@
             outgoing[chunk, pl.ds(8, 1), :] = bottom[0:1]
         if k:
             y_sends[k] = remote(
-                outgoing.at[pl.ds(2 * peer, 2)], landed.at[pl.ds(2 * my_y, 2)],
+                outgoing.at[pl.ds(2 * peer, 2)], landed.at[pl.ds(2 * k, 2)],
                 send_y.at[k - 1], recv_y.at[k - 1], device_id,
             )
-    landed[pl.ds(2 * my_y, 2)] = outgoing[pl.ds(2 * my_y, 2)]
+    landed[pl.ds(0, 2)] = outgoing[pl.ds(2 * my_y, 2)]
     side_sends = []
     for k in VIEW_ORDER:
         peer = view_peer(view, k)
@@ -596,7 +591,7 @@
     for tile in range(TILES_DEV):
         for chunk in range(ENTRIES // LANES):
             n = tile * (ENTRIES // LANES) + chunk
-            high, low = entry_slot(lists, tile, chunk)
+            high, low = entry_slot(lists, my_y, tile, chunk)
             fill_masks(high, 16, masks, n * 256)
             right[:, pl.ds(n * LANES, LANES)] = hot_rows(low, LANES)
 
@@ -608,13 +603,17 @@
                 fill_masks(index >> 8, 8, view_masks, (k * 16 + n) * 128)
                 view_right[k, :, pl.ds(n * LANES, LANES)] = hot_rows(index & 255, 256)
 
-    for k in Y_ORDER[::-1]:
-        y_sends[k].wait()
-
-    def to_zc(j, half, rows):
-        staged[8 * half + j] = rows
-
-    regroup(lambda i, half: landed[2 * i + half], to_zc)
+    blocks = [jnp.zeros((FEATS, LANES), F32)] * ZC_DEVS
+    group = lax.broadcasted_iota(jnp.int32, (FEATS, LANES), 1) // 16
+    for k in Y_ARRIVAL:
+        if k:
+            y_sends[k].wait()
+        for zc in range(ZC_DEVS):
+            rows = landed[2 * k + zc // 8]
+            turn = 16 * ((k - zc) % 8)
+            blocks[zc] = jnp.where(group == k, pltpu.roll(rows, turn, 1) if turn else rows, blocks[zc])
+    for zc in range(ZC_DEVS):
+        staged[zc] = blocks[zc]
     zc_sends = {}
     for k in ZC_ORDER:
         peer, device_id = zc_peer(my_y, my_zc, k)
@@ -635,7 +634,7 @@
             keep_colours(loader(half), saved, (2 * k + half) * KEPT)
         view_factors(k)
 
-    places = [entry_slot(lists, n // 4, n % 4) for n in range(8)]
+    places = [entry_slot(lists, my_y, n // 4, n % 4) for n in range(8)]
     places = [(jnp.broadcast_to(high, (8, LANES)), jnp.broadcast_to(low, (8, LANES))) for high, low in places]
     tops = [jnp.zeros((8, LANES), F32)] * 8
     bottoms = [jnp.zeros((8, LANES), F32)] * 8
@@ -677,17 +676,10 @@
     for k in Y_ORDER:
         peer, device_id = y_peer(my_y, my_zc, k)
         y_sends[k] = remote(
-            staged_back.at[pl.ds(2 * peer, 2)], returned.at[pl.ds(2 * my_y, 2)],
+            staged_back.at[pl.ds(2 * (Y_DEVS - k), 2)], returned.at[pl.ds(2 * my_y, 2)],
             send_y2.at[k - 1], recv_y2.at[k - 1], device_id,
         )
-        if k == FAR_Y:
-            for other in VIEW_ORDER:
-                view_sends[other, 7] = remote(
-                    staged_back.at[pl.ds(2 * peer, 2)], every.at[other, pl.ds(14, 2)],
-                    send_view.at[other - 1, 7], recv_view.at[other - 1, 7],
-                    far_view_peer(my_y, my_zc, view, other),
-                )
-    returned[pl.ds(2 * my_y, 2)] = staged_back[pl.ds(2 * my_y, 2)]
+    returned[pl.ds(2 * my_y, 2)] = staged_back[pl.ds(0, 2)]
 
     def add_left(k, p, block):
         for half in range(2):
@@ -709,7 +701,7 @@
         if step:
             y_sends[step].wait()
         y = lax.rem(my_y + Y_DEVS - step, Y_DEVS)
-        for k in VIEW_ORDER if step != FAR_Y else ():
+        for k in VIEW_ORDER:
             view_sends[k, p] = remote(
                 returned.at[pl.ds(2 * y, 2)], every.at[k, pl.ds(2 * p, 2)],
                 send_view.at[k - 1, p], recv_view.at[k - 1, p], view_peer(view, k),

time: 48.1 us -> 46.2 us (0.960)
  Pallas kernels: 47.2 us -> 45.4 us
    pallas_call x1, Pallas kernels: 46 us -> 44.2 us  [render_call(): pl.pallas_call(render_kernel, out_shape=(pltpu.VMEM(targets.shape, F32),...]
where the time goes in v6:
time: 46.2 us; the launch traced here: 46.1 us
  Pallas kernels  45.4 us (98%)
  between operations  0.64 us (1%)
    pallas_call x1, Pallas kernels, render_call(): pl.pallas_call(render_kernel, out_shape=(pltpu.VMEM(targets.shape, F32),...  44.2 us
    pallas_call x1, Pallas kernels, finish_call(): pl.pallas_call(finish_kernel, out_shape=(jax.ShapeDtypeStruct(operands[0]...  1.25 us

profile of v6, /device:TPU:1, one launch (start us, length us, event | category | flops | bytes accessed | tf_op | source)
XLA Modules:
  0.0 46.1 jit_solution(14549188123226629291)
XLA Ops:
  0.6 44.2 %render.1 = (f32[1,3,2,256]{3,2,1,0:T(2,128)S(1)}, f32[1024,128]{1,0:T(8,128)S(1)}, f32[118,8,128]{2,1,0:T(8,128)S(1)}, f32[320,8,128]{2,1,0:T(8,128)S(1)}, f32[...) custom-call(f32[1,3]{1,0:T(1,128)} %camera_hbm.1, s32[1,2]{1,0:T(1,128)} %ids_hbm.1, ...), custom_call_target="tpu_custom_call" | custom-call | tf_op jit(solution)/shard_map/render/pallas_call | solution.py:842
  44.8 1.2 %finish.1 = (f32[1,3,2,256]{3,2,1,0:T(2,128)}, f32[59,2048]{1,0:T(8,128)}) custom-call(f32[1,3,2,256]{3,2,1,0:T(2,128)S(1)} %get-tuple-element.11.pictures, f32[1024,128]{1,0:T(8,128)S(1)} %get-tuple-element.12.view_grads, f32[118,8,128]{2,1,0:T(8,128)S(1)} %get-tuple-element.13.dense, f32[320,8,128]{2,1,0:T(8,128)S(1)} %get-tuple-element.14.saved, ...), custom_call_target="tpu_custom_call" | custom-call | tf_op jit(solution)/shard_map/finish/pallas_call | solution.py:815

commit v7 on v6

--- a/solution.py
+++ b/solution.py
@@ -220,21 +220,6 @@
     return top, bottom
 
 
-def block_transpose(rows):
-    group = lax.broadcasted_iota(jnp.int32, rows[0].shape, 1) // 16
-    for step in (1, 2, 4):
-        odd = (group & step) != 0
-        fresh = list(rows)
-        for i in range(8):
-            if i & step:
-                continue
-            first, second = rows[i], rows[i + step]
-            fresh[i] = jnp.where(odd, pltpu.roll(second, 16 * step, 1), first)
-            fresh[i + step] = jnp.where(odd, second, pltpu.roll(first, LANES - 16 * step, 1))
-        rows = fresh
-    return rows
-
-
 def remote(src_ref, dst_ref, send_sem, recv_sem, device_id):
     copy = pltpu.make_async_remote_copy(
         src_ref=src_ref,
@@ -270,12 +255,6 @@
     for peer in peers:
         pl.semaphore_signal(barrier, inc=1, device_id=peer, device_id_type=pl.DeviceIdType.MESH)
     return barrier, len(peers)
-
-
-def regroup(load, store):
-    for half in range(2):
-        for j, rows in enumerate(block_transpose([load(i, half) for i in range(8)])):
-            store(j, half, rows)
 
 
 def part_lanes(chunk):
@@ -495,7 +474,7 @@
 def render_kernel(
     camera_hbm, ids_hbm, len_hbm, params_hbm, slots_hbm, lists_hbm, targets_hbm,
     pictures, view_grads, dense, saved, shape_rows, totals, colour,
-    camera, tile_ids, tile_len, params, packed, lists, targets, slots, cams,
+    camera, tile_ids, tile_len, params, packed, lists, targets, slots, turned, cams,
     table, outgoing, landed, staged, received, slot_grads, landed_back, staged_back, returned, every,
     feats, planes, parts, upper, lower, grads, masks, left, right, view_masks, view_left, view_right,
     load_sem, send_y, recv_y, send_zc, recv_zc, send_zc2, recv_zc2, send_y2, recv_y2,
@@ -596,10 +575,16 @@
             right[:, pl.ds(n * LANES, LANES)] = hot_rows(low, LANES)
 
     def view_factors(k):
+        even, odd = [slots[k, pl.ds(i, 8, stride=2), :] for i in range(2)]
+        lane = lax.broadcasted_iota(jnp.int32, (8, LANES), 1)
+        for half in range(2):
+            owner = (my_zc - (8 * half + (lane >> 4))) & (ZC_DEVS - 1)
+            column = ((owner & 7) << 4) | (lane & 15)
+            turned[2 * k + half] = jnp.where(owner < 8, lane_gather(even, column), lane_gather(odd, column))
         for p, step in enumerate(Y_ARRIVAL):
             for half in range(2):
                 n = 2 * p + half
-                index = slots[k, pl.ds(2 * lax.rem(my_y + Y_DEVS - step, Y_DEVS) + half, 1), :]
+                index = turned[2 * k + half, pl.ds(lax.rem(my_y + Y_DEVS - step, Y_DEVS), 1), :]
                 fill_masks(index >> 8, 8, view_masks, (k * 16 + n) * 128)
                 view_right[k, :, pl.ds(n * LANES, LANES)] = hot_rows(index & 255, 256)
 
@@ -660,18 +645,23 @@
     for k in ZC_ORDER:
         peer, device_id = zc_peer(my_y, my_zc, k)
         zc_sends[k] = remote(
-            slot_grads.at[peer], landed_back.at[my_zc], send_zc2.at[k - 1], recv_zc2.at[k - 1], device_id
+            slot_grads.at[peer], landed_back.at[k], send_zc2.at[k - 1], recv_zc2.at[k - 1], device_id
         )
-    landed_back[my_zc] = slot_grads[my_zc]
+    landed_back[0] = slot_grads[my_zc]
     view_forward(1)
     view_forward(2)
-    for k in ZC_ORDER[::-1]:
-        zc_sends[k].wait()
-
-    def to_y(j, half, rows):
-        staged_back[2 * j + half] = rows
-
-    regroup(lambda i, half: landed_back[8 * half + i], to_y)
+    blocks = [[jnp.zeros((FEATS, LANES), F32)] * 2 for _ in range(Y_DEVS)]
+    for k in ZC_ARRIVAL:
+        if k:
+            zc_sends[k].wait()
+        rows = landed_back[k]
+        half, place = divmod(k, 8)
+        for j in range(Y_DEVS):
+            turn = 16 * ((place - j) % 8)
+            blocks[j][half] = jnp.where(group == place, pltpu.roll(rows, turn, 1) if turn else rows, blocks[j][half])
+    for j in range(Y_DEVS):
+        for half in range(2):
+            staged_back[2 * j + half] = blocks[j][half]
     view_sends = {}
     for k in Y_ORDER:
         peer, device_id = y_peer(my_y, my_zc, k)
@@ -861,6 +851,7 @@
             pltpu.VMEM(lists.shape, jnp.int32),
             pltpu.VMEM(targets.shape, F32),
             pltpu.VMEM((VIEW_DEVS, 16, LANES), jnp.int32),
+            pltpu.VMEM((2 * VIEW_DEVS, 8, LANES), jnp.int32),
             pltpu.VMEM((VIEW_DEVS,) + tile, F32),
             pltpu.VMEM((256, LANES), F32),
         ]

time: 46.2 us -> 45.8 us (level)
  no operation moved by 1% of the time
where the time goes in v7:
time: 45.8 us; the launch traced here: 45.6 us
  Pallas kernels  45 us (98%)
  between operations  0.64 us (1%)
    pallas_call x1, Pallas kernels, render_call(): pl.pallas_call(render_kernel, out_shape=(pltpu.VMEM(targets.shape, F32),...  43.7 us
    pallas_call x1, Pallas kernels, finish_call(): pl.pallas_call(finish_kernel, out_shape=(jax.ShapeDtypeStruct(operands[0]...  1.25 us

profile of v7, /device:TPU:1, one launch (start us, length us, event | category | flops | bytes accessed | tf_op | source)
XLA Modules:
  0.0 45.6 jit_solution(11880509550150868713)
XLA Ops:
  0.6 43.7 %render.1 = (f32[1,3,2,256]{3,2,1,0:T(2,128)S(1)}, f32[1024,128]{1,0:T(8,128)S(1)}, f32[118,8,128]{2,1,0:T(8,128)S(1)}, f32[320,8,128]{2,1,0:T(8,128)S(1)}, f32[...) custom-call(f32[1,3]{1,0:T(1,128)} %camera_hbm.1, s32[1,2]{1,0:T(1,128)} %ids_hbm.1, ...), custom_call_target="tpu_custom_call" | custom-call | tf_op jit(solution)/shard_map/render/pallas_call | solution.py:832
  44.4 1.2 %finish.1 = (f32[1,3,2,256]{3,2,1,0:T(2,128)}, f32[59,2048]{1,0:T(8,128)}) custom-call(f32[1,3,2,256]{3,2,1,0:T(2,128)S(1)} %get-tuple-element.11.pictures, f32[1024,128]{1,0:T(8,128)S(1)} %get-tuple-element.12.view_grads, f32[118,8,128]{2,1,0:T(8,128)S(1)} %get-tuple-element.13.dense, f32[320,8,128]{2,1,0:T(8,128)S(1)} %get-tuple-element.14.saved, ...), custom_call_target="tpu_custom_call" | custom-call | tf_op jit(solution)/shard_map/finish/pallas_call | solution.py:805

commit v8 on v6

--- a/solution.py
+++ b/solution.py
@@ -564,20 +564,21 @@
         put_features(6, keep_colours(loader(half), saved, half * KEPT), half)
 
     side_loads[1].wait()
-    pl.semaphore_wait(barrier, greetings)
-    y_sends = {}
     for k in Y_ORDER + (0,):
-        peer, device_id = y_peer(my_y, my_zc, k)
+        peer, _ = y_peer(my_y, my_zc, k)
         for half in range(2):
             chunk = 2 * peer + half
             top, bottom = gather_chunk(table, slots[0, pl.ds(chunk, 1), :])
             outgoing[chunk, pl.ds(0, 8), :] = top
             outgoing[chunk, pl.ds(8, 1), :] = bottom[0:1]
-        if k:
-            y_sends[k] = remote(
-                outgoing.at[pl.ds(2 * peer, 2)], landed.at[pl.ds(2 * k, 2)],
-                send_y.at[k - 1], recv_y.at[k - 1], device_id,
-            )
+    pl.semaphore_wait(barrier, greetings)
+    y_sends = {}
+    for k in Y_ORDER:
+        peer, device_id = y_peer(my_y, my_zc, k)
+        y_sends[k] = remote(
+            outgoing.at[pl.ds(2 * peer, 2)], landed.at[pl.ds(2 * k, 2)],
+            send_y.at[k - 1], recv_y.at[k - 1], device_id,
+        )
     landed[pl.ds(0, 2)] = outgoing[pl.ds(2 * my_y, 2)]
     side_sends = []
     for k in VIEW_ORDER:

time: 46.2 us -> 46.1 us (level)
  no operation moved by 1% of the time
where the time goes in v8:
time: 46.1 us; the launch traced here: 46 us
  Pallas kernels  45.3 us (98%)
  between operations  0.64 us (1%)
    pallas_call x1, Pallas kernels, render_call(): pl.pallas_call(render_kernel, out_shape=(pltpu.VMEM(targets.shape, F32),...  44.1 us
    pallas_call x1, Pallas kernels, finish_call(): pl.pallas_call(finish_kernel, out_shape=(jax.ShapeDtypeStruct(operands[0]...  1.25 us

profile of v8, /device:TPU:1, one launch (start us, length us, event | category | flops | bytes accessed | tf_op | source)
XLA Modules:
  0.0 46.0 jit_solution(11551801832564712963)
XLA Ops:
  0.6 44.1 %render.1 = (f32[1,3,2,256]{3,2,1,0:T(2,128)S(1)}, f32[1024,128]{1,0:T(8,128)S(1)}, f32[118,8,128]{2,1,0:T(8,128)S(1)}, f32[320,8,128]{2,1,0:T(8,128)S(1)}, f32[...) custom-call(f32[1,3]{1,0:T(1,128)} %camera_hbm.1, s32[1,2]{1,0:T(1,128)} %ids_hbm.1, ...), custom_call_target="tpu_custom_call" | custom-call | tf_op jit(solution)/shard_map/render/pallas_call | solution.py:843
  44.7 1.2 %finish.1 = (f32[1,3,2,256]{3,2,1,0:T(2,128)}, f32[59,2048]{1,0:T(8,128)}) custom-call(f32[1,3,2,256]{3,2,1,0:T(2,128)S(1)} %get-tuple-element.11.pictures, f32[1024,128]{1,0:T(8,128)S(1)} %get-tuple-element.12.view_grads, f32[118,8,128]{2,1,0:T(8,128)S(1)} %get-tuple-element.13.dense, f32[320,8,128]{2,1,0:T(8,128)S(1)} %get-tuple-element.14.saved, ...), custom_call_target="tpu_custom_call" | custom-call | tf_op jit(solution)/shard_map/finish/pallas_call | solution.py:816
